TPU v7x, 32 devices: a whole 2x2x4 slice. The times are simulated.
32 devices in a mesh: dp: 16 (over z, y, core), fsdp: 2 (over x).
Axes of the slice: x: 2, y: 2, z: 4, core: 2. Of those that a mesh axis runs over, the one named last changes fastest.
Arguments:
- tokens: bfloat16 [16384, 768], P(('dp', 'fsdp')), may hold values from -6 to 6
- lengths: int32 [32], P(('dp', 'fsdp')), may hold values from 128 to 512, as said below
- buckets: int32 [32, 3, 512, 512], P(('dp', 'fsdp')), may hold values from 0 to 31
- qkv_weight: bfloat16 [768, 2304], P('fsdp'), may hold values from -0.21875 to 0.21875
- q_bias: bfloat16 [768], P('fsdp'), may hold values from -3 to 3
- v_bias: bfloat16 [768], P('fsdp'), may hold values from -0.3125 to 0.3125
- out_weight: bfloat16 [768, 768], P('fsdp'), may hold values from -1.75 to 1.75
- out_bias: bfloat16 [768], P('fsdp'), may hold values from -1.75 to 1.75
- bias_table: bfloat16 [96, 12], P('fsdp'), may hold values from -3 to 3
- norm1_gain: bfloat16 [768], P('fsdp'), may hold values from 0.5 to 1.5
- norm1_bias: bfloat16 [768], P('fsdp'), may hold values from -1.75 to 1.75
- up_weight: bfloat16 [768, 3072], P('fsdp'), may hold values from -0.21875 to 0.21875
- up_bias: bfloat16 [3072], P('fsdp'), may hold values from -1.75 to 1.75
- down_weight: bfloat16 [3072, 768], P('fsdp'), may hold values from -0.109375 to 0.109375
- down_bias: bfloat16 [768], P('fsdp'), may hold values from -1.75 to 1.75
- norm2_gain: bfloat16 [768], P('fsdp'), may hold values from 0.5 to 1.5
- norm2_bias: bfloat16 [768], P('fsdp'), may hold values from -1.75 to 1.75
- cotangent: bfloat16 [16384, 768], P(('dp', 'fsdp')), may hold values from -6 to 6
Outputs:
- output: bfloat16 [16384, 768], P(('dp', 'fsdp'))
- tokens_grad: bfloat16 [16384, 768], P(('dp', 'fsdp'))
- qkv_weight_grad: float32 [768, 2304], P('fsdp')
- q_bias_grad: float32 [768], P('fsdp')
- v_bias_grad: float32 [768], P('fsdp')
- out_weight_grad: float32 [768, 768], P('fsdp')
- out_bias_grad: float32 [768], P('fsdp')
- bias_table_grad: float32 [96, 12], P('fsdp')
- norm1_gain_grad: float32 [768], P('fsdp')
- norm1_bias_grad: float32 [768], P('fsdp')
- up_weight_grad: float32 [768, 3072], P('fsdp')
- up_bias_grad: float32 [3072], P('fsdp')
- down_weight_grad: float32 [3072, 768], P('fsdp')
- down_bias_grad: float32 [768], P('fsdp')
- norm2_gain_grad: float32 [768], P('fsdp')
- norm2_bias_grad: float32 [768], P('fsdp')
Inputs may be any that keep to these rules, and one draw needn't show every extreme that they name: `lengths`: each window has at least a quarter of its rows real, and some window has exactly 512.
All inputs are finite; a program needn't handle non-finite values.
Results may differ from a plain program's by a relative error of at most 0.02.
Values may be sent and summed in bfloat16 or wider, within the bound.
No kernel may reach another device: no remote copies, remote signals or barrier semaphores. Data moves between devices by JAX's collectives and lax.ppermute only.
A program may use at most 192 MiB of HBM per device.

v0:
```python
import jax
import jax.numpy as jnp
from jax import lax
from jax.sharding import PartitionSpec as P

EPSILON = 1e-05
MASKED = -1000000000.0


def norm_forward(inputs, gain_vec, shift_vec):
    center = inputs - jnp.mean(inputs, axis=-1, keepdims=True)
    inverse = lax.rsqrt(jnp.mean(center * center, axis=-1, keepdims=True) + EPSILON)
    scaled = center * inverse
    return (scaled * gain_vec + shift_vec, scaled, inverse)


def norm_backward(grad_in, scaled, inverse, gain_vec):
    gain_grad = jnp.sum(grad_in * scaled, axis=0)
    shift_grad = jnp.sum(grad_in, axis=0)
    inner_term = grad_in * gain_vec
    centered = inner_term - jnp.mean(inner_term, axis=-1, keepdims=True)
    grad_out = inverse * (centered - scaled * jnp.mean(inner_term * scaled, axis=-1, keepdims=True))
    return (gain_grad, shift_grad, grad_out)


def expand_part(flat_ids, levels, part_index):
    return (flat_ids[part_index][None, :] == levels[:, None]).astype(jnp.bfloat16)


def pair_bias(bucket, table, levels):
    flat_ids = bucket.reshape(3, -1)
    bucket_count = levels.shape[0]
    summed = None
    for part_index in range(3):
        onehot = expand_part(flat_ids, levels, part_index)
        table_rows = table[part_index * bucket_count : (part_index + 1) * bucket_count]
        bias_term = lax.dot_general(
            table_rows, onehot, (((0,), (0,)), ((), ())), preferred_element_type=jnp.float32
        )
        summed = bias_term if summed is None else summed + bias_term
    return summed


def table_grad(bucket, grad_scores, levels):
    flat_ids = bucket.reshape(3, -1)
    pieces = []
    for part_index in range(3):
        onehot = expand_part(flat_ids, levels, part_index)
        pieces.append(
            lax.dot_general(
                onehot, grad_scores, (((1,), (1,)), ((), ())), preferred_element_type=jnp.float32
            )
        )
    return jnp.concatenate(pieces, axis=0)


def masked_scores(queries, keys_low, bucket, length, table, levels):
    window_len = queries.shape[0]
    head_count = queries.shape[1]
    scores = jnp.einsum("qhd,khd->hqk", queries, keys_low, preferred_element_type=jnp.float32)
    scores = scores + pair_bias(bucket, table, levels).reshape(head_count, window_len, window_len)
    key_keep = jnp.arange(window_len, dtype=jnp.int32) < length
    return jnp.where(key_keep[None, None, :], scores, MASKED)


def contract_rows(left, right):
    return lax.dot_general(
        left, right, (((0,), (0,)), ((), ())), preferred_element_type=jnp.float32
    )


def contract_cols(left, right):
    return lax.dot_general(
        left, right, (((1,), (1,)), ((), ())), preferred_element_type=jnp.float32
    )


def column_sum(grad_low):
    return jnp.sum(grad_low.astype(jnp.float32), axis=0)


def per_device(
    tokens,
    lengths,
    buckets,
    qkv_weight,
    q_bias,
    v_bias,
    out_weight,
    out_bias,
    bias_table,
    norm1_gain,
    norm1_bias,
    up_weight,
    up_bias,
    down_weight,
    down_bias,
    norm2_gain,
    norm2_bias,
    cotangent,
):
    attn_set = (
        lax.all_gather(qkv_weight, "fsdp", axis=0, tiled=True),
        lax.all_gather(q_bias, "fsdp", axis=0, tiled=True),
        lax.all_gather(v_bias, "fsdp", axis=0, tiled=True),
        lax.all_gather(out_weight, "fsdp", axis=0, tiled=True),
        lax.all_gather(out_bias, "fsdp", axis=0, tiled=True),
        lax.all_gather(bias_table, "fsdp", axis=0, tiled=True),
        lax.all_gather(norm1_gain, "fsdp", axis=0, tiled=True),
        lax.all_gather(norm1_bias, "fsdp", axis=0, tiled=True),
    )
    window_count = lengths.shape[0]
    window_len = buckets.shape[2]
    model_width = tokens.shape[1]
    head_count = bias_table.shape[1]
    head_size = model_width // head_count
    factor = head_size ** (-0.5)
    row_count = window_count * window_len
    w_qkv, b_query, b_value, w_out, b_out, table, gain_one, shift_one = attn_set
    levels = jnp.arange(table.shape[0] // 3, dtype=jnp.int32)
    row_valid = (
        (jnp.arange(window_len, dtype=jnp.int32)[None, :] < lengths[:, None])
        .astype(jnp.float32)
        .reshape(row_count, 1)
    )
    packed = jnp.dot(tokens, w_qkv, preferred_element_type=jnp.float32)
    queries = ((packed[:, :model_width] + b_query.astype(jnp.float32)) * factor).astype(
        jnp.bfloat16
    )
    keys_low = packed[:, model_width : 2 * model_width].astype(jnp.bfloat16)
    values_low = (packed[:, 2 * model_width :] + b_value.astype(jnp.float32)).astype(jnp.bfloat16)
    head_shape = (window_count, window_len, head_count, head_size)
    q_heads = queries.reshape(head_shape)
    k_heads = keys_low.reshape(head_shape)
    v_heads = values_low.reshape(head_shape)

    def attend(window_item):
        q_one, k_one, v_one, bucket, length = window_item
        scores = masked_scores(q_one, k_one, bucket, length, table, levels)
        row_max = jnp.max(scores, axis=-1, keepdims=True)
        shifted_exp = jnp.exp(scores - row_max)
        normalizer = jnp.sum(shifted_exp, axis=-1, keepdims=True)
        attn_probs = (shifted_exp / normalizer).astype(jnp.bfloat16)
        mixed_one = jnp.einsum(
            "hqk,khd->qhd", attn_probs, v_one, preferred_element_type=jnp.float32
        )
        return (mixed_one.astype(jnp.bfloat16), row_max + jnp.log(normalizer))

    mixed_heads, logsum = lax.map(attend, (q_heads, k_heads, v_heads, buckets, lengths))
    mixed_flat = mixed_heads.reshape(row_count, model_width)
    attn_out = jnp.dot(mixed_flat, w_out, preferred_element_type=jnp.float32) + b_out.astype(
        jnp.float32
    )
    first_norm, scaled_one, inverse_one = norm_forward(
        tokens.astype(jnp.float32) + attn_out,
        gain_one.astype(jnp.float32),
        shift_one.astype(jnp.float32),
    )
    first_low = first_norm.astype(jnp.bfloat16)
    ffn_set = (
        lax.all_gather(up_weight, "fsdp", axis=0, tiled=True),
        lax.all_gather(up_bias, "fsdp", axis=0, tiled=True),
        lax.all_gather(down_weight, "fsdp", axis=0, tiled=True),
        lax.all_gather(down_bias, "fsdp", axis=0, tiled=True),
        lax.all_gather(norm2_gain, "fsdp", axis=0, tiled=True),
        lax.all_gather(norm2_bias, "fsdp", axis=0, tiled=True),
    )
    w_up, b_up, w_down, b_down, gain_two, shift_two = ffn_set
    hidden_in = jnp.dot(first_low, w_up, preferred_element_type=jnp.float32) + b_up.astype(
        jnp.float32
    )
    hidden, gelu_back = jax.vjp(lambda inputs: jax.nn.gelu(inputs, approximate=False), hidden_in)
    hidden_low = hidden.astype(jnp.bfloat16)
    branch = jnp.dot(hidden_low, w_down, preferred_element_type=jnp.float32) + b_down.astype(
        jnp.float32
    )
    second_norm, scaled_two, inverse_two = norm_forward(
        first_norm + branch, gain_two.astype(jnp.float32), shift_two.astype(jnp.float32)
    )
    output = (second_norm * row_valid).astype(jnp.bfloat16)
    attn_back = (
        lax.all_gather(qkv_weight, "fsdp", axis=0, tiled=True),
        lax.all_gather(q_bias, "fsdp", axis=0, tiled=True),
        lax.all_gather(v_bias, "fsdp", axis=0, tiled=True),
        lax.all_gather(out_weight, "fsdp", axis=0, tiled=True),
        lax.all_gather(out_bias, "fsdp", axis=0, tiled=True),
        lax.all_gather(bias_table, "fsdp", axis=0, tiled=True),
        lax.all_gather(norm1_gain, "fsdp", axis=0, tiled=True),
        lax.all_gather(norm1_bias, "fsdp", axis=0, tiled=True),
    )
    ffn_back = (
        lax.all_gather(up_weight, "fsdp", axis=0, tiled=True),
        lax.all_gather(up_bias, "fsdp", axis=0, tiled=True),
        lax.all_gather(down_weight, "fsdp", axis=0, tiled=True),
        lax.all_gather(down_bias, "fsdp", axis=0, tiled=True),
        lax.all_gather(norm2_gain, "fsdp", axis=0, tiled=True),
        lax.all_gather(norm2_bias, "fsdp", axis=0, tiled=True),
    )
    qkv_back, _, _, out_back, _, table_back, gain_one_back, _ = attn_back
    up_back, _, down_back, _, gain_two_back, _ = ffn_back
    grad_second = cotangent.astype(jnp.float32) * row_valid
    g_gain_two, g_shift_two, grad_sum_two = norm_backward(
        grad_second, scaled_two, inverse_two, gain_two_back.astype(jnp.float32)
    )
    grad_branch = grad_sum_two.astype(jnp.bfloat16)
    g_down = contract_rows(hidden_low, grad_branch)
    g_down_bias = column_sum(grad_branch)
    grad_hidden = contract_cols(grad_branch, down_back)
    grad_hidden_in = gelu_back(grad_hidden)[0].astype(jnp.bfloat16)
    g_up = contract_rows(first_low, grad_hidden_in)
    g_up_bias = column_sum(grad_hidden_in)
    grad_first = grad_sum_two + contract_cols(grad_hidden_in, up_back)
    g_gain_one, g_shift_one, grad_sum_one = norm_backward(
        grad_first, scaled_one, inverse_one, gain_one_back.astype(jnp.float32)
    )
    grad_attn = grad_sum_one.astype(jnp.bfloat16)
    g_out = contract_rows(mixed_flat, grad_attn)
    g_out_bias = column_sum(grad_attn)
    grad_mixed = contract_cols(grad_attn, out_back).astype(jnp.bfloat16).reshape(head_shape)

    def attend_back(table_acc, window_item):
        q_one, k_one, v_one, bucket, length, logsum_one, grad_one = window_item
        scores = masked_scores(q_one, k_one, bucket, length, table_back, levels)
        attn_probs = jnp.exp(scores - logsum_one)
        grad_probs = jnp.einsum("qhd,khd->hqk", grad_one, v_one, preferred_element_type=jnp.float32)
        grad_values = jnp.einsum(
            "hqk,qhd->khd",
            attn_probs.astype(jnp.bfloat16),
            grad_one,
            preferred_element_type=jnp.float32,
        )
        row_inner = jnp.sum(attn_probs * grad_probs, axis=-1, keepdims=True)
        grad_scores = (attn_probs * (grad_probs - row_inner)).astype(jnp.bfloat16)
        grad_queries = jnp.einsum(
            "hqk,khd->qhd", grad_scores, k_one, preferred_element_type=jnp.float32
        )
        grad_keys = jnp.einsum(
            "hqk,qhd->khd", grad_scores, q_one, preferred_element_type=jnp.float32
        )
        table_acc = table_acc + table_grad(bucket, grad_scores.reshape(head_count, -1), levels)
        return (
            table_acc,
            (
                grad_queries.astype(jnp.bfloat16),
                grad_keys.astype(jnp.bfloat16),
                grad_values.astype(jnp.bfloat16),
            ),
        )

    table_start = jnp.zeros(table_back.shape, jnp.float32)
    g_table, (grad_q, grad_k, grad_v) = lax.scan(
        attend_back, table_start, (q_heads, k_heads, v_heads, buckets, lengths, logsum, grad_mixed)
    )
    grad_q = grad_q.reshape(row_count, model_width) * factor
    grad_k = grad_k.reshape(row_count, model_width)
    grad_v = grad_v.reshape(row_count, model_width)
    grad_packed = jnp.concatenate([grad_q, grad_k, grad_v], axis=1)
    g_qkv = contract_rows(tokens, grad_packed)
    g_query_bias = column_sum(grad_q)
    g_value_bias = column_sum(grad_v)
    tokens_grad = (grad_sum_one + contract_cols(grad_packed, qkv_back)).astype(jnp.bfloat16)
    row_parts = (
        lax.psum_scatter(
            g_qkv.astype(jnp.bfloat16), "fsdp", scatter_dimension=0, tiled=True
        ).astype(jnp.float32),
        lax.psum_scatter(
            g_query_bias.astype(jnp.bfloat16), "fsdp", scatter_dimension=0, tiled=True
        ).astype(jnp.float32),
        lax.psum_scatter(
            g_value_bias.astype(jnp.bfloat16), "fsdp", scatter_dimension=0, tiled=True
        ).astype(jnp.float32),
        lax.psum_scatter(
            g_out.astype(jnp.bfloat16), "fsdp", scatter_dimension=0, tiled=True
        ).astype(jnp.float32),
        lax.psum_scatter(
            g_out_bias.astype(jnp.bfloat16), "fsdp", scatter_dimension=0, tiled=True
        ).astype(jnp.float32),
        lax.psum_scatter(
            g_table.astype(jnp.bfloat16), "fsdp", scatter_dimension=0, tiled=True
        ).astype(jnp.float32),
        lax.psum_scatter(
            g_gain_one.astype(jnp.bfloat16), "fsdp", scatter_dimension=0, tiled=True
        ).astype(jnp.float32),
        lax.psum_scatter(
            g_shift_one.astype(jnp.bfloat16), "fsdp", scatter_dimension=0, tiled=True
        ).astype(jnp.float32),
        lax.psum_scatter(g_up.astype(jnp.bfloat16), "fsdp", scatter_dimension=0, tiled=True).astype(
            jnp.float32
        ),
        lax.psum_scatter(
            g_up_bias.astype(jnp.bfloat16), "fsdp", scatter_dimension=0, tiled=True
        ).astype(jnp.float32),
        lax.psum_scatter(
            g_down.astype(jnp.bfloat16), "fsdp", scatter_dimension=0, tiled=True
        ).astype(jnp.float32),
        lax.psum_scatter(
            g_down_bias.astype(jnp.bfloat16), "fsdp", scatter_dimension=0, tiled=True
        ).astype(jnp.float32),
        lax.psum_scatter(
            g_gain_two.astype(jnp.bfloat16), "fsdp", scatter_dimension=0, tiled=True
        ).astype(jnp.float32),
        lax.psum_scatter(
            g_shift_two.astype(jnp.bfloat16), "fsdp", scatter_dimension=0, tiled=True
        ).astype(jnp.float32),
    )
    finals = (
        lax.psum(row_parts[0].astype(jnp.bfloat16), "dp").astype(jnp.float32),
        lax.psum(row_parts[1].astype(jnp.bfloat16), "dp").astype(jnp.float32),
        lax.psum(row_parts[2].astype(jnp.bfloat16), "dp").astype(jnp.float32),
        lax.psum(row_parts[3].astype(jnp.bfloat16), "dp").astype(jnp.float32),
        lax.psum(row_parts[4].astype(jnp.bfloat16), "dp").astype(jnp.float32),
        lax.psum(row_parts[5].astype(jnp.bfloat16), "dp").astype(jnp.float32),
        lax.psum(row_parts[6].astype(jnp.bfloat16), "dp").astype(jnp.float32),
        lax.psum(row_parts[7].astype(jnp.bfloat16), "dp").astype(jnp.float32),
        lax.psum(row_parts[8].astype(jnp.bfloat16), "dp").astype(jnp.float32),
        lax.psum(row_parts[9].astype(jnp.bfloat16), "dp").astype(jnp.float32),
        lax.psum(row_parts[10].astype(jnp.bfloat16), "dp").astype(jnp.float32),
        lax.psum(row_parts[11].astype(jnp.bfloat16), "dp").astype(jnp.float32),
        lax.psum(row_parts[12].astype(jnp.bfloat16), "dp").astype(jnp.float32),
        lax.psum(row_parts[13].astype(jnp.bfloat16), "dp").astype(jnp.float32),
    )
    return (
        output,
        tokens_grad,
        finals[0],
        finals[1],
        finals[2],
        finals[3],
        finals[4],
        finals[5],
        finals[6],
        finals[7],
        finals[8],
        finals[9],
        finals[10],
        finals[11],
        finals[12],
        finals[13],
    )


def solution(mesh):
    placed = (
        P(("dp", "fsdp"), None),
        P(("dp", "fsdp")),
        P(("dp", "fsdp"), None, None, None),
        P("fsdp", None),
        P("fsdp"),
        P("fsdp"),
        P("fsdp", None),
        P("fsdp"),
        P("fsdp", None),
        P("fsdp"),
        P("fsdp"),
        P("fsdp", None),
        P("fsdp"),
        P("fsdp", None),
        P("fsdp"),
        P("fsdp"),
        P("fsdp"),
        P(("dp", "fsdp"), None),
    )
    return jax.shard_map(
        per_device,
        mesh=mesh,
        in_specs=placed,
        out_specs=(
            P(("dp", "fsdp"), None),
            P(("dp", "fsdp"), None),
            P("fsdp", None),
            P("fsdp"),
            P("fsdp"),
            P("fsdp", None),
            P("fsdp"),
            P("fsdp", None),
            P("fsdp"),
            P("fsdp"),
            P("fsdp", None),
            P("fsdp"),
            P("fsdp", None),
            P("fsdp"),
            P("fsdp"),
            P("fsdp"),
        ),
        check_vma=False,
    )
```

profile of v0, /device:TPU:1, one launch (start us, length us, event | category | flops | bytes accessed | tf_op | source)
XLA Modules:
  0.0 660.6 jit_solution(8075170376899901769)
XLA Ops:
  10.8 3.7 all-gather.1
  14.6 3.2 all-gather
  17.8 3.2 all-gather.3
  21.1 3.5 all-gather.4
  24.6 3.5 all-gather.5
  28.2 3.5 all-gather.7
  31.8 3.5 all-gather.8
  35.3 3.5 all-gather.9
  38.9 3.6 all-gather.6
  42.6 3.6 all-gather.2
  47.4 8.3 %fusion.3 = f32[262144,12]{0,1:T(8,128)} fusion(s32[262144]{0:T(1024)S(1)} %bitcast.88, bf16[96,12]{0,1:T(8,128)(2,1)S(1)} %reshape.168), kind=kOutput, calls=%fused_computation.8 | convolution fusion | flops 209715200 | bytes 13633792 | tf_op jit(solution)/shard_map/while/body/eval_jaxpr/dot_general | solution.py:37
  55.8 13.2 %convolution_add_fusion.1 = f32[262144,12]{0,1:T(8,128)} fusion(f32[262144,12]{0,1:T(8,128)} %fusion.3, s32[262144]{0:T(1024)S(1)} %bitcast.92, bf16[96,12]{0,1:T(8,128)(2,1)S(1)} %reshape.168), kind=kOutput, calls=%fused_computation.1 | convolution fusion | flops 212860928 | bytes 26216704 | tf_op jit(solution)/shard_map/while/body/eval_jaxpr/dot_general | solution.py:37
  69.0 13.7 %convolution_add_fusion = f32[262144,12]{0,1:T(8,128)} fusion(f32[262144,12]{0,1:T(8,128)} %convolution_add_fusion.1, s32[262144]{0:T(1024)S(1)} %bitcast.90, bf16[96,12]{0,1:T(8,128)(2,1)S(1)} %reshape.168), kind=kOutput, calls=%fused_computation | convolution fusion | flops 212860928 | bytes 26216704 | tf_op jit(solution)/shard_map/while/body/eval_jaxpr/dot_general | solution.py:37
  82.6 18.2 %copy.82 = f32[2,8,512,512]{3,2,1,0:T(8,128)} copy(f32[2,8,512,512]{3,1,2,0:T(8,128)} %bitcast.76) | data formatting | bytes 33554432
  100.8 10.8 %slice.67 = f32[12,512,512]{2,1,0:T(8,128)} slice(f32[16,512,512]{2,1,0:T(8,128)} %bitcast.77), slice={[0:12], [0:512], [0:512]} | slice | bytes 25165824 | tf_op jit(solution)/shard_map/while/body/eval_jaxpr/reshape | solution.py:61
  111.6 12.6 %copy.63 = f32[12,512,512]{1,2,0:T(8,128)} copy(f32[12,512,512]{2,1,0:T(8,128)} %slice.67) | data formatting | bytes 25165824 | tf_op jit(solution)/shard_map/while/body/eval_jaxpr/reshape | solution.py:61
  124.3 4.0 fusion.60
  129.5 6.5 fusion.55
  140.6 3.6 fusion.32
  147.2 2.9 all-gather.19.cloned.1.call-done
  150.1 19.6 %multiply_convert_fusion.1 = (bf16[512,3072]{1,0:T(8,128)(2,1)}, f32[512,3072]{1,0:T(8,128)}, f32[512,3072]{1,0:T(8,128)}) fusion(f32[3072]{0:T(1024)S(1)} %bitcast.104, bf16[768,3072]{1,0:T(8,128)(2,1)} %all-gather.19.cloned.1.call-done, f32[512,768]{1,0:T(8,128)S(1)} %get-tuple-element.182, f32[768]{0:T(1024)S(1)} %reshape.187, f32[768]{0:T(1024)S(1)} %reshape.186, ...), kind=kOutput, calls=%fused_computation.28 | convolution fusion | flops 2521694208 | bytes 22042624 | tf_op jit(solution)/shard_map/dot_general | solution.py:169
  169.8 44.5 %all-gather.21.cloned.1.call-done = bf16[3072,768]{1,0:T(8,128)(2,1)} async-done(((bf16[1536,768]{1,0:T(8,128)(2,1)}), bf16[3072,768]{1,0:T(8,128)(2,1)}) %all-gather.21.cloned.1.call-update) | async-done | bytes 4718608 | tf_op jit(solution)/shard_map/all_gather | solution.py:163
  214.2 6.2 fusion.57
  223.2 8.8 %fusion.59 = (bf16[3072]{0:T(1024)(128)(2,1)S(1)}, bf16[512,3072]{1,0:T(8,128)(2,1)S(1)}) fusion(f32[512,3072]{1,0:T(8,128)} %get-tuple-element.172, bf16[3072,768]{1,0:T(8,128)(2,1)S(1)} %bitcast.110, f32[512,768]{1,0:T(8,128)S(1)} %get-tuple-element.168, f32[512,3072]{1,0:T(8,128)} %get-tuple-element.183, f32[3072]{0:T(1024)S(1)} %bitcast.105), kind=kOutput, calls=%fused_computation.127 | convolution fusion | flops 2441475072 | bytes 22038528 | tf_op jit(solution)/shard_map/dot_general | solution.py:73
  232.0 3.1 multiply_reduce_fusion.2
  238.0 6.9 %bitcast_reduce_fusion = (bf16[12,64]{1,0:T(8,128)(2,1)S(1)}, bf16[12,64,512]{2,1,0:T(8,128)(2,1)S(1)}) fusion(bf16[512,12,64]{0,2,1:T(8,128)(2,1)S(1)} %bitcast.86, f32[12,512,512]{1,2,0:T(8,128)} %copy-done, f32[12,512]{1,0:T(8,128)S(1)} %log_add_fusion), kind=kOutput, calls=%fused_computation.89 | convolution fusion | flops 409730304 | bytes 14181888 | tf_op jit(solution)/shard_map/while/body/eval_jaxpr/hqk,qhd->khd/dot_general | solution.py:226
  244.9 9.2 %multiply_reduce_fusion = (f32[12,512]{1,0:T(8,128)S(1)}, f32[12,512,512]{1,2,0:T(8,128)}) fusion(f32[12,512,512]{1,2,0:T(8,128)} %copy-done, f32[12,512]{1,0:T(8,128)S(1)} %log_add_fusion, bf16[512,12,64]{0,2,1:T(8,128)(2,1)S(1)} %bitcast.87, bf16[512,12,64]{0,2,1:T(8,128)(2,1)S(1)} %bitcast.95), kind=kOutput, calls=%fused_computation.16 | convolution fusion | flops 412084224 | bytes 26787840 | tf_op jit(solution)/shard_map/while/body/eval_jaxpr/qhd,khd->hqk/dot_general | solution.py:225
  254.1 7.0 %multiply_convert_fusion = bf16[12,512,512]{1,2,0:T(8,128)(2,1)S(1)} fusion(f32[12,512,512]{1,2,0:T(8,128)} %get-tuple-element.188, f32[12,512,512]{1,2,0:T(8,128)S(1)} %bitcast.75, f32[12,512]{1,0:T(8,128)S(1)} %get-tuple-element.187, f32[12,512]{1,0:T(8,128)S(1)} %log_add_fusion), kind=kLoop, calls=%fused_computation.15 | loop fusion | flops 12582912 | bytes 31506432 | tf_op jit(solution)/shard_map/while/body/eval_jaxpr/convert_element_type | solution.py:233
  265.3 3.8 fusion.22
  269.1 5.9 copy.75
  275.0 3.0 convolution_convert_fusion.3
  278.1 6.7 %convolution_convert_fusion = bf16[3072,768]{1,0:T(8,128)(2,1)} fusion(bf16[512,3072]{1,0:T(8,128)(2,1)} %get-tuple-element.171, f32[512,768]{1,0:T(8,128)S(1)} %copy-done.22), kind=kOutput, calls=%fused_computation.43 | convolution fusion | flops 2418671616 | bytes 9437184 | tf_op jit(solution)/shard_map/dot_general | solution.py:67
  286.3 6.4 convolution_convert_fusion.1
  292.8 9.1 %copy.69 = bf16[12,512,512]{2,1,0:T(8,128)(2,1)} copy(bf16[12,512,512]{1,2,0:T(8,128)(2,1)} %copy-done.1) | data formatting | bytes 12582912 | tf_op jit(solution)/shard_map/while/body/eval_jaxpr/convert_element_type | solution.py:233
  301.9 6.9 %pad.6 = bf16[16,512,512]{2,1,0:T(8,128)(2,1)} pad(bf16[12,512,512]{2,1,0:T(8,128)(2,1)} %copy.69, bf16[]{:T(256)} %constant.128.clone.1), padding=0_4x0_0x0_0 | pad | bytes 14680066
  308.8 11.4 %copy.83 = bf16[2,8,512,512]{3,1,2,0:T(8,128)(2,1)} copy(bf16[2,8,512,512]{3,2,1,0:T(8,128)(2,1)} %bitcast.78) | data formatting | bytes 16777216
  320.2 7.9 %fusion.37 = bf16[32,12]{0,1:T(8,128)(2,1)S(1)} fusion(bf16[12,262144]{1,0:T(8,128)(2,1)} %bitcast.81, s32[262144]{0:T(1024)S(1)} %bitcast.91), kind=kOutput, calls=%fused_computation.85 | convolution fusion | flops 209715584 | bytes 7340800 | tf_op jit(solution)/shard_map/while/body/eval_jaxpr/dot_general | solution.py:50
  328.2 5.3 fusion.36
  333.5 5.3 fusion.35
  339.7 4.0 copy.76
  343.6 3.7 reduce-scatter.10.cloned.1.call-done
  347.4 62.9 %reduce-scatter.14.cloned.1.call-done = bf16[1536,768]{1,0:T(8,128)(2,1)} async-done(((bf16[3072,768]{1,0:T(8,128)(2,1)}), bf16[1536,768]{1,0:T(8,128)(2,1)}) %reduce-scatter.14.cloned.1.call-update) | async-done | bytes 2359312 | tf_op jit(solution)/shard_map/reduce_scatter | solution.py:293
  410.3 63.0 %reduce-scatter.12.cloned.1.call-done = bf16[384,3072]{1,0:T(8,128)(2,1)} async-done(((bf16[768,3072]{1,0:T(8,128)(2,1)}), bf16[384,3072]{1,0:T(8,128)(2,1)}) %reduce-scatter.12.cloned.1.call-update) | async-done | bytes 2359312 | tf_op jit(solution)/shard_map/reduce_scatter | solution.py:287
  475.4 5.6 all-reduce.11
  481.6 5.2 add_convert_fusion.1
  487.6 59.8 %all-reduce.9 = (bf16[384]{0:T(512)(128)(2,1)S(1)}, bf16[384]{0:T(512)(128)(2,1)S(1)}, bf16[384]{0:T(512)(128)(2,1)S(1)}, bf16[48,12]{0,1:T(8,128)(2,1)S(1)}, bf...) all-reduce(bf16[384]{0:T(512)(128)(2,1)S(1)} %dynamic-slice.2, ...), channel_id=1, replica_groups=mesh['dp'=16,'fsdp'=2] {'dp'}, use_global_device_ids=true, to_apply=%region_15.16 | all-reduce | flops 5184 | bytes 20736 | tf_op jit(solution)/shard_map/psum | solution.py:308
  553.3 88.6 %all-reduce.14.cloned.1.call-done = (bf16[384,2304]{0,1:T(8,128)(2,1)}, bf16[384,768]{1,0:T(8,128)(2,1)}, bf16[384,3072]{1,0:T(8,128)(2,1)}, bf16[1536,768]{1,0:T(8,128)(2,1)}) async-done(((bf16[384,2304]{0,1:T(8,128)(2,1)}, bf16[384,768]{1,0:T(8,128)(2,1)}, bf16[384,3072]{1,0:T(8,128)(2,1)}, bf16[1536,768]{1,0:T(8,128)(2,1)}), (bf16[384,2304]{0,1:T(8,128)(2,1)}, bf16[384,768]{1,0:T(8,128)(2,1)}, ...) | async-done | bytes 7077904 | tf_op jit(solution)/shard_map/psum | solution.py:307
  644.2 4.0 copy.70
  (209 shorter events, 40.8 us)
Async XLA Ops:
  7.2 3.6 copy-start.28
  7.2 7.4 %copy-start.29 = (bf16[384]{0:T(512)(128)(2,1)S(1)}, bf16[384]{0:T(512)(128)(2,1)}, u32[]{:S(2)}) copy-start(bf16[384]{0:T(512)(128)(2,1)} %param.23) | copy-start | bytes 2308
  7.2 10.6 %copy-start.30 = (bf16[384]{0:T(512)(128)(2,1)S(1)}, bf16[384]{0:T(512)(128)(2,1)}, u32[]{:S(2)}) copy-start(bf16[384]{0:T(512)(128)(2,1)} %param.25) | copy-start | bytes 2308
  7.2 13.8 %copy-start.31 = (bf16[384]{0:T(512)(128)(2,1)S(1)}, bf16[384]{0:T(512)(128)(2,1)}, u32[]{:S(2)}) copy-start(bf16[384]{0:T(512)(128)(2,1)} %param.27) | copy-start | bytes 2308
  7.2 17.4 %copy-start.32 = (bf16[384]{0:T(512)(128)(2,1)S(1)}, bf16[384]{0:T(512)(128)(2,1)}, u32[]{:S(2)}) copy-start(bf16[384]{0:T(512)(128)(2,1)} %param.28) | copy-start | bytes 2308
  7.2 21.0 %copy-start.33 = (bf16[384]{0:T(512)(128)(2,1)S(1)}, bf16[384]{0:T(512)(128)(2,1)}, u32[]{:S(2)}) copy-start(bf16[384]{0:T(512)(128)(2,1)} %param.32) | copy-start | bytes 2308
  7.2 24.5 %copy-start.34 = (bf16[384]{0:T(512)(128)(2,1)S(1)}, bf16[384]{0:T(512)(128)(2,1)}, u32[]{:S(2)}) copy-start(bf16[384]{0:T(512)(128)(2,1)} %param.33) | copy-start | bytes 2308
  7.3 28.1 %copy-start.35 = (bf16[384]{0:T(512)(128)(2,1)S(1)}, bf16[384]{0:T(512)(128)(2,1)}, u32[]{:S(2)}) copy-start(bf16[384]{0:T(512)(128)(2,1)} %param.34) | copy-start | bytes 2308
  7.3 31.6 %copy-start.27 = (bf16[1536]{0:T(1024)(128)(2,1)S(1)}, bf16[1536]{0:T(1024)(128)(2,1)}, u32[]{:S(2)}) copy-start(bf16[1536]{0:T(1024)(128)(2,1)} %param.30) | copy-start | bytes 9220
  7.3 35.3 %copy-start.26 = (bf16[48,12]{0,1:T(8,128)(2,1)S(1)}, bf16[48,12]{0,1:T(8,128)(2,1)}, u32[]{:S(2)}) copy-start(bf16[48,12]{0,1:T(8,128)(2,1)} %param.26) | copy-start | bytes 3460
  7.3 39.0 %copy-start.15 = (s32[1,3,512,512]{3,2,1,0:T(8,128)S(1)}, s32[1,3,512,512]{3,2,1,0:T(8,128)}, u32[]{:S(2)}) copy-start(s32[1,3,512,512]{3,2,1,0:T(8,128)} %param.20) | copy-start | bytes 9437188
  7.3 117.0 %all-gather.15.cloned.1.call-start = ((), (), s32[]{:S(2)}) async-start(), calls=%async_computation.5 | async-start | bytes 5308416 | tf_op jit(solution)/shard_map/all_gather | solution.py:103
  8.0 136.2 %all-gather.17.cloned.1.call-start = ((), (), s32[]{:S(2)}) async-start(), calls=%async_computation.6 | async-start | bytes 1769472 | tf_op jit(solution)/shard_map/all_gather | solution.py:106
  8.8 141.4 %all-gather.19.cloned.1.call-start = ((), (), s32[]{:S(2)}) async-start(), calls=%async_computation.7 | async-start | bytes 7077888 | tf_op jit(solution)/shard_map/all_gather | solution.py:161
  9.5 204.7 %all-gather.21.cloned.1.call-start = ((), (), s32[]{:S(2)}) async-start(), calls=%async_computation.8 | async-start | bytes 7077888 | tf_op jit(solution)/shard_map/all_gather | solution.py:163
  10.1 329.6 %reduce-scatter.16.cloned.1.call-start = ((), (), s32[]{:S(2)}) async-start(), calls=%async_computation.12 | async-start | bytes 5308416
  46.8 22.1 %copy-start.9 = (s32[64,4,8,128]{3,1,2,0:T(4,128)}, s32[64,4,8,128]{3,1,2,0:T(4,128)S(1)}, u32[]{:S(2)}) copy-start(s32[64,4,8,128]{3,1,2,0:T(4,128)S(1)} %copy.81) | copy-start | bytes 3145732
  47.1 8.6 %copy-start.7 = (s32[64,4,8,128]{3,1,2,0:T(4,128)}, s32[64,4,8,128]{3,1,2,0:T(4,128)S(1)}, u32[]{:S(2)}) copy-start(s32[64,4,8,128]{3,1,2,0:T(4,128)S(1)} %copy.79) | copy-start | bytes 3145732
  47.4 8.4 %copy-start.11 = (s32[64,4,8,128]{3,1,2,0:T(4,128)}, s32[64,4,8,128]{3,1,2,0:T(4,128)S(1)}, u32[]{:S(2)}) copy-start(s32[64,4,8,128]{3,1,2,0:T(4,128)S(1)} %copy.80) | copy-start | bytes 3145732
  111.6 12.7 %copy-start.37 = (bf16[512,768]{1,0:T(8,128)(2,1)S(1)}, bf16[512,768]{1,0:T(8,128)(2,1)}, u32[]{:S(2)}) copy-start(bf16[512,768]{1,0:T(8,128)(2,1)} %param.18) | copy-start | bytes 2359300
  129.5 8.3 %copy-start.13 = (bf16[512,768]{0,1:T(8,128)(2,1)}, bf16[512,768]{0,1:T(8,128)(2,1)S(1)}, u32[]{:S(2)}) copy-start(bf16[512,768]{0,1:T(8,128)(2,1)S(1)} %copy.59) | copy-start | bytes 2359300
  136.0 4.6 copy-start
  146.9 88.3 %copy-start.5 = (f32[512,768]{1,0:T(8,128)}, f32[512,768]{1,0:T(8,128)S(1)}, u32[]{:S(2)}) copy-start(f32[512,768]{1,0:T(8,128)S(1)} %get-tuple-element.182) | copy-start | bytes 4718596
  214.2 8.9 %slice-start.5 = ((s8[4718592]{0:T(1024)(128)(4,1)}), s8[4194304]{0:T(1024)(128)(4,1)S(1)}, s32[]{:S(2)}) async-start(s8[4718592]{0:T(1024)(128)(4,1)} %bitcast.109), calls=%async_computation.20 | async-start | bytes 8388608
  214.2 6.5 copy-start.16
  214.2 9.0 %slice-start.6 = ((s8[4718592]{0:T(1024)(128)(4,1)}), s8[524288]{0:T(1024)(128)(4,1)S(1)}, s32[]{:S(2)}) async-start(s8[4718592]{0:T(1024)(128)(4,1)} %bitcast.109), calls=%async_computation.21 | async-start | bytes 1048576
  222.5 9.5 %slice-start.3 = ((s8[4718592]{0:T(1024)(128)(4,1)}), s8[4194304]{0:T(1024)(128)(4,1)S(1)}, s32[]{:S(2)}) async-start(s8[4718592]{0:T(1024)(128)(4,1)} %bitcast.107), calls=%async_computation.18 | async-start | bytes 8388608
  223.2 8.8 %copy-start.21 = (f32[512,768]{1,0:T(8,128)}, f32[512,768]{1,0:T(8,128)S(1)}, u32[]{:S(2)}) copy-start(f32[512,768]{1,0:T(8,128)S(1)} %get-tuple-element.168) | copy-start | bytes 4718596
  223.2 8.8 %slice-start.4 = ((s8[4718592]{0:T(1024)(128)(4,1)}), s8[524288]{0:T(1024)(128)(4,1)S(1)}, s32[]{:S(2)}) async-start(s8[4718592]{0:T(1024)(128)(4,1)} %bitcast.107), calls=%async_computation.19 | async-start | bytes 1048576
  238.0 6.9 %copy-start.14 = (bf16[512,768]{0,1:T(8,128)(2,1)S(1)}, bf16[512,768]{0,1:T(8,128)(2,1)}, u32[]{:S(2)}) copy-start(bf16[512,768]{0,1:T(8,128)(2,1)} %copy-done.13) | copy-start | bytes 2359300
  238.0 16.1 %slice-start = ((s8[12582912]{0:T(1024)(128)(4,1)}), s8[4194304]{0:T(1024)(128)(4,1)S(1)}, s32[]{:S(2)}) async-start(s8[12582912]{0:T(1024)(128)(4,1)} %bitcast.74), calls=%async_computation.15 | async-start | bytes 8388608
  238.0 16.1 %slice-start.1 = ((s8[12582912]{0:T(1024)(128)(4,1)}), s8[4194304]{0:T(1024)(128)(4,1)S(1)}, s32[]{:S(2)}) async-start(s8[12582912]{0:T(1024)(128)(4,1)} %bitcast.74), calls=%async_computation.16 | async-start | bytes 8388608
  244.9 19.5 %copy-start.23 = (bf16[12,64,512]{2,1,0:T(8,128)(2,1)}, bf16[12,64,512]{2,1,0:T(8,128)(2,1)S(1)}, u32[]{:S(2)}) copy-start(bf16[12,64,512]{2,1,0:T(8,128)(2,1)S(1)} %get-tuple-element.192) | copy-start | bytes 2359300
  244.9 9.2 %slice-start.2 = ((s8[12582912]{0:T(1024)(128)(4,1)}), s8[4194304]{0:T(1024)(128)(4,1)S(1)}, s32[]{:S(2)}) async-start(s8[12582912]{0:T(1024)(128)(4,1)} %bitcast.74), calls=%async_computation.17 | async-start | bytes 8388608
  269.1 6.0 copy-start.4
  275.0 72.4 %reduce-scatter.10.cloned.1.call-start = ((), (), s32[]{:S(2)}) async-start(), calls=%async_computation.9 | async-start | bytes 1769472 | tf_op jit(solution)/shard_map/reduce_scatter | solution.py:272
  278.1 132.2 %reduce-scatter.14.cloned.1.call-start = ((), (), s32[]{:S(2)}) async-start(), calls=%async_computation.11 | async-start | bytes 7077888 | tf_op jit(solution)/shard_map/reduce_scatter | solution.py:293
  284.9 188.3 %reduce-scatter.12.cloned.1.call-start = ((), (), s32[]{:S(2)}) async-start(), calls=%async_computation.10 | async-start | bytes 7077888 | tf_op jit(solution)/shard_map/reduce_scatter | solution.py:287
  292.8 194.1 %reduce-scatter.18.cloned.1.call-start = ((), (), s32[]{:S(2)}) async-start(), calls=%async_computation.13 | async-start | bytes 36864
  308.8 11.4 %copy-start.10 = (s32[64,4,8,128]{3,1,2,0:T(4,128)S(1)}, s32[64,4,8,128]{3,1,2,0:T(4,128)}, u32[]{:S(2)}) copy-start(s32[64,4,8,128]{3,1,2,0:T(4,128)} %copy-done.9) | copy-start | bytes 3145732
  320.2 8.0 %copy-start.2 = (bf16[2,8,512,512]{3,1,2,0:T(8,128)(2,1)S(1)}, bf16[2,8,512,512]{3,1,2,0:T(8,128)(2,1)}, u32[]{:S(2)}) copy-start(bf16[2,8,512,512]{3,1,2,0:T(8,128)(2,1)} %copy.83) | copy-start | bytes 25165828
  320.2 8.0 %copy-start.12 = (s32[64,4,8,128]{3,1,2,0:T(4,128)S(1)}, s32[64,4,8,128]{3,1,2,0:T(4,128)}, u32[]{:S(2)}) copy-start(s32[64,4,8,128]{3,1,2,0:T(4,128)} %copy-done.11) | copy-start | bytes 3145732
  328.2 5.3 copy-start.8
  339.6 133.7 %copy-start.39 = (u32[32]{0:T(128)S(1)}, u32[32]{0:T(128)}, u32[]{:S(2)}) copy-start(u32[32]{0:T(128)} %constant.133) | copy-start | bytes 388
  339.6 142.1 %copy-start.18 = (bf16[12,64,512]{2,1,0:T(8,128)(2,1)S(1)}, bf16[12,64,512]{2,1,0:T(8,128)(2,1)}, u32[]{:S(2)}) copy-start(bf16[12,64,512]{2,1,0:T(8,128)(2,1)} %copy-done.17) | copy-start | bytes 2359300
  339.6 142.0 %copy-start.24 = (bf16[12,64,512]{2,1,0:T(8,128)(2,1)S(1)}, bf16[12,64,512]{2,1,0:T(8,128)(2,1)}, u32[]{:S(2)}) copy-start(bf16[12,64,512]{2,1,0:T(8,128)(2,1)} %copy-done.23) | copy-start | bytes 2359300
  339.6 302.2 %all-reduce.14.cloned.1.call-start = ((), (), s32[]{:S(2)}) async-start(), calls=%async_computation.14 | async-start | bytes 14155776 | tf_op jit(solution)/shard_map/psum | solution.py:307
  641.9 6.3 copy-start.20
  (10 other events, 20.8 us)
Sparse Core Ops, SparseCore 0:
  9.7 51.8 all-gather.14
  63.1 22.7 all-gather.16
  87.5 62.6 all-gather.18
  151.5 62.6 all-gather.20
  275.1 47.6 reduce-scatter.15
  325.6 21.7 reduce-scatter.9
  350.2 59.9 reduce-scatter.13
  413.2 59.9 reduce-scatter.11
  475.5 9.3 reduce-scatter.17
  489.3 152.5 all-reduce.13
where the time goes:
time: 671 us; the launch traced here: 661 us
  waiting for transfers between devices  268 us (40%)
  matrix products  153 us (23%)
  blocking collectives  100 us (15%)
  local copies, waits for them, and re-layouts  94.6 us (14%)
  other arithmetic  26.4 us (4%)
  between operations  17.2 us (3%)
    psum x1, waiting for transfers between devices, per_device(): lax.psum(row_parts[0].astype(jnp.bfloat16), 'dp').astype(jnp.float32)  88.6 us
    reduce_scatter x1, waiting for transfers between devices, per_device(): lax.psum_scatter(g_up.astype(jnp.bfloat16), 'fsdp', scatter_dimension=0,...  63 us
    reduce_scatter x1, waiting for transfers between devices, per_device(): lax.psum_scatter(g_down.astype(jnp.bfloat16), 'fsdp', scatter_dimension=0...  62.9 us
    unnamed x128, local copies, waits for them, and re-layouts  60.6 us
    psum x1, blocking collectives, per_device(): lax.psum(row_parts[1].astype(jnp.bfloat16), 'dp').astype(jnp.float32)  59.8 us
    all_gather x1, waiting for transfers between devices, per_device(): lax.all_gather(down_weight, 'fsdp', axis=0, tiled=True)  44.5 us
    dot_general x3, matrix products, pair_bias(): lax.dot_general(table_rows, onehot, (((0,), (0,)), ((), ())), preferred_e...  35.2 us
    reshape x2, local copies, waits for them, and re-layouts, masked_scores(): pair_bias(bucket, table, levels).reshape(head_count, window_len, window_len)  23.5 us
  transfers between devices with their start and end apart: 10, of which 6 were waited for; matrix products, arithmetic and copies ran while one was open for 30% of the time, Pallas kernels for 0%

commit v1 on v0

v1 whole, which is shorter than its diff:
```python
import functools

import jax
import jax.numpy as jnp
from jax import lax
from jax.experimental import pallas as pl
from jax.experimental.pallas import tpu as pltpu
from jax.sharding import PartitionSpec as P

EPSILON = 1e-05
MASKED = -1000000000.0
BF = jnp.bfloat16
F32 = jnp.float32
NN = (((1,), (0,)), ((), ()))
NT = (((1,), (1,)), ((), ()))
TN = (((0,), (0,)), ((), ()))
VMEM_LIMIT = 56 * 2**20
WIDE = 128


def dg(left, right, dims):
    return lax.dot_general(left, right, dims, preferred_element_type=F32)


def onehot_rows(ids_ref, group, oh_ref, bucket_count, length):
    sub = lax.broadcasted_iota(jnp.int32, (16, length), 0)
    one = jnp.ones((16, length), BF)
    zero = jnp.zeros((16, length), BF)
    half = bucket_count // 2
    for kind in range(3):
        ids = ids_ref[kind, group]
        for pair in range(half):
            level = jnp.where(sub < 8, 2 * pair, 2 * pair + 1).astype(F32).astype(BF)
            oh_ref[pl.ds((kind * half + pair) * 16, 16), :] = jnp.where(ids == level, one, zero)


def bias_kernel(len_ref, ids_ref, table_ref, out_ref, oh_ref, *, bucket_count):
    block = pl.program_id(0)
    heads, rows, length = out_ref.shape
    valid = len_ref[0]

    def body(step, carry):
        parts = []
        for u in range(2):
            onehot_rows(ids_ref, step * 2 + u, oh_ref.at[u], bucket_count, length)
            part = dg(table_ref[...], oh_ref[u], NN)
            parts.append(part.reshape(heads, 8, length))
        bias = jnp.concatenate(parts, axis=1)
        key = lax.broadcasted_iota(jnp.int32, (1, 16, length), 1) + (block * rows + step * 16)
        out_ref[:, pl.ds(pl.multiple_of(step * 16, 16), 16), :] = jnp.where(
            key < valid, bias, MASKED
        ).astype(BF)
        return carry

    lax.fori_loop(0, rows // 16, body, 0, unroll=True)


def table_kernel(ids_ref, grad_ref, out_ref, oh_ref, *, bucket_count):
    heads, rows, length = grad_ref.shape

    @pl.when(pl.program_id(0) == 0)
    def _():
        out_ref[...] = jnp.zeros_like(out_ref)

    def body(step, carry):
        grads = grad_ref[:, pl.ds(pl.multiple_of(step * 16, 16), 16), :].astype(F32)
        total = None
        for u in range(2):
            onehot_rows(ids_ref, step * 2 + u, oh_ref.at[u], bucket_count, length)
            part = dg(
                oh_ref[u],
                grads[:, u * 8 : (u + 1) * 8, :].reshape(heads * 8, length).astype(BF),
                NT,
            )
            total = part if total is None else total + part
        out_ref[...] += total
        return carry

    lax.fori_loop(0, rows // 16, body, 0, unroll=True)


def attend_kernel(q_ref, k_ref, v_ref, bias_ref, p_ref, o_ref, *, size):
    width = q_ref.shape[1]
    lane = lax.broadcasted_iota(jnp.int32, (1, width), 1)
    q = q_ref[...]
    k = k_ref[...]
    vt = v_ref[...].T
    mixed = []
    for g in range(width // size):
        mine = (lane >= g * size) & (lane < (g + 1) * size)
        scores = dg(jnp.where(mine, k, jnp.zeros_like(k)), q, NT) + bias_ref[g].astype(F32)
        top = jnp.max(scores, axis=0, keepdims=True)
        shifted = jnp.exp(scores - top)
        norm = jnp.sum(shifted, axis=0, keepdims=True)
        probs = (shifted * (1.0 / norm)).astype(BF)
        p_ref[g] = probs
        mixed.append(dg(vt[g * size : (g + 1) * size], probs, NN))
    o_ref[...] = jnp.concatenate(mixed, axis=0).T.astype(BF)


def attend_back_kernel(
    q_ref, k_ref, v_ref, p_ref, o_ref, g_ref, out_ref, ds_ref, *, size, factor
):
    pair = pl.program_id(0)
    width = q_ref.shape[1]
    model = out_ref.shape[1] // 3
    count = width // size
    lane = lax.broadcasted_iota(jnp.int32, (1, width), 1)
    q = q_ref[...]
    v = v_ref[...]
    ob = g_ref[...]
    kt = k_ref[...].T
    product = o_ref[...].astype(F32) * ob.astype(F32)
    qs, ks, vs = [], [], []
    for g in range(count):
        mine = (lane >= g * size) & (lane < (g + 1) * size)
        spare = ((g + 1) % count) * size
        inner = jnp.sum(jnp.where(mine, product, 0.0), axis=1, keepdims=True)
        high = inner.astype(BF).astype(F32)
        extra = jnp.where(lane == spare, high, jnp.where(lane == spare + 1, inner - high, 0.0))
        minus = jnp.where((lane == spare) | (lane == spare + 1), -1.0, 0.0)
        left = jnp.where(mine, v, minus.astype(BF))
        right = jnp.where(mine, ob, extra.astype(BF))
        probs = p_ref[g]
        ds = (probs.astype(F32) * dg(left, right, NT)).astype(BF)
        ds_ref[g] = ds
        vs.append(dg(probs, ob, NN))
        ks.append(dg(ds, q, NN))
        qs.append(dg(kt[g * size : (g + 1) * size], ds, NN))

    def pick(items):
        chosen = items[0]
        for g in range(1, count):
            chosen = jnp.where(lane >= g * size, items[g], chosen)
        return chosen

    def place(start):
        return pl.ds(pl.multiple_of(start + pair * width, width), width)

    q_grad = jnp.concatenate(qs, axis=0).T.astype(BF).astype(F32) * factor
    out_ref[:, place(0)] = q_grad.astype(BF)
    out_ref[:, place(model)] = pick(ks).astype(BF)
    out_ref[:, place(2 * model)] = pick(vs).astype(BF)


def params():
    return pltpu.CompilerParams(vmem_limit_bytes=VMEM_LIMIT)


def twice(buckets):
    length = buckets.shape[-1]
    turned = jnp.swapaxes(buckets[0].astype(BF), 1, 2).reshape(3, length // 8, 1, 8, length)
    return jnp.broadcast_to(turned, (3, length // 8, 2, 8, length)).reshape(
        3, length // 8, 16, length
    )


def bias_scores(ids, valid, table, block=8):
    length = ids.shape[-1]
    bucket_count = table.shape[0] // 3
    heads = table.shape[1]
    spread = (table.T[:, None, :, None] * jnp.eye(8, dtype=BF)[None, :, None, :]).reshape(
        heads * 8, 3 * bucket_count * 8
    )
    return pl.pallas_call(
        functools.partial(bias_kernel, bucket_count=bucket_count),
        grid=(length // 8 // block,),
        in_specs=[
            pl.BlockSpec(memory_space=pltpu.SMEM),
            pl.BlockSpec((3, block, 16, length), lambda i: (0, i, 0, 0)),
            pl.BlockSpec(spread.shape, lambda i: (0, 0)),
        ],
        out_specs=pl.BlockSpec((heads, block * 8, length), lambda i: (0, i, 0)),
        out_shape=jax.ShapeDtypeStruct((heads, length, length), BF),
        scratch_shapes=[pltpu.VMEM((2, 3 * bucket_count * 8, length), BF)],
        compiler_params=params(),
        name="bias_scores",
    )(valid, ids, spread)


def table_grad(ids, grads, bucket_count, block=8):
    heads, length, _ = grads.shape
    wide = pl.pallas_call(
        functools.partial(table_kernel, bucket_count=bucket_count),
        grid=(length // 8 // block,),
        in_specs=[
            pl.BlockSpec((3, block, 16, length), lambda i: (0, i, 0, 0)),
            pl.BlockSpec((heads, block * 8, length), lambda i: (0, i, 0)),
        ],
        out_specs=pl.BlockSpec((3 * bucket_count * 8, heads * 8), lambda i: (0, 0)),
        out_shape=jax.ShapeDtypeStruct((3 * bucket_count * 8, heads * 8), F32),
        scratch_shapes=[pltpu.VMEM((2, 3 * bucket_count * 8, length), BF)],
        compiler_params=params(),
        name="table_grad",
    )(ids, grads)
    row = jnp.arange(3 * bucket_count * 8, dtype=jnp.int32) % 8
    col = jnp.arange(heads * 8, dtype=jnp.int32) % 8
    kept = jnp.where(row[:, None] == col[None, :], wide, 0.0)
    return kept.reshape(3 * bucket_count, 8, heads, 8).sum((1, 3))


def attend(qkv, bias, size):
    length = qkv.shape[0]
    model = qkv.shape[1] // 3
    blocks = model // WIDE
    group = WIDE // size
    return pl.pallas_call(
        functools.partial(attend_kernel, size=size),
        grid=(blocks,),
        in_specs=[
            pl.BlockSpec((length, WIDE), lambda i: (0, i)),
            pl.BlockSpec((length, WIDE), lambda i: (0, blocks + i)),
            pl.BlockSpec((length, WIDE), lambda i: (0, 2 * blocks + i)),
            pl.BlockSpec((group, length, length), lambda i: (i, 0, 0)),
        ],
        out_specs=[
            pl.BlockSpec((group, length, length), lambda i: (i, 0, 0)),
            pl.BlockSpec((length, WIDE), lambda i: (0, i)),
        ],
        out_shape=[
            jax.ShapeDtypeStruct((model // size, length, length), BF),
            jax.ShapeDtypeStruct((length, model), BF),
        ],
        compiler_params=params(),
        name="attend",
    )(qkv, qkv, qkv, bias)


def attend_back(qkv, probs, mixed, grad_mixed, size):
    length = qkv.shape[0]
    model = qkv.shape[1] // 3
    blocks = model // WIDE
    group = WIDE // size
    return pl.pallas_call(
        functools.partial(attend_back_kernel, size=size, factor=size**-0.5),
        grid=(blocks,),
        in_specs=[
            pl.BlockSpec((length, WIDE), lambda i: (0, i)),
            pl.BlockSpec((length, WIDE), lambda i: (0, blocks + i)),
            pl.BlockSpec((length, WIDE), lambda i: (0, 2 * blocks + i)),
            pl.BlockSpec((group, length, length), lambda i: (i, 0, 0)),
            pl.BlockSpec((length, WIDE), lambda i: (0, i)),
            pl.BlockSpec((length, WIDE), lambda i: (0, i)),
        ],
        out_specs=[
            pl.BlockSpec((length, 3 * model), lambda i: (0, 0)),
            pl.BlockSpec((group, length, length), lambda i: (i, 0, 0)),
        ],
        out_shape=[
            jax.ShapeDtypeStruct((length, 3 * model), BF),
            jax.ShapeDtypeStruct((model // size, length, length), BF),
        ],
        compiler_params=params(),
        name="attend_back",
    )(qkv, qkv, qkv, probs, mixed, grad_mixed)


class Axis:
    def __init__(self, name, total, stride, size):
        self.name = name
        self.total = total
        self.stride = stride
        self.size = size
        self.at = (lax.axis_index(name) // stride) % size

    def send(self, value, step):
        pairs = []
        for index in range(self.total):
            place = (index // self.stride) % self.size
            pairs.append((index, index + ((place + step) % self.size - place) * self.stride))
        return lax.ppermute(value, self.name, pairs)

    def peer(self, step):
        return (self.at + step) % self.size


def take(stack, index):
    return lax.dynamic_index_in_dim(stack, index, axis=0, keepdims=False)


def gather(axis, block):
    stack = jnp.zeros((axis.size,) + block.shape, block.dtype)
    stack = lax.dynamic_update_index_in_dim(stack, block, axis.at, 0)
    for step in range(1, axis.size):
        stack = lax.dynamic_update_index_in_dim(
            stack, axis.send(block, step), axis.peer(-step), 0
        )
    return stack


class Links:
    def __init__(self, dp, fsdp):
        core = 2 if dp % 2 == 0 else 1
        rest = dp // core
        near = 2 if rest % 2 == 0 else 1
        self.core = Axis("dp", dp, 1, core)
        self.near = Axis("dp", dp, core, near)
        self.far = Axis("dp", dp, core * near, rest // near)
        self.shard = Axis("fsdp", fsdp, 1, fsdp)

    def weight(self, block, after=None):
        core, near, shard = self.core, self.near, self.shard
        rows, columns = block.shape
        parts = block.reshape(core.size * near.size, rows // (core.size * near.size), columns)
        mine = take(parts, core.at * near.size + near.at)
        if after is not None:
            mine, _ = lax.optimization_barrier((mine, after))
        others = jnp.stack([shard.send(mine, step) for step in range(1, shard.size)])
        token = others
        shared = gather(core, gather(near, others))
        whole = jnp.zeros((shard.size, rows, columns), block.dtype)
        whole = lax.dynamic_update_index_in_dim(whole, block, shard.at, 0)
        for step in range(1, shard.size):
            piece = shared[:, :, step - 1].reshape(rows, columns)
            whole = lax.dynamic_update_index_in_dim(whole, piece, shard.peer(-step), 0)
        return whole.reshape(shard.size * rows, columns), token

    def vector(self, block):
        return gather(self.shard, block)

    def reduce(self, left, right):
        core, near, far, shard = self.core, self.near, self.far, self.shard
        rows = left.shape[1] // shard.size
        columns = right.shape[1] // core.size
        piece = rows // (near.size * far.size)
        shape = (shard.size, near.size, far.size, piece, columns)

        def product(index):
            return dg(left, lax.dynamic_slice_in_dim(right, index * columns, columns, 1), TN)

        total = product(core.at).reshape(shape)
        for step in range(1, core.size):
            total = total + core.send(product(core.peer(step)).astype(BF), step).reshape(shape).astype(F32)
        for axis in (shard, near, far):
            kept = take(total, axis.at)
            for step in range(1, axis.size):
                kept = kept + axis.send(take(total, axis.peer(step)).astype(BF), step).astype(F32)
            total = kept
        done = total.astype(BF)
        for axis in (far, near, core):
            done = gather(axis, done)
        done = done.reshape(core.size, rows, columns).astype(F32)
        return jnp.swapaxes(done, 0, 1).reshape(rows, core.size * columns)

    def reduce_vector(self, stack):
        shard = self.shard
        total = take(stack, shard.at)
        for step in range(1, shard.size):
            total = total + shard.send(take(stack, shard.peer(step)), step)
        for axis in (self.core, self.near, self.far):
            part = total
            for step in range(1, axis.size):
                total = total + axis.send(part, step)
        return total


def pack(items, shards):
    return jnp.concatenate([item.reshape(shards, -1) for item in items], axis=1)


def gelu_pair(inputs):
    hidden, back = jax.vjp(lambda u: jax.nn.gelu(u, approximate=False), inputs)
    return hidden, back(jnp.ones_like(inputs))[0]


def norm_forward(inputs, gain_vec, shift_vec):
    center = inputs - jnp.mean(inputs, axis=-1, keepdims=True)
    inverse = lax.rsqrt(jnp.mean(center * center, axis=-1, keepdims=True) + EPSILON)
    scaled = center * inverse
    return (scaled * gain_vec + shift_vec, scaled, inverse)


def norm_backward(grad_in, scaled, inverse, gain_vec):
    gain_grad = jnp.sum(grad_in * scaled, axis=0)
    shift_grad = jnp.sum(grad_in, axis=0)
    inner_term = grad_in * gain_vec
    centered = inner_term - jnp.mean(inner_term, axis=-1, keepdims=True)
    grad_out = inverse * (centered - scaled * jnp.mean(inner_term * scaled, axis=-1, keepdims=True))
    return (gain_grad, shift_grad, grad_out)


def column_sum(grad_low):
    return jnp.sum(grad_low.astype(F32), axis=0)


def per_device(
    dp,
    fsdp,
    tokens,
    lengths,
    buckets,
    qkv_weight,
    q_bias,
    v_bias,
    out_weight,
    out_bias,
    bias_table,
    norm1_gain,
    norm1_bias,
    up_weight,
    up_bias,
    down_weight,
    down_bias,
    norm2_gain,
    norm2_bias,
    cotangent,
):
    links = Links(dp, fsdp)
    length = buckets.shape[2]
    model = tokens.shape[1]
    heads = bias_table.shape[1]
    size = model // heads
    factor = size ** (-0.5)
    vectors = (
        bias_table,
        q_bias,
        v_bias,
        out_bias,
        norm1_gain,
        norm1_bias,
        up_bias,
        down_bias,
        norm2_gain,
        norm2_bias,
    )
    packed = links.vector(jnp.concatenate([item.reshape(-1) for item in vectors]))
    full = []
    start = 0
    for item in vectors:
        full.append(packed[:, start : start + item.size].reshape(-1))
        start += item.size
    table = full[0].reshape(-1, heads)
    b_query, b_value, b_out, gain_one, shift_one, b_up, b_down, gain_two, shift_two = [
        item.astype(F32) for item in full[1:]
    ]
    w_qkv, token = links.weight(qkv_weight)
    w_out, token = links.weight(out_weight, token)
    w_up, token = links.weight(up_weight, token)
    w_down, token = links.weight(down_weight, token)

    ids = twice(buckets)
    bias = bias_scores(ids, lengths, table)
    row_valid = (
        (jnp.arange(length, dtype=jnp.int32) < lengths[0]).astype(F32).reshape(length, 1)
    )
    shift_row = jnp.concatenate([b_query, jnp.zeros_like(b_query), b_value])
    scale_row = jnp.concatenate([jnp.full((model,), factor, F32), jnp.ones((2 * model,), F32)])
    qkv = ((dg(tokens, w_qkv, NN) + shift_row) * scale_row).astype(BF)
    probs, mixed = attend(qkv, bias, size)
    first_norm, scaled_one, inverse_one = norm_forward(
        tokens.astype(F32) + (dg(mixed, w_out, NN) + b_out), gain_one, shift_one
    )
    first_low = first_norm.astype(BF)
    hidden, slope = gelu_pair(dg(first_low, w_up, NN) + b_up)
    hidden_low = hidden.astype(BF)
    slope = slope.astype(BF)
    second_norm, scaled_two, inverse_two = norm_forward(
        first_norm + (dg(hidden_low, w_down, NN) + b_down), gain_two, shift_two
    )
    output = (second_norm * row_valid).astype(BF)

    grad_second = cotangent.astype(F32) * row_valid
    g_gain_two, g_shift_two, grad_sum_two = norm_backward(
        grad_second, scaled_two, inverse_two, gain_two
    )
    grad_branch = grad_sum_two.astype(BF)
    g_down = links.reduce(hidden_low, grad_branch)
    grad_hidden_in = (dg(grad_branch, w_down, NT) * slope.astype(F32)).astype(BF)
    g_up = links.reduce(first_low, grad_hidden_in)
    grad_first = grad_sum_two + dg(grad_hidden_in, w_up, NT)
    g_gain_one, g_shift_one, grad_sum_one = norm_backward(
        grad_first, scaled_one, inverse_one, gain_one
    )
    grad_attn = grad_sum_one.astype(BF)
    g_out = links.reduce(mixed, grad_attn)
    early = links.reduce_vector(
        pack(
            (
                column_sum(grad_attn),
                g_gain_one,
                g_shift_one,
                column_sum(grad_hidden_in),
                column_sum(grad_branch),
                g_gain_two,
                g_shift_two,
            ),
            fsdp,
        )
    )
    grad_mixed = dg(grad_attn, w_out, NT).astype(BF)
    grad_packed, grad_scores = attend_back(qkv, probs, mixed, grad_mixed, size)
    g_qkv = links.reduce(tokens, grad_packed)
    tokens_grad = (grad_sum_one + dg(grad_packed, w_qkv, NT)).astype(BF)
    g_table = table_grad(ids, grad_scores, table.shape[0] // 3)
    sums = column_sum(grad_packed)
    late = links.reduce_vector(pack((g_table, sums[:model], sums[2 * model :]), fsdp))

    def split(vector, sizes):
        pieces = []
        begin = 0
        for count in sizes:
            pieces.append(vector[begin : begin + count])
            begin += count
        return pieces

    narrow = out_bias.size
    g_out_bias, g_gain_one, g_shift_one, g_up_bias, g_down_bias, g_gain_two, g_shift_two = split(
        early, (narrow, narrow, narrow, up_bias.size, narrow, narrow, narrow)
    )
    g_table, g_query_bias, g_value_bias = split(late, (bias_table.size, narrow, narrow))
    return (
        output,
        tokens_grad,
        g_qkv,
        g_query_bias,
        g_value_bias,
        g_out,
        g_out_bias,
        g_table.reshape(bias_table.shape),
        g_gain_one,
        g_shift_one,
        g_up,
        g_up_bias,
        g_down,
        g_down_bias,
        g_gain_two,
        g_shift_two,
    )


def solution(mesh):
    rows = P(("dp", "fsdp"), None)
    mat = P("fsdp", None)
    vec = P("fsdp")
    return jax.shard_map(
        functools.partial(per_device, mesh.shape["dp"], mesh.shape["fsdp"]),
        mesh=mesh,
        in_specs=(
            rows,
            P(("dp", "fsdp")),
            P(("dp", "fsdp"), None, None, None),
            mat,
            vec,
            vec,
            mat,
            vec,
            mat,
            vec,
            vec,
            mat,
            vec,
            mat,
            vec,
            vec,
            vec,
            rows,
        ),
        out_specs=(
            rows,
            rows,
            mat,
            vec,
            vec,
            mat,
            vec,
            mat,
            vec,
            vec,
            mat,
            vec,
            mat,
            vec,
            vec,
            vec,
        ),
        check_vma=False,
    )
```

time: 671 us -> 485 us (0.72)
  waiting for transfers between devices: 268 us -> 122 us
  blocking collectives: 100 us -> 0 us
  starting transfers between devices: 0.4 us -> 96.2 us
  matrix products: 153 us -> 72.1 us
  Pallas kernels: 0 us -> 51 us
  between operations: 17.2 us -> 3.01 us
  local copies, waits for them, and re-layouts: 94.6 us -> 108 us
    reduce_scatter x3 -> x0, waiting for transfers between devices: 130 us -> none  [the longest x1 63 us: per_device(): lax.psum_scatter(g_up.astype(jnp.bfloat16), 'fsdp', scatter_dimension=0,...]
    ppermute x0 -> x69, waiting for transfers between devices: none -> 122 us  [send(): return lax.ppermute(value, self.name, pairs)]
    ppermute x0 -> x69, starting transfers between devices: none -> 96.2 us  [send(): return lax.ppermute(value, self.name, pairs)]
    psum x1 -> x0, waiting for transfers between devices: 88.6 us -> none  [per_device(): lax.psum(row_parts[0].astype(jnp.bfloat16), 'dp').astype(jnp.float32)]
    dot_general x24 -> x16, matrix products: 153 us -> 72.1 us  [dg(): return lax.dot_general(left, right, dims, preferred_element_type=F32)]
    psum x1 -> x0, blocking collectives: 59.8 us -> none  [per_device(): lax.psum(row_parts[1].astype(jnp.bfloat16), 'dp').astype(jnp.float32)]
    pallas_call x0 -> x4, Pallas kernels: none -> 51 us  [the longest x1 16.6 us: table_grad(): pl.pallas_call(functools.partial(table_kernel, bucket_count=bucket_count)...]
    all_gather x4 -> x0, waiting for transfers between devices: 47.4 us -> none  [the longest x1 44.5 us: per_device(): lax.all_gather(down_weight, 'fsdp', axis=0, tiled=True)]
  transfers between devices with their start and end apart: 10 -> 69, of which waited for: 6 -> 26; matrix products, arithmetic and copies ran while one was open for 30% -> 29% of each run, Pallas kernels for 0% -> 8%
where the time goes in v1:
time: 485 us; the launch traced here: 479 us
  waiting for transfers between devices  122 us (25%)
  local copies, waits for them, and re-layouts  108 us (22%)
  starting transfers between devices  96.2 us (20%)
  matrix products  72.1 us (15%)
  Pallas kernels  51 us (11%)
  other arithmetic  27.6 us (6%)
    ppermute x69, waiting for transfers between devices, send(): return lax.ppermute(value, self.name, pairs)  122 us
    ppermute x69, starting transfers between devices, send(): return lax.ppermute(value, self.name, pairs)  96.2 us
    dot_general x16, matrix products, dg(): return lax.dot_general(left, right, dims, preferred_element_type=F32)  72.1 us
    unnamed x103, local copies, waits for them, and re-layouts  32.1 us
    reshape x4, local copies, waits for them, and re-layouts, reduce(): return jnp.swapaxes(done, 0, 1).reshape(rows, core.size * columns)  16.8 us
    pallas_call x1, Pallas kernels, table_grad(): pl.pallas_call(functools.partial(table_kernel, bucket_count=bucket_count)...  16.6 us
    pallas_call x1, Pallas kernels, bias_scores(): pl.pallas_call(functools.partial(bias_kernel, bucket_count=bucket_count),...  11.7 us
    pallas_call x1, Pallas kernels, attend_back(): pl.pallas_call(functools.partial(attend_back_kernel, size=size, factor=si...  11.6 us
  transfers between devices with their start and end apart: 69, of which 26 were waited for; matrix products, arithmetic and copies ran while one was open for 29% of the time, Pallas kernels for 8%

profile of v1, /device:TPU:1, one launch (start us, length us, event | category | flops | bytes accessed | tf_op | source)
XLA Modules:
  0.0 479.4 jit_solution(15647068985004140317)
XLA Ops:
  1.5 6.3 %concatenate.12 = bf16[5184]{0:T(1024)(128)(2,1)S(1)} concatenate(bf16[576]{0:T(1024)(128)(2,1)S(1)} %reshape.343, bf16[384]{0:T(512)(128)(2,1)} %param.22, bf16[384]{0:T(512)(128)(2,1)} %param.23, bf16[384]{0:T(512)(128)(2,1)} %param.25, bf16[384]{0:T(512)(128)(2,1)} %param.27, bf16[384]{0:T(512)(128)(2,1)} %param.28, bf16[1536]{0:T(1024)(128)(2,1)} %param.30, ...), dimensions={0} | concatenate | bytes 20736 | tf_op jit(solution)/shard_map/concatenate | solution.py:426
  40.1 4.1 mul.189.table_ref
  46.3 11.7 %bias_scores.1.bias_ref = bf16[12,512,512]{2,1,0:T(8,128)(2,1)} custom-call(s32[1]{0:T(128)} %copy.172.len_ref, bf16[3,64,16,512]{3,2,1,0:T(8,128)(2,1)} %broadcast_bitcast_fusion.ids_ref, bf16[96,768]{1,0:T(8,128)(2,1)} %mul.189.table_ref), custom_call_target="tpu_custom_call" | custom-call | tf_op jit(solution)/shard_map/bias_scores/pallas_call | solution.py:165
  65.0 7.1 %collective-permute-done.5 = bf16[1,96,768]{2,1,0:T(8,128)(2,1)S(1)} collective-permute-done((bf16[1,96,768]{2,1,0:T(8,128)(2,1)S(1)}, bf16[1,96,768]{2,1,0:T(8,128)(2,1)S(1)}, u32[]{:S(2)}, u32[]{:S(2)}) %collective-permute-start.5) | collective-permute-done | bytes 147488 | tf_op jit(solution)/shard_map/ppermute | solution.py:271
  78.8 8.8 %collective-permute-done.8 = bf16[1,96,3072]{2,1,0:T(8,128)(2,1)S(1)} collective-permute-done((bf16[1,96,3072]{2,1,0:T(8,128)(2,1)S(1)}, bf16[1,96,3072]{2,1,0:T(8,128)(2,1)S(1)}, u32[]{:S(2)}, u32[]{:S(2)}) %collective-permute-start.8) | collective-permute-done | bytes 589856 | tf_op jit(solution)/shard_map/ppermute | solution.py:271
  87.7 4.4 collective-permute-start.9
  94.1 3.4 fusion.8.q_ref.k_ref.v_ref
  97.6 11.1 %attend.1 = (bf16[12,512,512]{2,1,0:T(8,128)(2,1)}, bf16[512,768]{1,0:T(8,128)(2,1)}) custom-call(bf16[512,2304]{1,0:T(8,128)(2,1)} %fusion.8.q_ref.k_ref.v_ref, bf16[512,2304]{1,0:T(8,128)(2,1)} %fusion.8.q_ref.k_ref.v_ref, bf16[512,2304]{1,0:T(8,128)(2,1)} %fusion.8.q_ref.k_ref.v_ref, bf16[12,512,512]{2,1,0:T(8,128)(2,1)} %bias_scores.1.bias_ref), custom_call_target="tpu_custom_call" | custom-call | tf_op jit(solution)/shard_map/attend/pallas_call | solution.py:207
  113.0 13.1 %collective-permute-done.11 = bf16[1,384,768]{2,1,0:T(8,128)(2,1)S(1)} collective-permute-done((bf16[1,384,768]{2,1,0:T(8,128)(2,1)S(1)}, bf16[1,384,768]{2,1,0:T(8,128)(2,1)S(1)}, u32[]{:S(2)}, u32[]{:S(2)}) %collective-permute-start.11) | collective-permute-done | bytes 589856 | tf_op jit(solution)/shard_map/ppermute | solution.py:271
  128.1 18.5 %multiply_convert_fusion.1 = (bf16[512,3072]{1,0:T(8,128)(2,1)S(1)}, f32[512,3072]{1,0:T(8,128)}, f32[512,3072]{1,0:T(8,128)}) fusion(f32[3072]{0:T(1024)S(1)} %copy-done.28, bf16[768,3072]{1,0:T(8,128)(2,1)S(1)} %bitcast.310, f32[512,768]{1,0:T(8,128)S(1)} %get-tuple-element.153, f32[768]{0:T(1024)S(1)} %reshape.372, f32[768]{0:T(1024)S(1)} %reshape.371, ...), kind=kOutput, calls=%fused_computation.5 | convolution fusion | flops 2521694208 | bytes 22042624 | tf_op jit(solution)/shard_map/dot_general | solution.py:22
  149.1 5.2 %fusion.93 = (f32[512]{0:T(512)S(1)}, f32[512,768]{1,0:T(8,128)S(1)}) fusion(f32[768]{0:T(1024)S(1)} %copy-done.33, bf16[512,3072]{1,0:T(8,128)(2,1)S(1)} %get-tuple-element.119, bf16[3072,768]{1,0:T(8,128)(2,1)} %bitcast.49, f32[768]{0:T(1024)S(1)} %reshape.372, f32[768]{0:T(1024)S(1)} %reshape.371, f32[512]{0:T(512)S(1)} %add_rsqrt_fusion.1, ...), kind=kOutput, calls=%fused_computation.260 | convolution fusion | flops 2418671104 | bytes 11025408 | tf_op jit(solution)/shard_map/dot_general | solution.py:22
  157.2 8.3 %convert_reduce_fusion = (f32[3072]{0:T(1024)S(1)}, bf16[512,3072]{1,0:T(8,128)(2,1)S(1)}) fusion(f32[512,3072]{1,0:T(8,128)} %get-tuple-element.120, f32[512,3072]{1,0:T(8,128)} %get-tuple-element.154, f32[3072]{0:T(1024)S(1)} %copy-done.28, bf16[512,768]{1,0:T(8,128)(2,1)S(1)} %get-tuple-element.111, bf16[3072,768]{1,0:T(8,128)(2,1)} %bitcast.49), kind=kOutput, calls=%fused_computation.2 | convolution fusion | flops 2442654720 | bytes 21258240 | tf_op jit(solution)/shard_map/dot_general | solution.py:22
  165.5 3.4 multiply_reduce_fusion.1
  173.2 11.6 %attend_back.1 = (bf16[512,2304]{1,0:T(8,128)(2,1)}, bf16[12,512,512]{2,1,0:T(8,128)(2,1)}) custom-call(bf16[512,2304]{1,0:T(8,128)(2,1)} %fusion.8.q_ref.k_ref.v_ref, bf16[512,2304]{1,0:T(8,128)(2,1)} %fusion.8.q_ref.k_ref.v_ref, bf16[512,2304]{1,0:T(8,128)(2,1)} %fusion.8.q_ref.k_ref.v_ref, bf16[12,512,512]{2,1,0:T(8,128)(2,1)} %get-tuple-element.27.p_ref, ...), custom_call_target="tpu_custom_call" | custom-call | tf_op jit(solution)/shard_map/attend_back/pallas_call | solution.py:234
  187.1 4.4 add_convert_fusion.1
  194.0 16.6 %table_grad.1 = f32[768,96]{1,0:T(8,128)} custom-call(bf16[3,64,16,512]{3,2,1,0:T(8,128)(2,1)} %broadcast_bitcast_fusion.ids_ref, bf16[12,512,512]{2,1,0:T(8,128)(2,1)} %get-tuple-element.29.grad_ref), custom_call_target="tpu_custom_call" | custom-call | tf_op jit(solution)/shard_map/table_grad/pallas_call | solution.py:183
  211.9 4.1 reshape.353
  216.1 2.8 reduce_sum.161
  223.8 5.1 %convolution_convert_fusion = bf16[3072,384]{1,0:T(8,128)(2,1)} fusion(bf16[512,3072]{1,0:T(8,128)(2,1)} %copy-done, bf16[512,768]{1,0:T(8,128)(2,1)S(1)} %get-tuple-element.111, s32[]{:T(128)S(6)} %select_n.427), kind=kOutput, calls=%fused_computation.27 | convolution fusion | flops 1209139200 | bytes 5898244 | tf_op jit(solution)/shard_map/dot_general | solution.py:22
  234.1 3.1 convolution_convert_fusion.1
  238.6 3.3 collective-permute-start.29
  247.6 2.8 collective-permute-start.35
  252.5 3.6 collective-permute-start.47
  270.1 3.9 collective-permute-done.39
  274.1 5.0 %collective-permute-start.40 = (bf16[2,4,48,384]{3,2,1,0:T(8,128)(2,1)S(1)}, bf16[2,4,48,384]{3,2,1,0:T(8,128)(2,1)S(1)}, u32[]{:S(2)}, u32[]{:S(2)}) collective-permute-start(bf16[2,4,48,384]{3,2,1,0:T(8,128)(2,1)S(1)} %bitcast_dynamic-update-slice_fusion.40), channel_id=1, source_target_pairs={{0,2},{2,0},{4,6},{6,4},{8,10},{10,8},{12,14},{14,12},{16,18},{18,... | collective-permute-start | bytes 884744 | tf_op jit(solution)/shard_map/ppermute | solution.py:271
  279.0 3.4 convert_add_fusion.2
  289.6 15.6 %collective-permute-done.14 = bf16[2,4,48,1152]{3,2,1,0:T(8,128)(2,1)} collective-permute-done((bf16[2,4,48,1152]{3,2,1,0:T(8,128)(2,1)}, bf16[2,4,48,1152]{3,2,1,0:T(8,128)(2,1)}, u32[]{:S(2)}, u32[]{:S(2)}) %collective-permute-start.14) | collective-permute-done | bytes 884768 | tf_op jit(solution)/shard_map/ppermute | solution.py:271
  307.2 3.4 convert_add_fusion.1
  311.3 6.8 %collective-permute-done.15 = bf16[4,48,1152]{2,1,0:T(8,128)(2,1)S(1)} collective-permute-done((bf16[4,48,1152]{2,1,0:T(8,128)(2,1)S(1)}, bf16[4,48,1152]{2,1,0:T(8,128)(2,1)S(1)}, u32[]{:S(2)}, u32[]{:S(2)}) %collective-permute-start.15) | collective-permute-done | bytes 442400 | tf_op jit(solution)/shard_map/ppermute | solution.py:271
  320.2 3.6 convert_add_fusion
  323.8 6.0 %collective-permute-done.17 = bf16[48,1152]{1,0:T(8,128)(2,1)S(1)} collective-permute-done((bf16[48,1152]{1,0:T(8,128)(2,1)S(1)}, bf16[48,1152]{1,0:T(8,128)(2,1)S(1)}, u32[]{:S(2)}, u32[]{:S(2)}) %collective-permute-start.17) | collective-permute-done | bytes 110624 | tf_op jit(solution)/shard_map/ppermute | solution.py:271
  335.5 5.3 %collective-permute-done.20 = bf16[48,1152]{1,0:T(8,128)(2,1)S(1)} collective-permute-done((bf16[48,1152]{1,0:T(8,128)(2,1)S(1)}, bf16[48,1152]{1,0:T(8,128)(2,1)S(1)}, u32[]{:S(2)}, u32[]{:S(2)}) %collective-permute-start.20) | collective-permute-done | bytes 110624 | tf_op jit(solution)/shard_map/ppermute | solution.py:271
  343.0 19.5 %collective-permute-done.59 = bf16[2,4,192,384]{3,2,1,0:T(8,128)(2,1)S(1)} collective-permute-done((bf16[2,4,192,384]{3,2,1,0:T(8,128)(2,1)S(1)}, bf16[2,4,192,384]{3,2,1,0:T(8,128)(2,1)S(1)}, u32[]{:S(2)}, u32[]{:S(2)}) %collective-permute-start.59) | collective-permute-done | bytes 1179680 | tf_op jit(solution)/shard_map/ppermute | solution.py:271
  369.1 6.8 %collective-permute-done.60 = bf16[4,192,384]{2,1,0:T(8,128)(2,1)S(1)} collective-permute-done((bf16[4,192,384]{2,1,0:T(8,128)(2,1)S(1)}, bf16[4,192,384]{2,1,0:T(8,128)(2,1)S(1)}, u32[]{:S(2)}, u32[]{:S(2)}) %collective-permute-start.60) | collective-permute-done | bytes 589856 | tf_op jit(solution)/shard_map/ppermute | solution.py:271
  376.2 3.9 collective-permute-start.63
  385.2 9.0 %collective-permute-start.54 = (bf16[48,1536]{1,0:T(8,128)(2,1)S(1)}, bf16[48,1536]{1,0:T(8,128)(2,1)S(1)}, u32[]{:S(2)}, u32[]{:S(2)}) collective-permute-start(bf16[48,1536]{1,0:T(8,128)(2,1)S(1)} %get-tuple-element.109), channel_id=1, source_target_pairs={{0,16},{2,18},{4,20},{6,22},{8,24},{10,26},{12,28},{14,30},{16,0},... | collective-permute-start | bytes 442376 | tf_op jit(solution)/shard_map/ppermute | solution.py:271
  394.1 4.0 collective-permute-done.62
  404.8 6.5 %collective-permute-start.66 = (bf16[192,384]{1,0:T(8,128)(2,1)S(1)}, bf16[192,384]{1,0:T(8,128)(2,1)S(1)}, u32[]{:S(2)}, u32[]{:S(2)}) collective-permute-start(bf16[192,384]{1,0:T(8,128)(2,1)S(1)} %get-tuple-element.107), channel_id=1, source_target_pairs={{0,24},{2,26},{4,28},{6,30},{8,0},{10,2},{12,4},{14,6},{16,8},{18,... | collective-permute-start | bytes 442376 | tf_op jit(solution)/shard_map/ppermute | solution.py:271
  412.1 5.1 %collective-permute-done.65 = bf16[192,384]{1,0:T(8,128)(2,1)S(1)} collective-permute-done((bf16[192,384]{1,0:T(8,128)(2,1)S(1)}, bf16[192,384]{1,0:T(8,128)(2,1)S(1)}, u32[]{:S(2)}, u32[]{:S(2)}) %collective-permute-start.65) | collective-permute-done | bytes 147488 | tf_op jit(solution)/shard_map/ppermute | solution.py:271
  423.8 8.9 %collective-permute-start.57 = (bf16[2,4,48,1536]{3,2,1,0:T(8,128)(2,1)}, bf16[2,4,48,1536]{3,2,1,0:T(8,128)(2,1)}, u32[]{:S(2)}, u32[]{:S(2)}) collective-permute-start(bf16[2,4,48,1536]{3,2,1,0:T(8,128)(2,1)} %bitcast_dynamic-update-slice_fusion.17), channel_id=1, source_target_pairs={{0,2},{2,0},{4,6},{6,4},{8,10},{10,8},{12,14},{14,12},{16,18},{18,... | collective-permute-start | bytes 3538952 | tf_op jit(solution)/shard_map/ppermute | solution.py:271
  434.9 3.3 copy.95
  438.2 2.9 copy.101
  447.6 3.0 convert_bitcast_fusion.1
  450.6 6.1 %copy.99 = f32[384,2,1536]{0,2,1:T(8,128)} copy(f32[384,2,1536]{2,0,1:T(8,128)} %convert_bitcast_fusion.1) | data formatting | bytes 9437184 | tf_op jit(solution)/shard_map/reshape | solution.py:343
  456.7 6.0 %copy.104 = f32[384,3072]{1,0:T(8,128)} copy(f32[384,3072]{0,1:T(8,128)} %bitcast.302) | data formatting | bytes 9437184
  464.3 2.7 convert_bitcast_fusion
  467.0 6.1 %copy.100 = f32[1536,2,384]{0,2,1:T(8,128)} copy(f32[1536,2,384]{2,0,1:T(8,128)} %convert_bitcast_fusion) | data formatting | bytes 9437184 | tf_op jit(solution)/shard_map/reshape | solution.py:343
  473.1 6.0 %copy.105 = f32[1536,768]{1,0:T(8,128)} copy(f32[1536,768]{0,1:T(8,128)} %bitcast.303) | data formatting | bytes 9437184
  (403 shorter events, 160.6 us)
Async XLA Ops:
  7.9 27.4 %collective-permute-start.3 = (bf16[5184]{0:T(1024)(128)(2,1)S(1)}, bf16[5184]{0:T(1024)(128)(2,1)}, u32[]{:S(2)}, u32[]{:S(2)}) collective-permute-start(bf16[5184]{0:T(1024)(128)(2,1)S(1)} %concatenate.12), channel_id=1, source_target_pairs={{0,1},{1,0},{2,3},{3,2},{4,5},{5,4},{6,7},{7,6},{8,9},{9,8},{10,11... | collective-permute-start | bytes 31112 | tf_op jit(solution)/shard_map/ppermute | solution.py:271
  11.8 46.2 %collective-permute-start = (bf16[96,2304]{1,0:T(8,128)(2,1)}, bf16[96,2304]{1,0:T(8,128)(2,1)}, u32[]{:S(2)}, u32[]{:S(2)}) collective-permute-start(bf16[96,2304]{1,0:T(8,128)(2,1)} %dynamic-slice_bitcast_fusion.2), channel_id=1, source_target_pairs={{0,1},{1,0},{2,3},{3,2},{4,5},{5,4},{6,7},{7,6},{8,9},{9,8},{10,11... | collective-permute-start | bytes 1327112 | tf_op jit(solution)/shard_map/ppermute | solution.py:271
  58.0 16.2 %collective-permute-start.1 = (bf16[1,96,2304]{2,1,0:T(8,128)(2,1)}, bf16[1,96,2304]{2,1,0:T(8,128)(2,1)S(1)}, u32[]{:S(2)}, u32[]{:S(2)}) collective-permute-start(bf16[1,96,2304]{2,1,0:T(8,128)(2,1)} %bitcast.4), channel_id=1, source_target_pairs={{0,4},{2,6},{4,0},{6,2},{8,12},{10,14},{12,8},{14,10},{16,20},{18,... | collective-permute-start | bytes 1327112 | tf_op jit(solution)/shard_map/ppermute | solution.py:271
  63.8 12.4 %collective-permute-start.7 = (bf16[96,3072]{1,0:T(8,128)(2,1)S(1)}, bf16[96,3072]{1,0:T(8,128)(2,1)S(1)}, u32[]{:S(2)}, u32[]{:S(2)}) collective-permute-start(bf16[96,3072]{1,0:T(8,128)(2,1)S(1)} %copy-done.21), channel_id=1, source_target_pairs={{0,1},{1,0},{2,3},{3,2},{4,5},{5,4},{6,7},{7,6},{8,9},{9,8},{10,11... | collective-permute-start | bytes 1769480 | tf_op jit(solution)/shard_map/ppermute | solution.py:271
  74.2 17.8 %collective-permute-start.2 = (bf16[2,1,96,2304]{3,2,0,1:T(8,128)(2,1)S(1)}, bf16[2,1,96,2304]{3,2,0,1:T(8,128)(2,1)S(1)}, u32[]{:S(2)}, u32[]{:S(2)}) collective-permute-start(bf16[2,1,96,2304]{3,2,0,1:T(8,128)(2,1)S(1)} %bitcast_dynamic-update-slice_fusion.26), channel_id=1, source_target_pairs={{0,2},{2,0},{4,6},{6,4},{8,10},{10,8},{12,14},{14,12},{16,18},{18,... | collective-permute-start | bytes 2654216 | tf_op jit(solution)/shard_map/ppermute | solution.py:271
  76.2 11.4 %collective-permute-start.8 = (bf16[1,96,3072]{2,1,0:T(8,128)(2,1)S(1)}, bf16[1,96,3072]{2,1,0:T(8,128)(2,1)S(1)}, u32[]{:S(2)}, u32[]{:S(2)}) collective-permute-start(bf16[1,96,3072]{2,1,0:T(8,128)(2,1)S(1)} %bitcast.328), channel_id=1, source_target_pairs={{0,4},{2,6},{4,0},{6,2},{8,12},{10,14},{12,8},{14,10},{16,20},{18,... | collective-permute-start | bytes 1769480 | tf_op jit(solution)/shard_map/ppermute | solution.py:271
  77.4 33.6 %collective-permute-start.10 = (bf16[384,768]{1,0:T(8,128)(2,1)S(1)}, bf16[384,768]{1,0:T(8,128)(2,1)S(1)}, u32[]{:S(2)}, u32[]{:S(2)}) collective-permute-start(bf16[384,768]{1,0:T(8,128)(2,1)S(1)} %copy-done.20), channel_id=1, source_target_pairs={{0,1},{1,0},{2,3},{3,2},{4,5},{5,4},{6,7},{7,6},{8,9},{9,8},{10,11... | collective-permute-start | bytes 1769480 | tf_op jit(solution)/shard_map/ppermute | solution.py:271
  87.7 39.6 %collective-permute-start.9 = (bf16[2,1,96,3072]{3,2,0,1:T(8,128)(2,1)S(1)}, bf16[2,1,96,3072]{3,2,0,1:T(8,128)(2,1)S(1)}, u32[]{:S(2)}, u32[]{:S(2)}) collective-permute-start(bf16[2,1,96,3072]{3,2,0,1:T(8,128)(2,1)S(1)} %bitcast_dynamic-update-slice_fusion.21), channel_id=1, source_target_pairs={{0,2},{2,0},{4,6},{6,4},{8,10},{10,8},{12,14},{14,12},{16,18},{18,... | collective-permute-start | bytes 3538952 | tf_op jit(solution)/shard_map/ppermute | solution.py:271
  111.1 15.0 %collective-permute-start.11 = (bf16[1,384,768]{2,1,0:T(8,128)(2,1)S(1)}, bf16[1,384,768]{2,1,0:T(8,128)(2,1)S(1)}, u32[]{:S(2)}, u32[]{:S(2)}) collective-permute-start(bf16[1,384,768]{2,1,0:T(8,128)(2,1)S(1)} %bitcast.329), channel_id=1, source_target_pairs={{0,4},{2,6},{4,0},{6,2},{8,12},{10,14},{12,8},{14,10},{16,20},{18,... | collective-permute-start | bytes 1769480 | tf_op jit(solution)/shard_map/ppermute | solution.py:271
  126.1 20.6 %collective-permute-start.12 = (bf16[2,1,384,768]{3,2,0,1:T(8,128)(2,1)S(1)}, bf16[2,1,384,768]{3,2,0,1:T(8,128)(2,1)S(1)}, u32[]{:S(2)}, u32[]{:S(2)}) collective-permute-start(bf16[2,1,384,768]{3,2,0,1:T(8,128)(2,1)S(1)} %bitcast_dynamic-update-slice_fusion.19), channel_id=1, source_target_pairs={{0,2},{2,0},{4,6},{6,4},{8,10},{10,8},{12,14},{14,12},{16,18},{18,... | collective-permute-start | bytes 3538952 | tf_op jit(solution)/shard_map/ppermute | solution.py:271
  193.9 85.1 %collective-permute-start.13 = (bf16[768,1152]{1,0:T(8,128)(2,1)}, bf16[768,1152]{1,0:T(8,128)(2,1)}, u32[]{:S(2)}, u32[]{:S(2)}) collective-permute-start(bf16[768,1152]{1,0:T(8,128)(2,1)} %fusion.9), channel_id=1, source_target_pairs={{0,2},{2,0},{4,6},{6,4},{8,10},{10,8},{12,14},{14,12},{16,18},{18,... | collective-permute-start | bytes 5308424 | tf_op jit(solution)/shard_map/ppermute | solution.py:271
  219.3 9.7 %collective-permute-start.24 = (f32[1344]{0:T(1024)S(1)}, f32[1344]{0:T(1024)S(1)}, u32[]{:S(2)}, u32[]{:S(2)}) collective-permute-start(f32[1344]{0:T(1024)S(1)} %get-tuple-element.104), channel_id=1, source_target_pairs={{0,1},{1,0},{2,3},{3,2},{4,5},{5,4},{6,7},{7,6},{8,9},{9,8},{10,11... | collective-permute-start | bytes 16136 | tf_op jit(solution)/shard_map/ppermute | solution.py:271
  223.0 8.7 %collective-permute-start.30 = (bf16[768,384]{1,0:T(8,128)(2,1)}, bf16[768,384]{1,0:T(8,128)(2,1)}, u32[]{:S(2)}, u32[]{:S(2)}) collective-permute-start(bf16[768,384]{1,0:T(8,128)(2,1)} %convolution_convert_fusion.4), channel_id=1, source_target_pairs={{0,2},{2,0},{4,6},{6,4},{8,10},{10,8},{12,14},{14,12},{16,18},{18,... | collective-permute-start | bytes 1769480 | tf_op jit(solution)/shard_map/ppermute | solution.py:271
  233.5 8.4 %collective-permute-start.31 = (bf16[2,4,48,384]{3,2,1,0:T(8,128)(2,1)S(1)}, bf16[2,4,48,384]{3,2,1,0:T(8,128)(2,1)S(1)}, u32[]{:S(2)}, u32[]{:S(2)}) collective-permute-start(bf16[2,4,48,384]{3,2,1,0:T(8,128)(2,1)S(1)} %fusion.39), channel_id=1, source_target_pairs={{0,1},{1,0},{2,3},{3,2},{4,5},{5,4},{6,7},{7,6},{8,9},{9,8},{10,11... | collective-permute-start | bytes 884744 | tf_op jit(solution)/shard_map/ppermute | solution.py:271
  237.2 9.0 %collective-permute-start.42 = (f32[3840]{0:T(1024)S(1)}, f32[3840]{0:T(1024)S(1)}, u32[]{:S(2)}, u32[]{:S(2)}) collective-permute-start(f32[3840]{0:T(1024)S(1)} %add.688), channel_id=1, source_target_pairs={{0,2},{2,0},{4,6},{6,4},{8,10},{10,8},{12,14},{14,12},{16,18},{18,... | collective-permute-start | bytes 46088 | tf_op jit(solution)/shard_map/ppermute | solution.py:271
  247.6 8.5 %collective-permute-start.35 = (bf16[48,384]{1,0:T(8,128)(2,1)S(1)}, bf16[48,384]{1,0:T(8,128)(2,1)S(1)}, u32[]{:S(2)}, u32[]{:S(2)}) collective-permute-start(bf16[48,384]{1,0:T(8,128)(2,1)S(1)} %get-tuple-element.132), channel_id=1, source_target_pairs={{0,24},{2,26},{4,28},{6,30},{8,0},{10,2},{12,4},{14,6},{16,8},{18,... | collective-permute-start | bytes 110600 | tf_op jit(solution)/shard_map/ppermute | solution.py:271
  250.4 8.6 %collective-permute-start.33 = (bf16[48,384]{1,0:T(8,128)(2,1)S(1)}, bf16[48,384]{1,0:T(8,128)(2,1)S(1)}, u32[]{:S(2)}, u32[]{:S(2)}) collective-permute-start(bf16[48,384]{1,0:T(8,128)(2,1)S(1)} %get-tuple-element.131), channel_id=1, source_target_pairs={{0,8},{2,10},{4,12},{6,14},{8,16},{10,18},{12,20},{14,22},{16,24},... | collective-permute-start | bytes 110600 | tf_op jit(solution)/shard_map/ppermute | solution.py:271
  252.5 54.7 %collective-permute-start.47 = (bf16[768,1536]{1,0:T(8,128)(2,1)}, bf16[768,1536]{1,0:T(8,128)(2,1)}, u32[]{:S(2)}, u32[]{:S(2)}) collective-permute-start(bf16[768,1536]{1,0:T(8,128)(2,1)} %convolution_convert_fusion.1), channel_id=1, source_target_pairs={{0,2},{2,0},{4,6},{6,4},{8,10},{10,8},{12,14},{14,12},{16,18},{18,... | collective-permute-start | bytes 7077896 | tf_op jit(solution)/shard_map/ppermute | solution.py:271
  259.0 61.1 %collective-permute-start.58 = (bf16[3072,384]{1,0:T(8,128)(2,1)}, bf16[3072,384]{1,0:T(8,128)(2,1)}, u32[]{:S(2)}, u32[]{:S(2)}) collective-permute-start(bf16[3072,384]{1,0:T(8,128)(2,1)} %convolution_convert_fusion), channel_id=1, source_target_pairs={{0,2},{2,0},{4,6},{6,4},{8,10},{10,8},{12,14},{14,12},{16,18},{18,... | collective-permute-start | bytes 7077896 | tf_op jit(solution)/shard_map/ppermute | solution.py:271
  274.1 11.3 %collective-permute-start.40 = (bf16[2,4,48,384]{3,2,1,0:T(8,128)(2,1)S(1)}, bf16[2,4,48,384]{3,2,1,0:T(8,128)(2,1)S(1)}, u32[]{:S(2)}, u32[]{:S(2)}) collective-permute-start(bf16[2,4,48,384]{3,2,1,0:T(8,128)(2,1)S(1)} %bitcast_dynamic-update-slice_fusion.40), channel_id=1, source_target_pairs={{0,2},{2,0},{4,6},{6,4},{8,10},{10,8},{12,14},{14,12},{16,18},{18,... | collective-permute-start | bytes 884744 | tf_op jit(solution)/shard_map/ppermute | solution.py:271
  283.6 21.6 %collective-permute-start.14 = (bf16[2,4,48,1152]{3,2,1,0:T(8,128)(2,1)}, bf16[2,4,48,1152]{3,2,1,0:T(8,128)(2,1)}, u32[]{:S(2)}, u32[]{:S(2)}) collective-permute-start(bf16[2,4,48,1152]{3,2,1,0:T(8,128)(2,1)} %fusion.25), channel_id=1, source_target_pairs={{0,1},{1,0},{2,3},{3,2},{4,5},{5,4},{6,7},{7,6},{8,9},{9,8},{10,11... | collective-permute-start | bytes 2654216 | tf_op jit(solution)/shard_map/ppermute | solution.py:271
  307.1 11.0 %collective-permute-start.15 = (bf16[4,48,1152]{2,1,0:T(8,128)(2,1)S(1)}, bf16[4,48,1152]{2,1,0:T(8,128)(2,1)S(1)}, u32[]{:S(2)}, u32[]{:S(2)}) collective-permute-start(bf16[4,48,1152]{2,1,0:T(8,128)(2,1)S(1)} %fusion.28), channel_id=1, source_target_pairs={{0,4},{2,6},{4,0},{6,2},{8,12},{10,14},{12,8},{14,10},{16,20},{18,... | collective-permute-start | bytes 1327112 | tf_op jit(solution)/shard_map/ppermute | solution.py:271
  310.8 30.2 %collective-permute-start.48 = (bf16[2,4,48,1536]{3,2,1,0:T(8,128)(2,1)S(1)}, bf16[2,4,48,1536]{3,2,1,0:T(8,128)(2,1)S(1)}, u32[]{:S(2)}, u32[]{:S(2)}) collective-permute-start(bf16[2,4,48,1536]{3,2,1,0:T(8,128)(2,1)S(1)} %fusion.19), channel_id=1, source_target_pairs={{0,1},{1,0},{2,3},{3,2},{4,5},{5,4},{6,7},{7,6},{8,9},{9,8},{10,11... | collective-permute-start | bytes 3538952 | tf_op jit(solution)/shard_map/ppermute | solution.py:271
  319.8 10.0 %collective-permute-start.17 = (bf16[48,1152]{1,0:T(8,128)(2,1)S(1)}, bf16[48,1152]{1,0:T(8,128)(2,1)S(1)}, u32[]{:S(2)}, u32[]{:S(2)}) collective-permute-start(bf16[48,1152]{1,0:T(8,128)(2,1)S(1)} %get-tuple-element.130), channel_id=1, source_target_pairs={{0,16},{2,18},{4,20},{6,22},{8,24},{10,26},{12,28},{14,30},{16,0},... | collective-permute-start | bytes 331784 | tf_op jit(solution)/shard_map/ppermute | solution.py:271
  319.8 10.0 %collective-permute-start.16 = (bf16[48,1152]{1,0:T(8,128)(2,1)S(1)}, bf16[48,1152]{1,0:T(8,128)(2,1)S(1)}, u32[]{:S(2)}, u32[]{:S(2)}) collective-permute-start(bf16[48,1152]{1,0:T(8,128)(2,1)S(1)} %get-tuple-element.128), channel_id=1, source_target_pairs={{0,8},{2,10},{4,12},{6,14},{8,16},{10,18},{12,20},{14,22},{16,24},... | collective-permute-start | bytes 331784 | tf_op jit(solution)/shard_map/ppermute | solution.py:271
  330.1 32.5 %collective-permute-start.59 = (bf16[2,4,192,384]{3,2,1,0:T(8,128)(2,1)S(1)}, bf16[2,4,192,384]{3,2,1,0:T(8,128)(2,1)S(1)}, u32[]{:S(2)}, u32[]{:S(2)}) collective-permute-start(bf16[2,4,192,384]{3,2,1,0:T(8,128)(2,1)S(1)} %fusion.20), channel_id=1, source_target_pairs={{0,1},{1,0},{2,3},{3,2},{4,5},{5,4},{6,7},{7,6},{8,9},{9,8},{10,11... | collective-permute-start | bytes 3538952 | tf_op jit(solution)/shard_map/ppermute | solution.py:271
  330.5 10.3 %collective-permute-start.20 = (bf16[48,1152]{1,0:T(8,128)(2,1)S(1)}, bf16[48,1152]{1,0:T(8,128)(2,1)S(1)}, u32[]{:S(2)}, u32[]{:S(2)}) collective-permute-start(bf16[48,1152]{1,0:T(8,128)(2,1)S(1)} %get-tuple-element.118), channel_id=1, source_target_pairs={{0,16},{2,18},{4,20},{6,22},{8,24},{10,26},{12,28},{14,30},{16,0},... | collective-permute-start | bytes 331784 | tf_op jit(solution)/shard_map/ppermute | solution.py:271
  331.9 8.9 %collective-permute-start.21 = (bf16[48,1152]{1,0:T(8,128)(2,1)S(1)}, bf16[48,1152]{1,0:T(8,128)(2,1)S(1)}, u32[]{:S(2)}, u32[]{:S(2)}) collective-permute-start(bf16[48,1152]{1,0:T(8,128)(2,1)S(1)} %get-tuple-element.118), channel_id=1, source_target_pairs={{0,24},{2,26},{4,28},{6,30},{8,0},{10,2},{12,4},{14,6},{16,8},{18,... | collective-permute-start | bytes 331784 | tf_op jit(solution)/shard_map/ppermute | solution.py:271
  340.8 23.5 %collective-permute-start.22 = (bf16[4,48,1152]{2,1,0:T(8,128)(2,1)S(1)}, bf16[4,48,1152]{2,1,0:T(8,128)(2,1)S(1)}, u32[]{:S(2)}, u32[]{:S(2)}) collective-permute-start(bf16[4,48,1152]{2,1,0:T(8,128)(2,1)S(1)} %bitcast_dynamic-update-slice_fusion.44), channel_id=1, source_target_pairs={{0,4},{2,6},{4,0},{6,2},{8,12},{10,14},{12,8},{14,10},{16,20},{18,... | collective-permute-start | bytes 1327112 | tf_op jit(solution)/shard_map/ppermute | solution.py:271
  341.5 25.5 %collective-permute-start.49 = (bf16[4,48,1536]{2,1,0:T(8,128)(2,1)S(1)}, bf16[4,48,1536]{2,1,0:T(8,128)(2,1)S(1)}, u32[]{:S(2)}, u32[]{:S(2)}) collective-permute-start(bf16[4,48,1536]{2,1,0:T(8,128)(2,1)S(1)} %fusion.26), channel_id=1, source_target_pairs={{0,4},{2,6},{4,0},{6,2},{8,12},{10,14},{12,8},{14,10},{16,20},{18,... | collective-permute-start | bytes 1769480 | tf_op jit(solution)/shard_map/ppermute | solution.py:271
  362.9 13.1 %collective-permute-start.60 = (bf16[4,192,384]{2,1,0:T(8,128)(2,1)S(1)}, bf16[4,192,384]{2,1,0:T(8,128)(2,1)S(1)}, u32[]{:S(2)}, u32[]{:S(2)}) collective-permute-start(bf16[4,192,384]{2,1,0:T(8,128)(2,1)S(1)} %fusion.27), channel_id=1, source_target_pairs={{0,4},{2,6},{4,0},{6,2},{8,12},{10,14},{12,8},{14,10},{16,20},{18,... | collective-permute-start | bytes 1769480 | tf_op jit(solution)/shard_map/ppermute | solution.py:271
  364.4 58.4 %collective-permute-start.23 = (bf16[2,4,48,1152]{3,2,1,0:T(8,128)(2,1)S(1)}, bf16[2,4,48,1152]{3,2,1,0:T(8,128)(2,1)S(1)}, u32[]{:S(2)}, u32[]{:S(2)}) collective-permute-start(bf16[2,4,48,1152]{3,2,1,0:T(8,128)(2,1)S(1)} %bitcast_dynamic-update-slice_fusion.24), channel_id=1, source_target_pairs={{0,2},{2,0},{4,6},{6,4},{8,10},{10,8},{12,14},{14,12},{16,18},{18,... | collective-permute-start | bytes 2654216 | tf_op jit(solution)/shard_map/ppermute | solution.py:271
  367.2 12.9 %collective-permute-start.52 = (bf16[48,1536]{1,0:T(8,128)(2,1)S(1)}, bf16[48,1536]{1,0:T(8,128)(2,1)S(1)}, u32[]{:S(2)}, u32[]{:S(2)}) collective-permute-start(bf16[48,1536]{1,0:T(8,128)(2,1)S(1)} %get-tuple-element.126), channel_id=1, source_target_pairs={{0,24},{2,26},{4,28},{6,30},{8,0},{10,2},{12,4},{14,6},{16,8},{18,... | collective-permute-start | bytes 442376 | tf_op jit(solution)/shard_map/ppermute | solution.py:271
  368.8 12.3 %collective-permute-start.51 = (bf16[48,1536]{1,0:T(8,128)(2,1)S(1)}, bf16[48,1536]{1,0:T(8,128)(2,1)S(1)}, u32[]{:S(2)}, u32[]{:S(2)}) collective-permute-start(bf16[48,1536]{1,0:T(8,128)(2,1)S(1)} %get-tuple-element.127), channel_id=1, source_target_pairs={{0,16},{2,18},{4,20},{6,22},{8,24},{10,26},{12,28},{14,30},{16,0},... | collective-permute-start | bytes 442376 | tf_op jit(solution)/shard_map/ppermute | solution.py:271
  368.8 12.3 %collective-permute-start.50 = (bf16[48,1536]{1,0:T(8,128)(2,1)S(1)}, bf16[48,1536]{1,0:T(8,128)(2,1)S(1)}, u32[]{:S(2)}, u32[]{:S(2)}) collective-permute-start(bf16[48,1536]{1,0:T(8,128)(2,1)S(1)} %get-tuple-element.125), channel_id=1, source_target_pairs={{0,8},{2,10},{4,12},{6,14},{8,16},{10,18},{12,20},{14,22},{16,24},... | collective-permute-start | bytes 442376 | tf_op jit(solution)/shard_map/ppermute | solution.py:271
  376.2 9.0 %collective-permute-start.63 = (bf16[192,384]{1,0:T(8,128)(2,1)S(1)}, bf16[192,384]{1,0:T(8,128)(2,1)S(1)}, u32[]{:S(2)}, u32[]{:S(2)}) collective-permute-start(bf16[192,384]{1,0:T(8,128)(2,1)S(1)} %get-tuple-element.123), channel_id=1, source_target_pairs={{0,24},{2,26},{4,28},{6,30},{8,0},{10,2},{12,4},{14,6},{16,8},{18,... | collective-permute-start | bytes 442376 | tf_op jit(solution)/shard_map/ppermute | solution.py:271
  380.1 18.1 %collective-permute-start.62 = (bf16[192,384]{1,0:T(8,128)(2,1)S(1)}, bf16[192,384]{1,0:T(8,128)(2,1)S(1)}, u32[]{:S(2)}, u32[]{:S(2)}) collective-permute-start(bf16[192,384]{1,0:T(8,128)(2,1)S(1)} %get-tuple-element.124), channel_id=1, source_target_pairs={{0,16},{2,18},{4,20},{6,22},{8,24},{10,26},{12,28},{14,30},{16,0},... | collective-permute-start | bytes 442376 | tf_op jit(solution)/shard_map/ppermute | solution.py:271
  381.1 17.1 %collective-permute-start.61 = (bf16[192,384]{1,0:T(8,128)(2,1)S(1)}, bf16[192,384]{1,0:T(8,128)(2,1)S(1)}, u32[]{:S(2)}, u32[]{:S(2)}) collective-permute-start(bf16[192,384]{1,0:T(8,128)(2,1)S(1)} %get-tuple-element.122), channel_id=1, source_target_pairs={{0,8},{2,10},{4,12},{6,14},{8,16},{10,18},{12,20},{14,22},{16,24},... | collective-permute-start | bytes 442376 | tf_op jit(solution)/shard_map/ppermute | solution.py:271
  381.2 20.0 %collective-permute-start.53 = (bf16[48,1536]{1,0:T(8,128)(2,1)S(1)}, bf16[48,1536]{1,0:T(8,128)(2,1)S(1)}, u32[]{:S(2)}, u32[]{:S(2)}) collective-permute-start(bf16[48,1536]{1,0:T(8,128)(2,1)S(1)} %get-tuple-element.109), channel_id=1, source_target_pairs={{0,8},{2,10},{4,12},{6,14},{8,16},{10,18},{12,20},{14,22},{16,24},... | collective-permute-start | bytes 442376 | tf_op jit(solution)/shard_map/ppermute | solution.py:271
  385.2 19.6 %collective-permute-start.54 = (bf16[48,1536]{1,0:T(8,128)(2,1)S(1)}, bf16[48,1536]{1,0:T(8,128)(2,1)S(1)}, u32[]{:S(2)}, u32[]{:S(2)}) collective-permute-start(bf16[48,1536]{1,0:T(8,128)(2,1)S(1)} %get-tuple-element.109), channel_id=1, source_target_pairs={{0,16},{2,18},{4,20},{6,22},{8,24},{10,26},{12,28},{14,30},{16,0},... | collective-permute-start | bytes 442376 | tf_op jit(solution)/shard_map/ppermute | solution.py:271
  398.2 13.1 %collective-permute-start.55 = (bf16[48,1536]{1,0:T(8,128)(2,1)S(1)}, bf16[48,1536]{1,0:T(8,128)(2,1)S(1)}, u32[]{:S(2)}, u32[]{:S(2)}) collective-permute-start(bf16[48,1536]{1,0:T(8,128)(2,1)S(1)} %get-tuple-element.109), channel_id=1, source_target_pairs={{0,24},{2,26},{4,28},{6,30},{8,0},{10,2},{12,4},{14,6},{16,8},{18,... | collective-permute-start | bytes 442376 | tf_op jit(solution)/shard_map/ppermute | solution.py:271
  399.8 11.6 %collective-permute-start.64 = (bf16[192,384]{1,0:T(8,128)(2,1)S(1)}, bf16[192,384]{1,0:T(8,128)(2,1)S(1)}, u32[]{:S(2)}, u32[]{:S(2)}) collective-permute-start(bf16[192,384]{1,0:T(8,128)(2,1)S(1)} %get-tuple-element.107), channel_id=1, source_target_pairs={{0,8},{2,10},{4,12},{6,14},{8,16},{10,18},{12,20},{14,22},{16,24},... | collective-permute-start | bytes 442376 | tf_op jit(solution)/shard_map/ppermute | solution.py:271
  401.3 15.9 %collective-permute-start.65 = (bf16[192,384]{1,0:T(8,128)(2,1)S(1)}, bf16[192,384]{1,0:T(8,128)(2,1)S(1)}, u32[]{:S(2)}, u32[]{:S(2)}) collective-permute-start(bf16[192,384]{1,0:T(8,128)(2,1)S(1)} %get-tuple-element.107), channel_id=1, source_target_pairs={{0,16},{2,18},{4,20},{6,22},{8,24},{10,26},{12,28},{14,30},{16,0},... | collective-permute-start | bytes 442376 | tf_op jit(solution)/shard_map/ppermute | solution.py:271
  404.8 13.1 %collective-permute-start.66 = (bf16[192,384]{1,0:T(8,128)(2,1)S(1)}, bf16[192,384]{1,0:T(8,128)(2,1)S(1)}, u32[]{:S(2)}, u32[]{:S(2)}) collective-permute-start(bf16[192,384]{1,0:T(8,128)(2,1)S(1)} %get-tuple-element.107), channel_id=1, source_target_pairs={{0,24},{2,26},{4,28},{6,30},{8,0},{10,2},{12,4},{14,6},{16,8},{18,... | collective-permute-start | bytes 442376 | tf_op jit(solution)/shard_map/ppermute | solution.py:271
  411.3 11.6 %collective-permute-start.56 = (bf16[4,48,1536]{2,1,0:T(8,128)(2,1)S(1)}, bf16[4,48,1536]{2,1,0:T(8,128)(2,1)S(1)}, u32[]{:S(2)}, u32[]{:S(2)}) collective-permute-start(bf16[4,48,1536]{2,1,0:T(8,128)(2,1)S(1)} %bitcast_dynamic-update-slice_fusion.36), channel_id=1, source_target_pairs={{0,4},{2,6},{4,0},{6,2},{8,12},{10,14},{12,8},{14,10},{16,20},{18,... | collective-permute-start | bytes 1769480 | tf_op jit(solution)/shard_map/ppermute | solution.py:271
  418.5 22.6 %collective-permute-start.67 = (bf16[4,192,384]{2,1,0:T(8,128)(2,1)}, bf16[4,192,384]{2,1,0:T(8,128)(2,1)}, u32[]{:S(2)}, u32[]{:S(2)}) collective-permute-start(bf16[4,192,384]{2,1,0:T(8,128)(2,1)} %bitcast_dynamic-update-slice_fusion.32), channel_id=1, source_target_pairs={{0,4},{2,6},{4,0},{6,2},{8,12},{10,14},{12,8},{14,10},{16,20},{18,... | collective-permute-start | bytes 1769480 | tf_op jit(solution)/shard_map/ppermute | solution.py:271
  423.8 22.5 %collective-permute-start.57 = (bf16[2,4,48,1536]{3,2,1,0:T(8,128)(2,1)}, bf16[2,4,48,1536]{3,2,1,0:T(8,128)(2,1)}, u32[]{:S(2)}, u32[]{:S(2)}) collective-permute-start(bf16[2,4,48,1536]{3,2,1,0:T(8,128)(2,1)} %bitcast_dynamic-update-slice_fusion.17), channel_id=1, source_target_pairs={{0,2},{2,0},{4,6},{6,4},{8,10},{10,8},{12,14},{14,12},{16,18},{18,... | collective-permute-start | bytes 3538952 | tf_op jit(solution)/shard_map/ppermute | solution.py:271
  443.1 19.7 %collective-permute-start.68 = (bf16[2,4,192,384]{3,2,1,0:T(8,128)(2,1)}, bf16[2,4,192,384]{3,2,1,0:T(8,128)(2,1)}, u32[]{:S(2)}, u32[]{:S(2)}) collective-permute-start(bf16[2,4,192,384]{3,2,1,0:T(8,128)(2,1)} %bitcast_dynamic-update-slice_fusion.15), channel_id=1, source_target_pairs={{0,2},{2,0},{4,6},{6,4},{8,10},{10,8},{12,14},{14,12},{16,18},{18,... | collective-permute-start | bytes 3538952 | tf_op jit(solution)/shard_map/ppermute | solution.py:271
  (66 other events, 772.9 us)

commit v2 on v1

v2 whole, which is shorter than its diff:
```python
import functools

import jax
import jax.numpy as jnp
from jax import lax
from jax.experimental import pallas as pl
from jax.experimental.pallas import tpu as pltpu
from jax.sharding import PartitionSpec as P

EPSILON = 1e-05
MASKED = -1000000000.0
BF = jnp.bfloat16
F32 = jnp.float32
NN = (((1,), (0,)), ((), ()))
NT = (((1,), (1,)), ((), ()))
TN = (((0,), (0,)), ((), ()))
VMEM_LIMIT = 56 * 2**20
WIDE = 128
ANY = pl.BlockSpec(memory_space=pl.ANY)
SMEM = pl.BlockSpec(memory_space=pltpu.SMEM)
VMEM = pl.BlockSpec(memory_space=pltpu.VMEM)


def dg(left, right, dims):
    return lax.dot_general(left, right, dims, preferred_element_type=F32)


def params():
    return pltpu.CompilerParams(vmem_limit_bytes=VMEM_LIMIT)


def shaped(shape, dtype):
    return jax.ShapeDtypeStruct(shape, dtype)


def onehot_rows(ids, oh_ref, bucket_count):
    length = ids[0].shape[1]
    sub = lax.broadcasted_iota(jnp.int32, (16, length), 0)
    one = jnp.ones((16, length), BF)
    zero = jnp.zeros((16, length), BF)
    half = bucket_count // 2
    for kind in range(3):
        both = jnp.concatenate([ids[kind], ids[kind]], axis=0).astype(BF)
        for pair in range(half):
            level = jnp.where(sub < 8, 2 * pair, 2 * pair + 1).astype(F32).astype(BF)
            oh_ref[pl.ds((kind * half + pair) * 16, 16), :] = jnp.where(both == level, one, zero)


def iota2(shape, dim):
    return lax.broadcasted_iota(jnp.int32, shape, dim)


def bias_kernel(len_ref, ids_ref, table_ref, out_ref, turned_ref, spread_ref, held_ref, oh_ref):
    block = pl.program_id(0)
    heads, rows, length = out_ref.shape
    entries = table_ref.shape[0]
    valid = len_ref[0]

    @pl.when(block == 0)
    def _():
        pick_head = (iota2((heads * 8, heads), 0) >> 3) == iota2((heads * 8, heads), 1)
        rows_of = dg(pick_head.astype(F32).astype(BF), table_ref[...], NT).astype(BF)
        shape = (entries, entries * 8)
        pick_entry = iota2(shape, 0) == (iota2(shape, 1) >> 3)
        wide = dg(rows_of, pick_entry.astype(F32).astype(BF), NN)
        shape = (heads * 8, entries * 8)
        same = (iota2(shape, 0) & 7) == (iota2(shape, 1) & 7)
        spread_ref[...] = jnp.where(same, wide, 0.0).astype(BF)

    for kind in range(3):
        turned = ids_ref[0, kind].astype(F32).T
        held_ref[kind] = turned
        turned_ref[kind] = turned.astype(BF)

    def body(step, carry):
        parts = []
        for u in range(2):
            group = pl.ds(pl.multiple_of(step * 16 + u * 8, 8), 8)
            onehot_rows([held_ref[kind, group, :] for kind in range(3)], oh_ref.at[u], entries // 3)
            parts.append(dg(spread_ref[...], oh_ref[u], NN).reshape(heads, 8, length))
        bias = jnp.concatenate(parts, axis=1)
        key = iota2((1, 16, length), 1) + (block * rows + step * 16)
        out_ref[:, pl.ds(pl.multiple_of(step * 16, 16), 16), :] = jnp.where(
            key < valid, bias, MASKED
        ).astype(BF)
        return carry

    lax.fori_loop(0, rows // 16, body, 0, unroll=4)


def bias_scores(buckets, valid, table, rows=128):
    length = buckets.shape[-1]
    entries, heads = table.shape
    return pl.pallas_call(
        bias_kernel,
        grid=(length // rows,),
        in_specs=[
            SMEM,
            pl.BlockSpec((1, 3, length, rows), lambda i: (0, 0, 0, i)),
            pl.BlockSpec((entries, heads), lambda i: (0, 0)),
        ],
        out_specs=[
            pl.BlockSpec((heads, rows, length), lambda i: (0, i, 0)),
            pl.BlockSpec((3, rows, length), lambda i: (0, i, 0)),
        ],
        out_shape=[shaped((heads, length, length), BF), shaped((3, length, length), BF)],
        scratch_shapes=[
            pltpu.VMEM((heads * 8, entries * 8), BF),
            pltpu.VMEM((3, rows, length), F32),
            pltpu.VMEM((2, entries * 8, length), BF),
        ],
        compiler_params=params(),
        name="bias_scores",
    )(valid, buckets, table)


def table_kernel(ids_ref, grad_ref, out_ref, acc_ref, oh_ref):
    heads, rows, length = grad_ref.shape
    entries = out_ref.shape[0]

    @pl.when(pl.program_id(0) == 0)
    def _():
        acc_ref[...] = jnp.zeros_like(acc_ref)

    def body(step, carry):
        tile = pl.ds(pl.multiple_of(step * 16, 16), 16)
        grads = grad_ref[:, tile, :].astype(F32)
        ids = [ids_ref[kind, tile, :].astype(F32) for kind in range(3)]
        total = None
        for u in range(2):
            part = slice(u * 8, (u + 1) * 8)
            onehot_rows([item[part] for item in ids], oh_ref.at[u], entries // 3)
            part = dg(oh_ref[u], grads[:, part, :].reshape(heads * 8, length).astype(BF), NT)
            total = part if total is None else total + part
        acc_ref[...] += total
        return carry

    lax.fori_loop(0, rows // 16, body, 0, unroll=4)

    @pl.when(pl.program_id(0) == pl.num_programs(0) - 1)
    def _():
        shape = acc_ref.shape
        same = (iota2(shape, 0) & 7) == (iota2(shape, 1) & 7)
        kept = jnp.where(same, acc_ref[...], 0.0)
        rows_in = kept.reshape(entries, 8, heads * 8).sum(axis=1)
        fold = ((iota2((heads * 8, heads), 0) >> 3) == iota2((heads * 8, heads), 1)).astype(F32)
        out_ref[...] = lax.dot_general(
            rows_in, fold, NN, precision=lax.Precision.HIGHEST, preferred_element_type=F32
        )


def table_grad(ids, grads, entries, rows=64):
    heads, length, _ = grads.shape
    return pl.pallas_call(
        table_kernel,
        grid=(length // rows,),
        in_specs=[
            pl.BlockSpec((3, rows, length), lambda i: (0, i, 0)),
            pl.BlockSpec((heads, rows, length), lambda i: (0, i, 0)),
        ],
        out_specs=pl.BlockSpec((entries, heads), lambda i: (0, 0)),
        out_shape=shaped((entries, heads), F32),
        scratch_shapes=[
            pltpu.VMEM((entries * 8, heads * 8), F32),
            pltpu.VMEM((2, entries * 8, length), BF),
        ],
        compiler_params=params(),
        name="table_grad",
    )(ids, grads)


class Weight:
    def __init__(self, pieces, unit, shape):
        self.pieces = pieces
        self.unit = unit
        self.shape = shape


def start_fetch(refs, units_ref, unit, whole_ref, sem_ref, first):
    copies = []
    for index, ref in enumerate(refs):
        begin = pl.multiple_of(units_ref[index] * unit, unit)
        copy = pltpu.make_async_copy(
            ref, whole_ref.at[pl.ds(begin, ref.shape[0])], sem_ref.at[first + index]
        )
        copy.start()
        copies.append(copy)
    return copies


def finish(copies):
    for copy in copies:
        copy.wait()


def attend_kernel(*refs, size, count, unit, factor):
    units_ref, x_ref, shift_ref, bias_ref = refs[:4]
    pieces = refs[4 : 4 + count]
    qkv_ref, p_ref, o_ref, w_ref, sem_ref = refs[4 + count :]
    pair = pl.program_id(0)
    model = x_ref.shape[1]
    width = o_ref.shape[1]

    @pl.when(pair == 0)
    def _():
        finish(start_fetch(pieces, units_ref, unit, w_ref, sem_ref, 0))
        for part in range(3):
            cols = slice(part * model, (part + 1) * model)
            value = dg(x_ref[...], w_ref[:, cols], NN) + shift_ref[:, cols]
            if part == 0:
                value = value * factor
            qkv_ref[:, cols] = value.astype(BF)

    def block(part):
        return qkv_ref[:, pl.ds(pl.multiple_of(part * model + pair * width, width), width)]

    lane = iota2((1, width), 1)
    q = block(0)
    k = block(1)
    vt = block(2).T
    mixed = []
    for g in range(width // size):
        mine = (lane >= g * size) & (lane < (g + 1) * size)
        scores = dg(jnp.where(mine, k, jnp.zeros_like(k)), q, NT) + bias_ref[g].astype(F32)
        top = jnp.max(scores, axis=0, keepdims=True)
        shifted = jnp.exp(scores - top)
        norm = jnp.sum(shifted, axis=0, keepdims=True)
        probs = (shifted * (1.0 / norm)).astype(BF)
        p_ref[g] = probs
        mixed.append(dg(vt[g * size : (g + 1) * size], probs, NN))
    o_ref[...] = jnp.concatenate(mixed, axis=0).T.astype(BF)


def attend(units, tokens, shift_row, weight, bias, size):
    length, model = tokens.shape
    group = WIDE // size
    count = len(weight.pieces)
    return pl.pallas_call(
        functools.partial(
            attend_kernel, size=size, count=count, unit=weight.unit, factor=size**-0.5
        ),
        grid=(model // WIDE,),
        in_specs=[
            SMEM,
            pl.BlockSpec((length, model), lambda i: (0, 0)),
            pl.BlockSpec((1, 3 * model), lambda i: (0, 0)),
            pl.BlockSpec((group, length, length), lambda i: (i, 0, 0)),
        ]
        + [ANY] * count,
        out_specs=[
            pl.BlockSpec((length, 3 * model), lambda i: (0, 0)),
            pl.BlockSpec((group, length, length), lambda i: (i, 0, 0)),
            pl.BlockSpec((length, WIDE), lambda i: (0, i)),
        ],
        out_shape=[
            shaped((length, 3 * model), BF),
            shaped((model // size, length, length), BF),
            shaped((length, model), BF),
        ],
        scratch_shapes=[
            pltpu.VMEM(weight.shape, BF),
            pltpu.SemaphoreType.DMA((count,)),
        ],
        compiler_params=params(),
        name="attend",
    )(units, tokens, shift_row, bias, *weight.pieces)


def attend_back_kernel(
    q_ref, k_ref, v_ref, p_ref, o_ref, g_ref, out_ref, ds_ref, *, size, factor
):
    pair = pl.program_id(0)
    width = q_ref.shape[1]
    model = out_ref.shape[1] // 3
    count = width // size
    lane = iota2((1, width), 1)
    q = q_ref[...]
    v = v_ref[...]
    ob = g_ref[...]
    kt = k_ref[...].T
    product = o_ref[...].astype(F32) * ob.astype(F32)
    qs, ks, vs = [], [], []
    for g in range(count):
        mine = (lane >= g * size) & (lane < (g + 1) * size)
        spare = ((g + 1) % count) * size
        inner = jnp.sum(jnp.where(mine, product, 0.0), axis=1, keepdims=True)
        high = inner.astype(BF).astype(F32)
        extra = jnp.where(lane == spare, high, jnp.where(lane == spare + 1, inner - high, 0.0))
        minus = jnp.where((lane == spare) | (lane == spare + 1), -1.0, 0.0)
        left = jnp.where(mine, v, minus.astype(BF))
        right = jnp.where(mine, ob, extra.astype(BF))
        probs = p_ref[g]
        ds = (probs.astype(F32) * dg(left, right, NT)).astype(BF)
        ds_ref[g] = ds
        vs.append(dg(probs, ob, NN))
        ks.append(dg(ds, q, NN))
        qs.append(dg(kt[g * size : (g + 1) * size], ds, NN))

    def pick(items):
        chosen = items[0]
        for g in range(1, count):
            chosen = jnp.where(lane >= g * size, items[g], chosen)
        return chosen

    def place(start):
        return pl.ds(pl.multiple_of(start + pair * width, width), width)

    q_grad = jnp.concatenate(qs, axis=0).T.astype(BF).astype(F32) * factor
    out_ref[:, place(0)] = q_grad.astype(BF)
    out_ref[:, place(model)] = pick(ks).astype(BF)
    out_ref[:, place(2 * model)] = pick(vs).astype(BF)


def attend_back(qkv, probs, mixed, grad_mixed, size):
    length = qkv.shape[0]
    model = qkv.shape[1] // 3
    blocks = model // WIDE
    group = WIDE // size
    return pl.pallas_call(
        functools.partial(attend_back_kernel, size=size, factor=size**-0.5),
        grid=(blocks,),
        in_specs=[
            pl.BlockSpec((length, WIDE), lambda i: (0, i)),
            pl.BlockSpec((length, WIDE), lambda i: (0, blocks + i)),
            pl.BlockSpec((length, WIDE), lambda i: (0, 2 * blocks + i)),
            pl.BlockSpec((group, length, length), lambda i: (i, 0, 0)),
            pl.BlockSpec((length, WIDE), lambda i: (0, i)),
            pl.BlockSpec((length, WIDE), lambda i: (0, i)),
        ],
        out_specs=[
            pl.BlockSpec((length, 3 * model), lambda i: (0, 0)),
            pl.BlockSpec((group, length, length), lambda i: (i, 0, 0)),
        ],
        out_shape=[
            shaped((length, 3 * model), BF),
            shaped((model // size, length, length), BF),
        ],
        compiler_params=params(),
        name="attend_back",
    )(qkv, qkv, qkv, probs, mixed, grad_mixed)


def norm_forward(inputs, gain_vec, shift_vec):
    center = inputs - jnp.mean(inputs, axis=-1, keepdims=True)
    inverse = lax.rsqrt(jnp.mean(center * center, axis=-1, keepdims=True) + EPSILON)
    scaled = center * inverse
    return (scaled * gain_vec + shift_vec, scaled, inverse)


def norm_backward(grad_in, scaled, inverse, gain_vec):
    inner_term = grad_in * gain_vec
    centered = inner_term - jnp.mean(inner_term, axis=-1, keepdims=True)
    return inverse * (centered - scaled * jnp.mean(inner_term * scaled, axis=-1, keepdims=True))


def gelu_pair(u):
    square = jnp.exp(u * u * -0.5)
    t = 1.0 / (1.0 + jnp.abs(u) * (0.3275911 * 0.7071067811865476))
    poly = t * (
        0.254829592
        + t * (-0.284496736 + t * (1.421413741 + t * (-1.453152027 + t * 1.061405429)))
    )
    tail = 0.5 * poly * square
    below = jnp.where(u >= 0.0, 1.0 - tail, tail)
    return u * below, below + u * (square * 0.3989422804014327)


def column_sum(values):
    return jnp.sum(values, axis=0, keepdims=True)


OUT_B, GAIN1, SHIFT1, DOWN_B, GAIN2, SHIFT2 = range(2, 8)


def forward_kernel(*refs, count, unit_out, unit_up, unit_down, chunk):
    units_ref, len_ref, mixed_ref, x_ref, cot_ref, vec_ref, upb_ref = refs[:7]
    out_pieces = refs[7 : 7 + count]
    up_pieces = refs[7 + count : 7 + 2 * count]
    down_pieces = refs[7 + 2 * count : 7 + 3 * count]
    (
        y_ref,
        n1_ref,
        z1_ref,
        r1_ref,
        hidden_out,
        slope_out,
        fb_ref,
        r2_ref,
        sums_ref,
        w_out,
        w_up,
        w_down,
        hidden,
        slope,
        sem_ref,
        out_sem,
    ) = refs[7 + 3 * count :]
    first = start_fetch(out_pieces, units_ref, unit_out, w_out, sem_ref, 0)
    second = start_fetch(up_pieces, units_ref, unit_up, w_up, sem_ref, count)
    third = start_fetch(down_pieces, units_ref, unit_down, w_down, sem_ref, 2 * count)

    def vec(row):
        return vec_ref[row : row + 1, :]

    finish(first)
    summed = x_ref[...].astype(F32) + (dg(mixed_ref[...], w_out[...], NN) + vec(OUT_B))
    n1, z1, r1 = norm_forward(summed, vec(GAIN1), vec(SHIFT1))
    low = n1.astype(BF)
    n1_ref[...] = low
    z1_ref[...] = z1
    r1_ref[...] = r1
    finish(second)
    total = hidden.shape[1]
    for begin in range(0, total, chunk):
        cols = slice(begin, begin + chunk)
        h, s = gelu_pair(dg(low, w_up[:, cols], NN) + upb_ref[:, cols])
        hidden[:, cols] = h.astype(BF)
        slope[:, cols] = s.astype(BF)
    saves = [
        pltpu.make_async_copy(hidden, hidden_out, out_sem.at[0]),
        pltpu.make_async_copy(slope, slope_out, out_sem.at[1]),
    ]
    for save in saves:
        save.start()
    finish(third)
    n2, z2, r2 = norm_forward(
        n1 + (dg(hidden[...], w_down[...], NN) + vec(DOWN_B)), vec(GAIN2), vec(SHIFT2)
    )
    rows = x_ref.shape[0]
    valid = (iota2((rows, 1), 0) < len_ref[0]).astype(F32)
    y_ref[...] = (n2 * valid).astype(BF)
    g2 = cot_ref[...].astype(F32) * valid
    back = norm_backward(g2, z2, r2, vec(GAIN2))
    r2_ref[...] = back
    fb = back.astype(BF)
    fb_ref[...] = fb
    sums_ref[...] = jnp.concatenate(
        [column_sum(fb.astype(F32)), column_sum(g2 * z2), column_sum(g2)]
        + [jnp.zeros((5, x_ref.shape[1]), F32)],
        axis=0,
    )
    finish(saves)


def forward(units, lengths, mixed, tokens, cotangent, vecs, up_bias, w_out, w_up, w_down):
    length, model = tokens.shape
    wide = up_bias.shape[1]
    count = len(w_out.pieces)
    return pl.pallas_call(
        functools.partial(
            forward_kernel,
            count=count,
            unit_out=w_out.unit,
            unit_up=w_up.unit,
            unit_down=w_down.unit,
            chunk=512,
        ),
        in_specs=[SMEM, SMEM] + [VMEM] * 5 + [ANY] * (3 * count),
        out_specs=[VMEM] * 4 + [ANY] * 2 + [VMEM] * 3,
        out_shape=[
            shaped((length, model), BF),
            shaped((length, model), BF),
            shaped((length, model), F32),
            shaped((length, 1), F32),
            shaped((length, wide), BF),
            shaped((length, wide), BF),
            shaped((length, model), BF),
            shaped((length, model), F32),
            shaped((8, model), F32),
        ],
        scratch_shapes=[
            pltpu.VMEM(w_out.shape, BF),
            pltpu.VMEM(w_up.shape, BF),
            pltpu.VMEM(w_down.shape, BF),
            pltpu.VMEM((length, wide), BF),
            pltpu.VMEM((length, wide), BF),
            pltpu.SemaphoreType.DMA((3 * count,)),
            pltpu.SemaphoreType.DMA((2,)),
        ],
        compiler_params=params(),
        name="forward",
    )(
        units,
        lengths,
        mixed,
        tokens,
        cotangent,
        vecs,
        up_bias,
        *w_out.pieces,
        *w_up.pieces,
        *w_down.pieces,
    )


def backward_kernel(*refs, count, unit_out, unit_up, unit_down, chunk):
    units_ref, fb_ref, r2_ref, z1_ref, r1_ref, vec_ref, slope_in = refs[:7]
    out_pieces = refs[7 : 7 + count]
    up_pieces = refs[7 + count : 7 + 2 * count]
    down_pieces = refs[7 + 2 * count : 7 + 3 * count]
    (
        ub_out,
        back_ref,
        ab_ref,
        ob_ref,
        sums_ref,
        upsum_ref,
        w_out,
        w_up,
        w_down,
        slope,
        sem_ref,
        own_sem,
    ) = refs[7 + 3 * count :]
    load = pltpu.make_async_copy(slope_in, slope, own_sem.at[0])
    third = start_fetch(down_pieces, units_ref, unit_down, w_down, sem_ref, 0)
    load.start()
    second = start_fetch(up_pieces, units_ref, unit_up, w_up, sem_ref, count)
    first = start_fetch(out_pieces, units_ref, unit_out, w_out, sem_ref, 2 * count)
    fb = fb_ref[...]
    finish(third)
    load.wait()
    for begin in range(0, slope.shape[1], chunk):
        cols = slice(begin, begin + chunk)
        ub = (slope[:, cols].astype(F32) * dg(fb, w_down[cols, :], NT)).astype(BF)
        slope[:, cols] = ub
        upsum_ref[:, cols] = column_sum(ub.astype(F32))
    save = pltpu.make_async_copy(slope, ub_out, own_sem.at[1])
    save.start()
    finish(second)
    n1b = r2_ref[...] + dg(slope[...], w_up[...], NT)
    z1 = z1_ref[...]
    back = norm_backward(n1b, z1, r1_ref[...], vec_ref[GAIN1 : GAIN1 + 1, :])
    back_ref[...] = back
    ab = back.astype(BF)
    ab_ref[...] = ab
    sums_ref[...] = jnp.concatenate(
        [column_sum(ab.astype(F32)), column_sum(n1b * z1), column_sum(n1b)]
        + [jnp.zeros((5, z1.shape[1]), F32)],
        axis=0,
    )
    finish(first)
    ob_ref[...] = dg(ab, w_out[...], NT).astype(BF)
    save.wait()


def backward(units, fb, r2, z1, r1, vecs, slope, w_out, w_up, w_down):
    length, model = fb.shape
    wide = slope.shape[1]
    count = len(w_out.pieces)
    return pl.pallas_call(
        functools.partial(
            backward_kernel,
            count=count,
            unit_out=w_out.unit,
            unit_up=w_up.unit,
            unit_down=w_down.unit,
            chunk=512,
        ),
        in_specs=[SMEM] + [VMEM] * 5 + [ANY] * (1 + 3 * count),
        out_specs=[ANY] + [VMEM] * 5,
        out_shape=[
            shaped((length, wide), BF),
            shaped((length, model), F32),
            shaped((length, model), BF),
            shaped((length, model), BF),
            shaped((8, model), F32),
            shaped((1, wide), F32),
        ],
        scratch_shapes=[
            pltpu.VMEM(w_out.shape, BF),
            pltpu.VMEM(w_up.shape, BF),
            pltpu.VMEM(w_down.shape, BF),
            pltpu.VMEM((length, wide), BF),
            pltpu.SemaphoreType.DMA((3 * count,)),
            pltpu.SemaphoreType.DMA((2,)),
        ],
        compiler_params=params(),
        name="backward",
    )(
        units,
        fb,
        r2,
        z1,
        r1,
        vecs,
        slope,
        *w_out.pieces,
        *w_up.pieces,
        *w_down.pieces,
    )


def inputs_kernel(*refs, count, unit):
    units_ref, pb_ref, back_ref = refs[:3]
    pieces = refs[3 : 3 + count]
    out_ref, sums_ref, w_ref, sem_ref = refs[3 + count :]
    copies = start_fetch(pieces, units_ref, unit, w_ref, sem_ref, 0)
    pb = pb_ref[...]
    sums_ref[...] = column_sum(pb.astype(F32))
    finish(copies)
    out_ref[...] = (back_ref[...] + dg(pb, w_ref[...], NT)).astype(BF)


def inputs_grad(units, grad_packed, back, weight):
    length, model = back.shape
    count = len(weight.pieces)
    return pl.pallas_call(
        functools.partial(inputs_kernel, count=count, unit=weight.unit),
        in_specs=[SMEM] + [VMEM] * 2 + [ANY] * count,
        out_specs=[VMEM] * 2,
        out_shape=[shaped((length, model), BF), shaped((1, 3 * model), F32)],
        scratch_shapes=[
            pltpu.VMEM(weight.shape, BF),
            pltpu.SemaphoreType.DMA((count,)),
        ],
        compiler_params=params(),
        name="inputs_grad",
    )(units, grad_packed, back, *weight.pieces)


def product_kernel(at_ref, left_ref, right_ref, *rest):
    value = dg(left_ref[...], right_ref[...], TN)
    if len(rest) == 2:
        value = value + rest[0][...].astype(F32)
    rest[-1][...] = value.astype(BF)


def product(left, right, half, halves, extra=None):
    length, rows = left.shape
    columns = right.shape[1] // halves
    if rows % WIDE or columns % WIDE:
        value = dg(left, lax.dynamic_slice_in_dim(right, half * columns, columns, 1), TN)
        return (value if extra is None else value + extra.astype(F32)).astype(BF)
    step = WIDE
    while step < 512 and rows % (2 * step) == 0:
        step *= 2
    spec = pl.BlockSpec((step, columns), lambda i, at: (i, 0))
    return pl.pallas_call(
        product_kernel,
        grid_spec=pltpu.PrefetchScalarGridSpec(
            num_scalar_prefetch=1,
            grid=(rows // step,),
            in_specs=[
                pl.BlockSpec((length, step), lambda i, at: (0, i)),
                pl.BlockSpec((length, columns), lambda i, at: (0, at[0])),
            ]
            + ([] if extra is None else [spec]),
            out_specs=spec,
        ),
        out_shape=shaped((rows, columns), BF),
        compiler_params=params(),
        name="product",
    )(half.reshape(1), left, right, *(() if extra is None else (extra,)))


def finish_kernel(at_ref, mine_ref, theirs_ref, out_ref):
    columns = mine_ref.shape[1]
    first = at_ref[0] == 0
    mine = mine_ref[...]
    theirs = theirs_ref[...]
    out_ref[:, :columns] = jnp.where(first, mine, theirs).astype(F32)
    out_ref[:, columns:] = jnp.where(first, theirs, mine).astype(F32)


def finish_pair(core, mine, theirs):
    rows, columns = mine.shape
    step = rows // 4 if (rows // 4) % 16 == 0 else rows
    spec = pl.BlockSpec((step, columns), lambda i: (i, 0))
    return pl.pallas_call(
        finish_kernel,
        grid=(rows // step,),
        in_specs=[SMEM, spec, spec],
        out_specs=pl.BlockSpec((step, 2 * columns), lambda i: (i, 0)),
        out_shape=shaped((rows, 2 * columns), F32),
        compiler_params=params(),
        name="finish_pair",
    )(core.reshape(1), mine, theirs)


class Axis:
    def __init__(self, name, total, stride, size):
        self.name = name
        self.total = total
        self.stride = stride
        self.size = size
        self.at = (lax.axis_index(name) // stride) % size

    def send(self, value, step):
        pairs = []
        for index in range(self.total):
            place = (index // self.stride) % self.size
            pairs.append((index, index + ((place + step) % self.size - place) * self.stride))
        return lax.ppermute(value, self.name, pairs)

    def peer(self, step):
        return (self.at + step) % self.size


def tie(value, *others):
    return lax.optimization_barrier((value,) + others)[0]


def take(stack, index, dim=0):
    return lax.dynamic_index_in_dim(stack, index, axis=dim, keepdims=False)


def gather(axis, block, dim=0):
    if axis.size == 1:
        return jnp.expand_dims(block, dim)
    shape = [1] * (block.ndim + 1)
    shape[dim] = axis.size
    place = jnp.arange(axis.size, dtype=jnp.int32).reshape(shape)
    stack = jnp.expand_dims(block, dim)
    for step in range(1, axis.size):
        got = jnp.expand_dims(axis.send(block, step), dim)
        stack = jnp.where(place == axis.peer(-step), got, stack)
    return stack


class Links:
    def __init__(self, dp, fsdp):
        core = 2 if dp % 2 == 0 else 1
        rest = dp // core
        near = 2 if rest % 2 == 0 else 1
        self.core = Axis("dp", dp, 1, core)
        self.near = Axis("dp", dp, core, near)
        self.far = Axis("dp", dp, core * near, rest // near)
        self.shard = Axis("fsdp", fsdp, 1, fsdp)

    def plan(self, least_rows):
        core, near, shard = self.core, self.near, self.shard
        self.sharing = (core, near)
        if least_rows % (core.size * near.size * 16):
            self.sharing = (core,)
        parts = 1
        for axis in self.sharing:
            parts *= axis.size
        self.parts = parts
        units = [shard.at * parts]
        for step in range(1, shard.size):
            base = shard.peer(-step) * parts
            if len(self.sharing) == 1:
                spots = [core.peer(-s) for s in range(core.size)]
            else:
                spots = [
                    core.peer(-s) * near.size + near.peer(-t)
                    for s in range(core.size)
                    for t in range(near.size)
                ]
            units += [base + spot for spot in spots]
        return jnp.stack(units).astype(jnp.int32)

    def fetch(self, block, *after):
        core, near, shard = self.core, self.near, self.shard
        rows, columns = block.shape
        unit = rows // self.parts
        stack = block.reshape(self.parts, unit, columns)
        spot = core.at if len(self.sharing) == 1 else core.at * near.size + near.at
        mine = take(stack, spot)
        if after:
            mine = tie(mine, *after)
        pieces = [block]
        hops = []
        for step in range(1, shard.size):
            group = [shard.send(mine, step)]
            hops.append(group[0])
            if len(self.sharing) > 1:
                group += [near.send(group[0], t) for t in range(1, near.size)]
            pieces += group
            for s in range(1, core.size):
                pieces += [core.send(item, s) for item in group]
        return Weight(pieces, unit, (rows * shard.size, columns)), hops

    def halves(self, left, right, *after):
        core = self.core
        if core.size == 1:
            return product(left, right, core.at, 1)
        sent = product(left, right, core.peer(1), core.size)
        got = core.send(sent, 1)
        return sent, lambda: product(left, right, core.at, core.size, got)

    def spread(self, half):
        rows, columns = half.shape
        sizes = (self.shard.size, self.near.size, self.far.size)
        return half.reshape(sizes + (rows // (sizes[0] * sizes[1] * sizes[2]), columns))

    def hop(self, terms, axis, dim, *after):
        if axis.size == 1:
            return [take(term, axis.at, dim) for term in terms], []

        def part(index):
            total = None
            for term in terms:
                piece = take(term, index, dim).astype(F32)
                total = piece if total is None else total + piece
            return total.astype(BF)

        kept = [take(term, axis.at, dim) for term in terms]
        sent = []
        for step in range(1, axis.size):
            value = part(axis.peer(step))
            sent.append(tie(value, *after) if after else value)
        return kept + [axis.send(value, step + 1) for step, value in enumerate(sent)], sent

    def settle(self, terms):
        total = terms[0].astype(F32)
        for term in terms[1:]:
            total = total + term.astype(F32)
        return total.astype(BF)

    def spread_out(self, block):
        whole = gather(self.near, gather(self.far, block))
        whole = whole.reshape(-1, block.shape[-1])
        if self.core.size == 1:
            return whole.astype(F32)
        return finish_pair(self.core.at, whole, self.core.send(whole, 1))

    def reduce_vector(self, stack):
        shard = self.shard
        total = take(stack, shard.at)
        for step in range(1, shard.size):
            total = total + shard.send(take(stack, shard.peer(step)), step)
        for axis in (self.core, self.near, self.far):
            part = total
            for step in range(1, axis.size):
                total = total + axis.send(part, step)
        return total


def pack(items, shards):
    return jnp.concatenate([item.reshape(shards, -1) for item in items], axis=1)


def split(vector, sizes):
    pieces = []
    begin = 0
    for count in sizes:
        pieces.append(vector[begin : begin + count])
        begin += count
    return pieces


def per_device(
    dp,
    fsdp,
    tokens,
    lengths,
    buckets,
    qkv_weight,
    q_bias,
    v_bias,
    out_weight,
    out_bias,
    bias_table,
    norm1_gain,
    norm1_bias,
    up_weight,
    up_bias,
    down_weight,
    down_bias,
    norm2_gain,
    norm2_bias,
    cotangent,
):
    links = Links(dp, fsdp)
    model = tokens.shape[1]
    heads = bias_table.shape[1]
    size = model // heads
    units = links.plan(min(out_weight.shape[0], down_weight.shape[0]))

    w_qkv, hop_qkv = links.fetch(qkv_weight)
    table = gather(links.shard, bias_table).reshape(-1, heads)
    narrow = (q_bias, v_bias, out_bias, norm1_gain, norm1_bias, down_bias, norm2_gain, norm2_bias)
    row = jnp.arange(8, dtype=jnp.int32)[:, None]
    rows = jnp.broadcast_to(narrow[0][None], (8, narrow[0].size))
    for index in range(1, 8):
        rows = jnp.where(row == index, narrow[index][None], rows)
    vecs = jnp.swapaxes(gather(links.shard, rows), 0, 1).reshape(8, model).astype(F32)
    up_vec = gather(links.shard, up_bias).reshape(1, -1).astype(F32)
    w_out, hop_out = links.fetch(out_weight, *hop_qkv)
    w_up, hop_up = links.fetch(up_weight, *hop_qkv)
    w_down, _ = links.fetch(down_weight, *hop_up)

    bias, ids = bias_scores(buckets, lengths, table)
    shift_row = jnp.concatenate([vecs[0:1], jnp.zeros((1, model), F32), vecs[1:2]], axis=1)
    qkv, probs, mixed = attend(units, tokens, shift_row, w_qkv, bias, size)
    output, n1, z1, r1, hidden, slope, fb, r2, sums_two = forward(
        units, lengths, mixed, tokens, cotangent, vecs, up_vec, w_out, w_up, w_down
    )

    sent_down, half_down = links.halves(hidden, fb)
    fb = tie(fb, sent_down)
    ub, back, ab, ob, sums_one, up_sum = backward(
        units, fb, r2, z1, r1, vecs, slope, w_out, w_up, w_down
    )
    down = links.spread(half_down())
    down, sent = links.hop([down], links.shard, 0)
    ub = tie(ub, *sent)
    sent_up, half_up = links.halves(n1, ub)
    ab = tie(ab, sent_up)
    sent_out, half_out = links.halves(mixed, ab)
    up = links.spread(half_up())
    up, sent = links.hop([up], links.near, 1)
    out = links.spread(half_out())
    ob = tie(ob, out, *sent)
    grad_packed, grad_scores = attend_back(qkv, probs, mixed, ob, size)
    sent_qkv, half_qkv = links.halves(tokens, grad_packed)
    qkv_part = links.spread(half_qkv())
    grad_scores = tie(grad_scores, qkv_part)
    g_table = table_grad(ids, grad_scores, table.shape[0])
    grad_packed = tie(grad_packed, g_table)
    tokens_grad, packed_sums = inputs_grad(units, grad_packed, back, w_qkv)

    got_down = down[-1]
    down, _ = links.hop(down, links.near, 0, up[-1])
    down, _ = links.hop(down, links.far, 0)
    up, _ = links.hop(up, links.shard, 0, got_down)
    got_up = up[-1]
    up, _ = links.hop(up, links.far, 0)
    out, _ = links.hop([out], links.shard, 0, got_up)
    qkv_terms, _ = links.hop([qkv_part], links.shard, 0, got_up)
    out, _ = links.hop(out, links.near, 0)
    out, _ = links.hop(out, links.far, 0)
    qkv_terms, _ = links.hop(qkv_terms, links.near, 0)
    qkv_terms, _ = links.hop(qkv_terms, links.far, 0)

    g_down = links.spread_out(links.settle(down))
    g_up = links.spread_out(links.settle(up))
    g_out = links.spread_out(links.settle(out))
    g_qkv = links.spread_out(links.settle(qkv_terms))

    early = links.reduce_vector(
        pack((sums_one[0], sums_one[1], sums_one[2], up_sum, sums_two[0], sums_two[1], sums_two[2]), fsdp)
    )
    late = links.reduce_vector(
        pack((g_table, packed_sums[0, :model], packed_sums[0, 2 * model :]), fsdp)
    )
    part = out_bias.size
    g_out_bias, g_gain_one, g_shift_one, g_up_bias, g_down_bias, g_gain_two, g_shift_two = split(
        early, (part, part, part, up_bias.size, part, part, part)
    )
    g_table, g_query_bias, g_value_bias = split(late, (bias_table.size, part, part))
    return (
        output,
        tokens_grad,
        g_qkv,
        g_query_bias,
        g_value_bias,
        g_out,
        g_out_bias,
        g_table.reshape(bias_table.shape),
        g_gain_one,
        g_shift_one,
        g_up,
        g_up_bias,
        g_down,
        g_down_bias,
        g_gain_two,
        g_shift_two,
    )


def solution(mesh):
    rows = P(("dp", "fsdp"), None)
    mat = P("fsdp", None)
    vec = P("fsdp")
    return jax.shard_map(
        functools.partial(per_device, mesh.shape["dp"], mesh.shape["fsdp"]),
        mesh=mesh,
        in_specs=(
            rows,
            P(("dp", "fsdp")),
            P(("dp", "fsdp"), None, None, None),
            mat,
            vec,
            vec,
            mat,
            vec,
            mat,
            vec,
            vec,
            mat,
            vec,
            mat,
            vec,
            vec,
            vec,
            rows,
        ),
        out_specs=(
            rows,
            rows,
            mat,
            vec,
            vec,
            mat,
            vec,
            mat,
            vec,
            vec,
            mat,
            vec,
            mat,
            vec,
            vec,
            vec,
        ),
        check_vma=False,
    )
```

time: 485 us -> 414 us (0.85)
  Pallas kernels: 51 us -> 155 us
  local copies, waits for them, and re-layouts: 108 us -> 29.2 us
  matrix products: 72.1 us -> 0 us
  waiting for transfers between devices: 122 us -> 100 us
    pallas_call x3 -> x18, Pallas kernels: 39.5 us -> 144 us  [the longest x8 39.9 us: product(): pl.pallas_call(product_kernel, grid_spec=pltpu.PrefetchScalarGridSpec(num...]
    dot_general x16 -> x0, matrix products: 72.1 us -> none  [dg(): return lax.dot_general(left, right, dims, preferred_element_type=F32)]
    reshape x7 -> x0, local copies, waits for them, and re-layouts: 23 us -> none  [the longest x4 16.8 us: reduce(): return jnp.swapaxes(done, 0, 1).reshape(rows, core.size * columns)]
    unnamed x103 -> x117, local copies, waits for them, and re-layouts: 32.1 us -> 10.6 us
    ppermute x69 -> x75, waiting for transfers between devices: 122 us -> 100 us  [send(): return lax.ppermute(value, self.name, pairs)]
    dynamic_update_slice x54 -> x0, local copies, waits for them, and re-layouts: 18.9 us -> none  [the longest x29 8.92 us: gather(): lax.dynamic_update_index_in_dim(stack, axis.send(block, step), axis.peer(...]
    reduce_sum x7 -> x0, other arithmetic: 10.7 us -> none  [the longest x3 6.38 us: column_sum(): return jnp.sum(grad_low.astype(F32), axis=0)]
    convert_element_type x4 -> x13, other arithmetic: 1.34 us -> 11.6 us  [the longest x8 7.56 us: part(): return total.astype(BF)]
  transfers between devices with their start and end apart: 69 -> 75, of which waited for: 26 -> 20; matrix products, arithmetic and copies ran while one was open for 29% -> 11% of each run, Pallas kernels for 8% -> 28%
where the time goes in v2:
time: 414 us; the launch traced here: 407 us
  Pallas kernels  155 us (37%)
  waiting for transfers between devices  100 us (24%)
  starting transfers between devices  95.2 us (23%)
  local copies, waits for them, and re-layouts  29.2 us (7%)
  other arithmetic  24.5 us (6%)
    ppermute x75, waiting for transfers between devices, send(): return lax.ppermute(value, self.name, pairs)  100 us
    ppermute x75, starting transfers between devices, send(): return lax.ppermute(value, self.name, pairs)  95.2 us
    pallas_call x8, Pallas kernels, product(): pl.pallas_call(product_kernel, grid_spec=pltpu.PrefetchScalarGridSpec(num...  39.9 us
    pallas_call x1, Pallas kernels, forward(): pl.pallas_call(functools.partial(forward_kernel, count=count, unit_out=w_...  19.3 us
    pallas_call x1, Pallas kernels, table_grad(): pl.pallas_call(table_kernel, grid=(length // rows,), in_specs=[pl.BlockSp...  17 us
    pallas_call x4, Pallas kernels, finish_pair(): pl.pallas_call(finish_kernel, grid=(rows // step,), in_specs=[SMEM, spec,...  16.2 us
    pallas_call x1, Pallas kernels, attend(): pl.pallas_call(functools.partial(attend_kernel, size=size, count=count, u...  15.7 us
    pallas_call x1, Pallas kernels, backward(): pl.pallas_call(functools.partial(backward_kernel, count=count, unit_out=w...  15.6 us
  transfers between devices with their start and end apart: 75, of which 20 were waited for; matrix products, arithmetic and copies ran while one was open for 11% of the time, Pallas kernels for 28%

profile of v2, /device:TPU:1, one launch (start us, length us, event | category | flops | bytes accessed | tf_op | source)
XLA Modules:
  0.0 407.2 jit_solution(8088934754348359722)
XLA Ops:
  1.9 2.1 collective-permute-start.2
  5.1 8.8 %collective-permute-done.2.refs_5_.refs_4_ = bf16[96,2304]{1,0:T(8,128)(2,1)S(1)} collective-permute-done((bf16[96,2304]{1,0:T(8,128)(2,1)S(1)}, bf16[96,2304]{1,0:T(8,128)(2,1)S(1)}, u32[]{:S(2)}, u32[]{:S(2)}) %collective-permute-start.2) | collective-permute-done | bytes 442400 | tf_op jit(solution)/shard_map/ppermute | solution.py:694
  16.1 11.3 %collective-permute-done.11.refs_13_ = bf16[96,3072]{1,0:T(8,128)(2,1)S(1)} collective-permute-done((bf16[96,3072]{1,0:T(8,128)(2,1)S(1)}, bf16[96,3072]{1,0:T(8,128)(2,1)S(1)}, u32[]{:S(2)}, u32[]{:S(2)}) %collective-permute-start.11) | collective-permute-done | bytes 589856 | tf_op jit(solution)/shard_map/ppermute | solution.py:694
  30.8 12.6 %collective-permute-done.7.refs_8_ = bf16[96,768]{1,0:T(8,128)(2,1)S(1)} collective-permute-done((bf16[96,768]{1,0:T(8,128)(2,1)S(1)}, bf16[96,768]{1,0:T(8,128)(2,1)S(1)}, u32[]{:S(2)}, u32[]{:S(2)}) %collective-permute-start.7) | collective-permute-done | bytes 147488 | tf_op jit(solution)/shard_map/ppermute | solution.py:694
  49.6 13.0 %bias_scores.1 = (bf16[12,512,512]{2,1,0:T(8,128)(2,1)}, bf16[3,512,512]{2,1,0:T(8,128)(2,1)}) custom-call(s32[1]{0:T(128)S(6)} %copy.46.len_ref.refs_1_, s32[1,3,512,512]{3,2,1,0:T(8,128)} %ids_ref.1, bf16[96,12]{1,0:T(8,128)(2,1)} %bitcast_select_fusion.4.table_ref), custom_call_target="tpu_custom_call" | custom-call | tf_op jit(solution)/shard_map/bias_scores/pallas_call | solution.py:94
  63.6 4.8 %collective-permute-start.4 = (bf16[96,2304]{1,0:T(8,128)(2,1)S(1)}, bf16[96,2304]{1,0:T(8,128)(2,1)S(1)}, u32[]{:S(2)}, u32[]{:S(2)}) collective-permute-start(bf16[96,2304]{1,0:T(8,128)(2,1)S(1)} %collective-permute-done.2.refs_5_.refs_4_), channel_id=1, source_target_pairs={{0,2},{2,0},{4,6},{6,4},{8,10},{10,8},{12,14},{14,12},{16,18},{18,... | collective-permute-start | bytes 1327112 | tf_op jit(solution)/shard_map/ppermute | solution.py:694
  69.1 11.3 %collective-permute-done.3.refs_6_.refs_5_ = bf16[96,2304]{1,0:T(8,128)(2,1)S(1)} collective-permute-done((bf16[96,2304]{1,0:T(8,128)(2,1)S(1)}, bf16[96,2304]{1,0:T(8,128)(2,1)S(1)}, u32[]{:S(2)}, u32[]{:S(2)}) %collective-permute-start.3) | collective-permute-done | bytes 442400 | tf_op jit(solution)/shard_map/ppermute | solution.py:694
  80.4 4.0 collective-permute-start.5
  86.9 15.7 %attend.1 = (bf16[512,2304]{1,0:T(8,128)(2,1)}, bf16[12,512,512]{2,1,0:T(8,128)(2,1)}, bf16[512,768]{1,0:T(8,128)(2,1)}) custom-call(s32[5]{0:T(128)} %stack.23.refs_0_, bf16[512,768]{1,0:T(8,128)(2,1)} %left_ref.3, f32[1,2304]{1,0:T(1,128)} %fusion.34.refs_2_, bf16[12,512,512]{2,1,0:T(8,128)(2,1)} %get-tuple-element.53.refs_3_, bf16[384,2304]{1,0:T(8,128)(2,1)} %refs_3_.3, ...), custom_call_target="tpu_custom_call" | custom-call | tf_op jit(solution)/shard_map/attend/pallas_call | solution.py:238
  104.2 19.3 %forward.1 = (bf16[512,768]{1,0:T(8,128)(2,1)}, bf16[512,768]{1,0:T(8,128)(2,1)}, f32[512,768]{1,0:T(8,128)}, f32[512,1]{1,0:T(8,128)}, bf16[512,3072]{1,0:T(8,1...) custom-call(s32[5]{0:T(128)} %stack.23.refs_0_, ...), custom_call_target="tpu_custom_call" | custom-call | tf_op jit(solution)/shard_map/forward/pallas_call | solution.py:449
  123.5 6.4 %product.8 = bf16[3072,384]{1,0:T(8,128)(2,1)} custom-call(s32[1]{0:T(128)} %bitcast.17.at_ref, bf16[512,3072]{1,0:T(8,128)(2,1)} %get-tuple-element.62.left_ref, bf16[512,768]{1,0:T(8,128)(2,1)} %get-tuple-element.63.right_ref.refs_1_), custom_call_target="tpu_custom_call" | custom-call | tf_op jit(solution)/shard_map/product/pallas_call | solution.py:639
  130.1 15.6 %backward.1 = (bf16[512,3072]{1,0:T(8,128)(2,1)}, f32[512,768]{1,0:T(8,128)}, bf16[512,768]{1,0:T(8,128)(2,1)}, bf16[512,768]{1,0:T(8,128)(2,1)}, f32[8,768]{1,0:T(8,128)}, /*index=5*/f32[1,3072]{1,0:T(1,128)}) custom-call(s32[5]{0:T(128)} %stack.23.refs_0_, bf16[512,768]{1,0:T(8,128)(2,1)} %get-tuple-element.63.right_ref.refs_1_, ...), custom_call_target="tpu_custom_call" | custom-call | tf_op jit(solution)/shard_map/backward/pallas_call | solution.py:551
  147.2 6.8 %product.9 = bf16[3072,384]{1,0:T(8,128)(2,1)} custom-call(s32[1]{0:T(128)} %bitcast.18.at_ref, bf16[512,3072]{1,0:T(8,128)(2,1)} %get-tuple-element.62.left_ref, bf16[512,768]{1,0:T(8,128)(2,1)} %get-tuple-element.63.right_ref.refs_1_, bf16[3072,384]{1,0:T(8,128)(2,1)} %copy-done.14), custom_call_target="tpu_custom_call" | custom-call | tf_op jit(solution)/shard_map/product/pallas_call | solution.py:639
  154.0 2.5 dynamic-slice_bitcast_fusion.1
  156.5 4.7 %product.10 = bf16[768,1536]{1,0:T(8,128)(2,1)} custom-call(s32[1]{0:T(128)} %bitcast.17.at_ref, bf16[512,768]{1,0:T(8,128)(2,1)} %get-tuple-element.70.left_ref, bf16[512,3072]{1,0:T(8,128)(2,1)} %get-tuple-element.72.right_ref), custom_call_target="tpu_custom_call" | custom-call | tf_op jit(solution)/shard_map/product/pallas_call | solution.py:639
  162.1 3.4 product.11
  167.4 5.3 %product.13 = bf16[768,1536]{1,0:T(8,128)(2,1)} custom-call(s32[1]{0:T(128)} %bitcast.18.at_ref, bf16[512,768]{1,0:T(8,128)(2,1)} %get-tuple-element.70.left_ref, bf16[512,3072]{1,0:T(8,128)(2,1)} %get-tuple-element.72.right_ref, bf16[768,1536]{1,0:T(8,128)(2,1)} %copy-done.15), custom_call_target="tpu_custom_call" | custom-call | tf_op jit(solution)/shard_map/product/pallas_call | solution.py:639
  172.7 2.4 dynamic-slice_bitcast_fusion
  179.4 3.6 product.12
  183.0 11.4 %attend_back.1 = (bf16[512,2304]{1,0:T(8,128)(2,1)}, bf16[12,512,512]{2,1,0:T(8,128)(2,1)}) custom-call(bf16[512,2304]{1,0:T(8,128)(2,1)} %get-tuple-element.59.q_ref.k_ref.v_ref, bf16[512,2304]{1,0:T(8,128)(2,1)} %get-tuple-element.59.q_ref.k_ref.v_ref, bf16[512,2304]{1,0:T(8,128)(2,1)} %get-tuple-element.59.q_ref.k_ref.v_ref, ...), custom_call_target="tpu_custom_call" | custom-call | tf_op jit(solution)/shard_map/attend_back/pallas_call | solution.py:319
  194.5 4.8 %product.14 = bf16[768,1152]{1,0:T(8,128)(2,1)} custom-call(s32[1]{0:T(128)} %bitcast.17.at_ref, bf16[512,768]{1,0:T(8,128)(2,1)} %left_ref.3, bf16[512,2304]{1,0:T(8,128)(2,1)} %get-tuple-element.79.right_ref.refs_1_), custom_call_target="tpu_custom_call" | custom-call | tf_op jit(solution)/shard_map/product/pallas_call | solution.py:639
  201.0 2.1 fusion
  204.2 2.2 fusion.1
  211.7 9.0 %collective-permute-done.52 = f32[3840]{0:T(1024)S(1)} collective-permute-done((f32[3840]{0:T(1024)}, f32[3840]{0:T(1024)S(1)}, u32[]{:S(2)}, u32[]{:S(2)}) %collective-permute-start.52) | collective-permute-done | bytes 15392 | tf_op jit(solution)/shard_map/ppermute | solution.py:694
  226.8 2.3 collective-permute-start.68
  232.1 4.8 %product.15 = bf16[768,1152]{1,0:T(8,128)(2,1)} custom-call(s32[1]{0:T(128)} %bitcast.18.at_ref, bf16[512,768]{1,0:T(8,128)(2,1)} %left_ref.3, bf16[512,2304]{1,0:T(8,128)(2,1)} %get-tuple-element.79.right_ref.refs_1_, bf16[768,1152]{1,0:T(8,128)(2,1)} %collective-permute-done.22.rest_0_), custom_call_target="tpu_custom_call" | custom-call | tf_op jit(solution)/shard_map/product/pallas_call | solution.py:639
  236.9 17.0 %table_grad.1 = f32[96,12]{1,0:T(8,128)} custom-call(bf16[3,512,512]{2,1,0:T(8,128)(2,1)} %get-tuple-element.76.ids_ref, bf16[12,512,512]{2,1,0:T(8,128)(2,1)} %get-tuple-element.78.grad_ref), custom_call_target="tpu_custom_call" | custom-call | tf_op jit(solution)/shard_map/table_grad/pallas_call | solution.py:154
  253.9 7.0 %inputs_grad.1 = (bf16[512,768]{1,0:T(8,128)(2,1)}, f32[1,2304]{1,0:T(1,128)}) custom-call(s32[5]{0:T(128)} %stack.23.refs_0_, bf16[512,2304]{1,0:T(8,128)(2,1)} %get-tuple-element.79.right_ref.refs_1_, f32[512,768]{1,0:T(8,128)} %get-tuple-element.80.refs_2_, bf16[384,2304]{1,0:T(8,128)(2,1)} %refs_3_.3, bf16[96,2304]{1,0:T(8,128)(2,1)} %copy-done.16, ...), custom_call_target="tpu_custom_call" | custom-call | tf_op jit(solution)/shard_map/inputs_grad/pallas_call | solution.py:608
  261.2 2.9 collective-permute-start.60
  266.3 4.1 collective-permute-done.59
  270.4 11.3 %collective-permute-start.72 = (bf16[192,384]{1,0:T(8,128)(2,1)S(1)}, bf16[192,384]{1,0:T(8,128)(2,1)S(1)}, u32[]{:S(2)}, u32[]{:S(2)}) collective-permute-start(bf16[192,384]{1,0:T(8,128)(2,1)S(1)} %fusion.9), channel_id=1, source_target_pairs={{0,8},{2,10},{4,12},{6,14},{8,16},{10,18},{12,20},{14,22},{16,24},... | collective-permute-start | bytes 442376 | tf_op jit(solution)/shard_map/ppermute | solution.py:694
  283.1 4.1 %collective-permute-start.61 = (bf16[48,1536]{1,0:T(8,128)(2,1)S(1)}, bf16[48,1536]{1,0:T(8,128)(2,1)S(1)}, u32[]{:S(2)}, u32[]{:S(2)}) collective-permute-start(bf16[48,1536]{1,0:T(8,128)(2,1)S(1)} %fusion.16), channel_id=1, source_target_pairs={{0,24},{2,26},{4,28},{6,30},{8,0},{10,2},{12,4},{14,6},{16,8},{18,... | collective-permute-start | bytes 442376 | tf_op jit(solution)/shard_map/ppermute | solution.py:694
  292.4 8.5 %collective-permute-done.62 = bf16[48,1536]{1,0:T(8,128)(2,1)S(1)} collective-permute-done((bf16[48,1536]{1,0:T(8,128)(2,1)S(1)}, bf16[48,1536]{1,0:T(8,128)(2,1)S(1)}, u32[]{:S(2)}, u32[]{:S(2)}) %collective-permute-start.62) | collective-permute-done | bytes 147488 | tf_op jit(solution)/shard_map/ppermute | solution.py:694
  301.6 12.7 %collective-permute-done.27 = bf16[4,48,1152]{2,1,0:T(8,128)(2,1)S(1)} collective-permute-done((bf16[4,48,1152]{2,1,0:T(8,128)(2,1)S(1)}, bf16[4,48,1152]{2,1,0:T(8,128)(2,1)S(1)}, u32[]{:S(2)}, u32[]{:S(2)}) %collective-permute-start.27) | collective-permute-done | bytes 442400 | tf_op jit(solution)/shard_map/ppermute | solution.py:694
  314.6 3.2 collective-permute-start.30
  317.9 2.2 collective-permute-done.28
  321.9 5.6 %collective-permute-start.31 = (bf16[48,1152]{1,0:T(8,128)(2,1)S(1)}, bf16[48,1152]{1,0:T(8,128)(2,1)S(1)}, u32[]{:S(2)}, u32[]{:S(2)}) collective-permute-start(bf16[48,1152]{1,0:T(8,128)(2,1)S(1)} %fusion.24), channel_id=1, source_target_pairs={{0,24},{2,26},{4,28},{6,30},{8,0},{10,2},{12,4},{14,6},{16,8},{18,... | collective-permute-start | bytes 331784 | tf_op jit(solution)/shard_map/ppermute | solution.py:694
  329.7 7.7 %collective-permute-done.32 = bf16[48,1152]{1,0:T(8,128)(2,1)S(1)} collective-permute-done((bf16[48,1152]{1,0:T(8,128)(2,1)S(1)}, bf16[48,1152]{1,0:T(8,128)(2,1)S(1)}, u32[]{:S(2)}, u32[]{:S(2)}) %collective-permute-start.32) | collective-permute-done | bytes 110624 | tf_op jit(solution)/shard_map/ppermute | solution.py:694
  348.4 4.0 collective-permute-start.37
  353.8 3.2 collective-permute-start.47
  365.6 2.7 collective-permute-done.48
  374.5 3.7 collective-permute-start.35
  379.6 2.4 collective-permute-start.41
  384.0 3.7 collective-permute-start.51
  390.5 3.3 finish_pair.5
  393.9 4.4 %finish_pair.7 = f32[1536,768]{1,0:T(8,128)} custom-call(s32[1]{0:T(128)} %bitcast.18.at_ref, bf16[1536,384]{1,0:T(8,128)(2,1)} %copy-done.3, bf16[1536,384]{1,0:T(8,128)(2,1)} %collective-permute-done.74.theirs_ref), custom_call_target="tpu_custom_call" | custom-call | tf_op jit(solution)/shard_map/finish_pair/pallas_call | solution.py:670
  398.3 4.4 %finish_pair.6 = f32[384,3072]{1,0:T(8,128)} custom-call(s32[1]{0:T(128)} %bitcast.18.at_ref, bf16[384,1536]{1,0:T(8,128)(2,1)} %copy-done.2, bf16[384,1536]{1,0:T(8,128)(2,1)} %collective-permute-done.65.theirs_ref), custom_call_target="tpu_custom_call" | custom-call | tf_op jit(solution)/shard_map/finish_pair/pallas_call | solution.py:670
  402.7 4.1 %finish_pair.4 = f32[384,2304]{1,0:T(8,128)} custom-call(s32[1]{0:T(128)} %bitcast.18.at_ref, bf16[384,1152]{1,0:T(8,128)(2,1)} %copy-done.4, bf16[384,1152]{1,0:T(8,128)(2,1)} %collective-permute-done.35.theirs_ref), custom_call_target="tpu_custom_call" | custom-call | tf_op jit(solution)/shard_map/finish_pair/pallas_call | solution.py:670
  (326 shorter events, 91.8 us)
Async XLA Ops:
  1.9 12.0 %collective-permute-start.2 = (bf16[96,2304]{1,0:T(8,128)(2,1)S(1)}, bf16[96,2304]{1,0:T(8,128)(2,1)S(1)}, u32[]{:S(2)}, u32[]{:S(2)}) collective-permute-start(bf16[96,2304]{1,0:T(8,128)(2,1)S(1)} %dynamic-slice_bitcast_fusion.5), channel_id=1, source_target_pairs={{0,1},{1,0},{2,3},{3,2},{4,5},{5,4},{6,7},{7,6},{8,9},{9,8},{10,11... | collective-permute-start | bytes 1327112 | tf_op jit(solution)/shard_map/ppermute | solution.py:694
  13.9 13.6 %collective-permute-start.11 = (bf16[96,3072]{1,0:T(8,128)(2,1)S(1)}, bf16[96,3072]{1,0:T(8,128)(2,1)S(1)}, u32[]{:S(2)}, u32[]{:S(2)}) collective-permute-start(bf16[96,3072]{1,0:T(8,128)(2,1)S(1)} %dynamic-slice_bitcast_fusion.4), channel_id=1, source_target_pairs={{0,1},{1,0},{2,3},{3,2},{4,5},{5,4},{6,7},{7,6},{8,9},{9,8},{10,11... | collective-permute-start | bytes 1769480 | tf_op jit(solution)/shard_map/ppermute | solution.py:694
  27.5 17.4 %collective-permute-start.15 = (bf16[384,768]{1,0:T(8,128)(2,1)S(1)}, bf16[384,768]{1,0:T(8,128)(2,1)S(1)}, u32[]{:S(2)}, u32[]{:S(2)}) collective-permute-start(bf16[384,768]{1,0:T(8,128)(2,1)S(1)} %dynamic-slice_bitcast_fusion.3), channel_id=1, source_target_pairs={{0,1},{1,0},{2,3},{3,2},{4,5},{5,4},{6,7},{7,6},{8,9},{9,8},{10,11... | collective-permute-start | bytes 1769480 | tf_op jit(solution)/shard_map/ppermute | solution.py:694
  28.3 18.6 %collective-permute-start.1 = (bf16[48,12]{0,1:T(8,128)(2,1)S(1)}, bf16[48,12]{0,1:T(8,128)(2,1)S(1)}, u32[]{:S(2)}, u32[]{:S(2)}) collective-permute-start(bf16[48,12]{0,1:T(8,128)(2,1)S(1)} %copy-done.44), channel_id=1, source_target_pairs={{0,1},{1,0},{2,3},{3,2},{4,5},{5,4},{6,7},{7,6},{8,9},{9,8},{10,11... | collective-permute-start | bytes 3464 | tf_op jit(solution)/shard_map/ppermute | solution.py:694
  29.9 13.5 %collective-permute-start.7 = (bf16[96,768]{1,0:T(8,128)(2,1)S(1)}, bf16[96,768]{1,0:T(8,128)(2,1)S(1)}, u32[]{:S(2)}, u32[]{:S(2)}) collective-permute-start(bf16[96,768]{1,0:T(8,128)(2,1)S(1)} %dynamic-slice_bitcast_fusion.7), channel_id=1, source_target_pairs={{0,1},{1,0},{2,3},{3,2},{4,5},{5,4},{6,7},{7,6},{8,9},{9,8},{10,11... | collective-permute-start | bytes 442376 | tf_op jit(solution)/shard_map/ppermute | solution.py:694
  43.4 24.9 %collective-permute-start.8 = (bf16[96,768]{1,0:T(8,128)(2,1)S(1)}, bf16[96,768]{1,0:T(8,128)(2,1)S(1)}, u32[]{:S(2)}, u32[]{:S(2)}) collective-permute-start(bf16[96,768]{1,0:T(8,128)(2,1)S(1)} %collective-permute-done.7.refs_8_), channel_id=1, source_target_pairs={{0,4},{2,6},{4,0},{6,2},{8,12},{10,14},{12,8},{14,10},{16,20},{18,... | collective-permute-start | bytes 442376 | tf_op jit(solution)/shard_map/ppermute | solution.py:694
  43.9 41.1 %collective-permute-start.12 = (bf16[96,3072]{1,0:T(8,128)(2,1)S(1)}, bf16[96,3072]{1,0:T(8,128)(2,1)S(1)}, u32[]{:S(2)}, u32[]{:S(2)}) collective-permute-start(bf16[96,3072]{1,0:T(8,128)(2,1)S(1)} %collective-permute-done.11.refs_13_), channel_id=1, source_target_pairs={{0,4},{2,6},{4,0},{6,2},{8,12},{10,14},{12,8},{14,10},{16,20},{18,... | collective-permute-start | bytes 1769480 | tf_op jit(solution)/shard_map/ppermute | solution.py:694
  44.9 40.3 %collective-permute-start.16 = (bf16[384,768]{1,0:T(8,128)(2,1)S(1)}, bf16[384,768]{1,0:T(8,128)(2,1)S(1)}, u32[]{:S(2)}, u32[]{:S(2)}) collective-permute-start(bf16[384,768]{1,0:T(8,128)(2,1)S(1)} %collective-permute-done.15.refs_18_), channel_id=1, source_target_pairs={{0,4},{2,6},{4,0},{6,2},{8,12},{10,14},{12,8},{14,10},{16,20},{18,... | collective-permute-start | bytes 1769480 | tf_op jit(solution)/shard_map/ppermute | solution.py:694
  45.6 18.0 %collective-permute-start = (bf16[8,384]{1,0:T(8,128)(2,1)S(1)}, bf16[8,384]{1,0:T(8,128)(2,1)S(1)}, u32[]{:S(2)}, u32[]{:S(2)}) collective-permute-start(bf16[8,384]{1,0:T(8,128)(2,1)S(1)} %select_select_fusion.4), channel_id=1, source_target_pairs={{0,1},{1,0},{2,3},{3,2},{4,5},{5,4},{6,7},{7,6},{8,9},{9,8},{10,11... | collective-permute-start | bytes 18440 | tf_op jit(solution)/shard_map/ppermute | solution.py:694
  47.0 15.7 %collective-permute-start.6 = (bf16[1536]{0:T(1024)(128)(2,1)S(1)}, bf16[1536]{0:T(1024)(128)(2,1)S(1)}, u32[]{:S(2)}, u32[]{:S(2)}) collective-permute-start(bf16[1536]{0:T(1024)(128)(2,1)S(1)} %copy-done.45), channel_id=1, source_target_pairs={{0,1},{1,0},{2,3},{3,2},{4,5},{5,4},{6,7},{7,6},{8,9},{9,8},{10,11... | collective-permute-start | bytes 9224 | tf_op jit(solution)/shard_map/ppermute | solution.py:694
  62.6 17.8 %collective-permute-start.3 = (bf16[96,2304]{1,0:T(8,128)(2,1)S(1)}, bf16[96,2304]{1,0:T(8,128)(2,1)S(1)}, u32[]{:S(2)}, u32[]{:S(2)}) collective-permute-start(bf16[96,2304]{1,0:T(8,128)(2,1)S(1)} %collective-permute-done.2.refs_5_.refs_4_), channel_id=1, source_target_pairs={{0,4},{2,6},{4,0},{6,2},{8,12},{10,14},{12,8},{14,10},{16,20},{18,... | collective-permute-start | bytes 1327112 | tf_op jit(solution)/shard_map/ppermute | solution.py:694
  63.6 21.0 %collective-permute-start.4 = (bf16[96,2304]{1,0:T(8,128)(2,1)S(1)}, bf16[96,2304]{1,0:T(8,128)(2,1)S(1)}, u32[]{:S(2)}, u32[]{:S(2)}) collective-permute-start(bf16[96,2304]{1,0:T(8,128)(2,1)S(1)} %collective-permute-done.2.refs_5_.refs_4_), channel_id=1, source_target_pairs={{0,2},{2,0},{4,6},{6,4},{8,10},{10,8},{12,14},{14,12},{16,18},{18,... | collective-permute-start | bytes 1327112 | tf_op jit(solution)/shard_map/ppermute | solution.py:694
  68.3 16.1 %collective-permute-start.9 = (bf16[96,768]{1,0:T(8,128)(2,1)S(1)}, bf16[96,768]{1,0:T(8,128)(2,1)S(1)}, u32[]{:S(2)}, u32[]{:S(2)}) collective-permute-start(bf16[96,768]{1,0:T(8,128)(2,1)S(1)} %collective-permute-done.7.refs_8_), channel_id=1, source_target_pairs={{0,2},{2,0},{4,6},{6,4},{8,10},{10,8},{12,14},{14,12},{16,18},{18,... | collective-permute-start | bytes 442376 | tf_op jit(solution)/shard_map/ppermute | solution.py:694
  84.4 18.2 %collective-permute-start.13 = (bf16[96,3072]{1,0:T(8,128)(2,1)S(1)}, bf16[96,3072]{1,0:T(8,128)(2,1)S(1)}, u32[]{:S(2)}, u32[]{:S(2)}) collective-permute-start(bf16[96,3072]{1,0:T(8,128)(2,1)S(1)} %collective-permute-done.11.refs_13_), channel_id=1, source_target_pairs={{0,2},{2,0},{4,6},{6,4},{8,10},{10,8},{12,14},{14,12},{16,18},{18,... | collective-permute-start | bytes 1769480 | tf_op jit(solution)/shard_map/ppermute | solution.py:694
  84.6 18.1 %collective-permute-start.17 = (bf16[384,768]{1,0:T(8,128)(2,1)S(1)}, bf16[384,768]{1,0:T(8,128)(2,1)S(1)}, u32[]{:S(2)}, u32[]{:S(2)}) collective-permute-start(bf16[384,768]{1,0:T(8,128)(2,1)S(1)} %collective-permute-done.15.refs_18_), channel_id=1, source_target_pairs={{0,2},{2,0},{4,6},{6,4},{8,10},{10,8},{12,14},{14,12},{16,18},{18,... | collective-permute-start | bytes 1769480 | tf_op jit(solution)/shard_map/ppermute | solution.py:694
  85.1 17.6 %collective-permute-start.14 = (bf16[96,3072]{1,0:T(8,128)(2,1)S(1)}, bf16[96,3072]{1,0:T(8,128)(2,1)S(1)}, u32[]{:S(2)}, u32[]{:S(2)}) collective-permute-start(bf16[96,3072]{1,0:T(8,128)(2,1)S(1)} %collective-permute-done.12.refs_14_), channel_id=1, source_target_pairs={{0,2},{2,0},{4,6},{6,4},{8,10},{10,8},{12,14},{14,12},{16,18},{18,... | collective-permute-start | bytes 1769480 | tf_op jit(solution)/shard_map/ppermute | solution.py:694
  85.2 17.5 %collective-permute-start.18 = (bf16[384,768]{1,0:T(8,128)(2,1)S(1)}, bf16[384,768]{1,0:T(8,128)(2,1)S(1)}, u32[]{:S(2)}, u32[]{:S(2)}) collective-permute-start(bf16[384,768]{1,0:T(8,128)(2,1)S(1)} %collective-permute-done.16.refs_19_), channel_id=1, source_target_pairs={{0,2},{2,0},{4,6},{6,4},{8,10},{10,8},{12,14},{14,12},{16,18},{18,... | collective-permute-start | bytes 1769480 | tf_op jit(solution)/shard_map/ppermute | solution.py:694
  85.9 16.8 %collective-permute-start.10 = (bf16[96,768]{1,0:T(8,128)(2,1)S(1)}, bf16[96,768]{1,0:T(8,128)(2,1)S(1)}, u32[]{:S(2)}, u32[]{:S(2)}) collective-permute-start(bf16[96,768]{1,0:T(8,128)(2,1)S(1)} %collective-permute-done.8.refs_9_), channel_id=1, source_target_pairs={{0,2},{2,0},{4,6},{6,4},{8,10},{10,8},{12,14},{14,12},{16,18},{18,... | collective-permute-start | bytes 442376 | tf_op jit(solution)/shard_map/ppermute | solution.py:694
  130.0 15.8 %collective-permute-start.19 = (bf16[3072,384]{1,0:T(8,128)(2,1)}, bf16[3072,384]{1,0:T(8,128)(2,1)S(1)}, u32[]{:S(2)}, u32[]{:S(2)}) collective-permute-start(bf16[3072,384]{1,0:T(8,128)(2,1)} %product.8), channel_id=1, source_target_pairs={{0,2},{2,0},{4,6},{6,4},{8,10},{10,8},{12,14},{14,12},{16,18},{18,... | collective-permute-start | bytes 7077896 | tf_op jit(solution)/shard_map/ppermute | solution.py:694
  161.6 39.4 %collective-permute-start.24 = (bf16[2,4,192,384]{3,2,1,0:T(8,128)(2,1)}, bf16[2,4,192,384]{3,2,1,0:T(8,128)(2,1)}, u32[]{:S(2)}, u32[]{:S(2)}) collective-permute-start(bf16[2,4,192,384]{3,2,1,0:T(8,128)(2,1)} %dynamic-slice_bitcast_fusion.1), channel_id=1, source_target_pairs={{0,1},{1,0},{2,3},{3,2},{4,5},{5,4},{6,7},{7,6},{8,9},{9,8},{10,11... | collective-permute-start | bytes 3538952 | tf_op jit(solution)/shard_map/ppermute | solution.py:694
  165.5 13.1 %collective-permute-start.20 = (bf16[768,384]{1,0:T(8,128)(2,1)}, bf16[768,384]{1,0:T(8,128)(2,1)S(1)}, u32[]{:S(2)}, u32[]{:S(2)}) collective-permute-start(bf16[768,384]{1,0:T(8,128)(2,1)} %product.11), channel_id=1, source_target_pairs={{0,2},{2,0},{4,6},{6,4},{8,10},{10,8},{12,14},{14,12},{16,18},{18,... | collective-permute-start | bytes 1769480 | tf_op jit(solution)/shard_map/ppermute | solution.py:694
  175.1 28.0 %collective-permute-start.23 = (bf16[2,4,48,1536]{3,2,1,0:T(8,128)(2,1)}, bf16[2,4,48,1536]{3,2,1,0:T(8,128)(2,1)}, u32[]{:S(2)}, u32[]{:S(2)}) collective-permute-start(bf16[2,4,48,1536]{3,2,1,0:T(8,128)(2,1)} %dynamic-slice_bitcast_fusion), channel_id=1, source_target_pairs={{0,4},{2,6},{4,0},{6,2},{8,12},{10,14},{12,8},{14,10},{16,20},{18,... | collective-permute-start | bytes 3538952 | tf_op jit(solution)/shard_map/ppermute | solution.py:694
  199.3 32.4 %collective-permute-start.22 = (bf16[768,1152]{1,0:T(8,128)(2,1)}, bf16[768,1152]{1,0:T(8,128)(2,1)}, u32[]{:S(2)}, u32[]{:S(2)}) collective-permute-start(bf16[768,1152]{1,0:T(8,128)(2,1)} %product.14), channel_id=1, source_target_pairs={{0,2},{2,0},{4,6},{6,4},{8,10},{10,8},{12,14},{14,12},{16,18},{18,... | collective-permute-start | bytes 5308424 | tf_op jit(solution)/shard_map/ppermute | solution.py:694
  203.1 20.9 %collective-permute-start.66 = (bf16[4,192,384]{2,1,0:T(8,128)(2,1)}, bf16[4,192,384]{2,1,0:T(8,128)(2,1)}, u32[]{:S(2)}, u32[]{:S(2)}) collective-permute-start(bf16[4,192,384]{2,1,0:T(8,128)(2,1)} %fusion), channel_id=1, source_target_pairs={{0,4},{2,6},{4,0},{6,2},{8,12},{10,14},{12,8},{14,10},{16,20},{18,... | collective-permute-start | bytes 1769480 | tf_op jit(solution)/shard_map/ppermute | solution.py:694
  206.4 22.8 %collective-permute-start.25 = (bf16[4,48,1536]{2,1,0:T(8,128)(2,1)}, bf16[4,48,1536]{2,1,0:T(8,128)(2,1)S(1)}, u32[]{:S(2)}, u32[]{:S(2)}) collective-permute-start(bf16[4,48,1536]{2,1,0:T(8,128)(2,1)} %fusion.1), channel_id=1, source_target_pairs={{0,1},{1,0},{2,3},{3,2},{4,5},{5,4},{6,7},{7,6},{8,9},{9,8},{10,11... | collective-permute-start | bytes 1769480 | tf_op jit(solution)/shard_map/ppermute | solution.py:694
  209.9 10.8 %collective-permute-start.52 = (f32[3840]{0:T(1024)}, f32[3840]{0:T(1024)S(1)}, u32[]{:S(2)}, u32[]{:S(2)}) collective-permute-start(f32[3840]{0:T(1024)} %get-tuple-element.106), channel_id=1, source_target_pairs={{0,1},{1,0},{2,3},{3,2},{4,5},{5,4},{6,7},{7,6},{8,9},{9,8},{10,11... | collective-permute-start | bytes 46088 | tf_op jit(solution)/shard_map/ppermute | solution.py:694
  222.0 117.9 %collective-permute-start.53 = (f32[3840]{0:T(1024)S(1)}, f32[3840]{0:T(1024)}, u32[]{:S(2)}, u32[]{:S(2)}) collective-permute-start(f32[3840]{0:T(1024)S(1)} %add.762), channel_id=1, source_target_pairs={{0,2},{2,0},{4,6},{6,4},{8,10},{10,8},{12,14},{14,12},{16,18},{18,... | collective-permute-start | bytes 46088 | tf_op jit(solution)/shard_map/ppermute | solution.py:694
  225.5 35.5 %collective-permute-start.67 = (bf16[192,384]{1,0:T(8,128)(2,1)S(1)}, bf16[192,384]{1,0:T(8,128)(2,1)S(1)}, u32[]{:S(2)}, u32[]{:S(2)}) collective-permute-start(bf16[192,384]{1,0:T(8,128)(2,1)S(1)} %get-tuple-element.118), channel_id=1, source_target_pairs={{0,8},{2,10},{4,12},{6,14},{8,16},{10,18},{12,20},{14,22},{16,24},... | collective-permute-start | bytes 442376 | tf_op jit(solution)/shard_map/ppermute | solution.py:694
  226.8 34.3 %collective-permute-start.68 = (bf16[192,384]{1,0:T(8,128)(2,1)S(1)}, bf16[192,384]{1,0:T(8,128)(2,1)S(1)}, u32[]{:S(2)}, u32[]{:S(2)}) collective-permute-start(bf16[192,384]{1,0:T(8,128)(2,1)S(1)} %get-tuple-element.120), channel_id=1, source_target_pairs={{0,16},{2,18},{4,20},{6,22},{8,24},{10,26},{12,28},{14,30},{16,0},... | collective-permute-start | bytes 442376 | tf_op jit(solution)/shard_map/ppermute | solution.py:694
  229.2 34.9 %collective-permute-start.69 = (bf16[192,384]{1,0:T(8,128)(2,1)S(1)}, bf16[192,384]{1,0:T(8,128)(2,1)}, u32[]{:S(2)}, u32[]{:S(2)}) collective-permute-start(bf16[192,384]{1,0:T(8,128)(2,1)S(1)} %get-tuple-element.119), channel_id=1, source_target_pairs={{0,24},{2,26},{4,28},{6,30},{8,0},{10,2},{12,4},{14,6},{16,8},{18,... | collective-permute-start | bytes 442376 | tf_op jit(solution)/shard_map/ppermute | solution.py:694
  231.6 34.0 %collective-permute-start.58 = (bf16[48,1536]{1,0:T(8,128)(2,1)S(1)}, bf16[48,1536]{1,0:T(8,128)(2,1)}, u32[]{:S(2)}, u32[]{:S(2)}) collective-permute-start(bf16[48,1536]{1,0:T(8,128)(2,1)S(1)} %get-tuple-element.121), channel_id=1, source_target_pairs={{0,8},{2,10},{4,12},{6,14},{8,16},{10,18},{12,20},{14,22},{16,24},... | collective-permute-start | bytes 442376 | tf_op jit(solution)/shard_map/ppermute | solution.py:694
  264.1 25.7 %collective-permute-start.26 = (bf16[2,4,48,1152]{3,2,1,0:T(8,128)(2,1)S(1)}, bf16[2,4,48,1152]{3,2,1,0:T(8,128)(2,1)S(1)}, u32[]{:S(2)}, u32[]{:S(2)}) collective-permute-start(bf16[2,4,48,1152]{3,2,1,0:T(8,128)(2,1)S(1)} %dynamic-slice_bitcast_fusion.2), channel_id=1, source_target_pairs={{0,1},{1,0},{2,3},{3,2},{4,5},{5,4},{6,7},{7,6},{8,9},{9,8},{10,11... | collective-permute-start | bytes 2654216 | tf_op jit(solution)/shard_map/ppermute | solution.py:694
  265.7 17.2 %collective-permute-start.70 = (bf16[192,384]{1,0:T(8,128)(2,1)S(1)}, bf16[192,384]{1,0:T(8,128)(2,1)S(1)}, u32[]{:S(2)}, u32[]{:S(2)}) collective-permute-start(bf16[192,384]{1,0:T(8,128)(2,1)S(1)} %fusion.9), channel_id=1, source_target_pairs={{0,24},{2,26},{4,28},{6,30},{8,0},{10,2},{12,4},{14,6},{16,8},{18,... | collective-permute-start | bytes 442376 | tf_op jit(solution)/shard_map/ppermute | solution.py:694
  270.4 12.7 %collective-permute-start.71 = (bf16[192,384]{1,0:T(8,128)(2,1)S(1)}, bf16[192,384]{1,0:T(8,128)(2,1)S(1)}, u32[]{:S(2)}, u32[]{:S(2)}) collective-permute-start(bf16[192,384]{1,0:T(8,128)(2,1)S(1)} %fusion.9), channel_id=1, source_target_pairs={{0,16},{2,18},{4,20},{6,22},{8,24},{10,26},{12,28},{14,30},{16,0},... | collective-permute-start | bytes 442376 | tf_op jit(solution)/shard_map/ppermute | solution.py:694
  270.4 17.9 %collective-permute-start.72 = (bf16[192,384]{1,0:T(8,128)(2,1)S(1)}, bf16[192,384]{1,0:T(8,128)(2,1)S(1)}, u32[]{:S(2)}, u32[]{:S(2)}) collective-permute-start(bf16[192,384]{1,0:T(8,128)(2,1)S(1)} %fusion.9), channel_id=1, source_target_pairs={{0,8},{2,10},{4,12},{6,14},{8,16},{10,18},{12,20},{14,22},{16,24},... | collective-permute-start | bytes 442376 | tf_op jit(solution)/shard_map/ppermute | solution.py:694
  282.9 31.7 %collective-permute-start.42 = (bf16[2,4,48,384]{3,2,1,0:T(8,128)(2,1)S(1)}, bf16[2,4,48,384]{3,2,1,0:T(8,128)(2,1)S(1)}, u32[]{:S(2)}, u32[]{:S(2)}) collective-permute-start(bf16[2,4,48,384]{3,2,1,0:T(8,128)(2,1)S(1)} %dynamic-slice_bitcast_fusion.6), channel_id=1, source_target_pairs={{0,1},{1,0},{2,3},{3,2},{4,5},{5,4},{6,7},{7,6},{8,9},{9,8},{10,11... | collective-permute-start | bytes 884744 | tf_op jit(solution)/shard_map/ppermute | solution.py:694
  288.3 12.6 %collective-permute-start.62 = (bf16[48,1536]{1,0:T(8,128)(2,1)S(1)}, bf16[48,1536]{1,0:T(8,128)(2,1)S(1)}, u32[]{:S(2)}, u32[]{:S(2)}) collective-permute-start(bf16[48,1536]{1,0:T(8,128)(2,1)S(1)} %fusion.16), channel_id=1, source_target_pairs={{0,16},{2,18},{4,20},{6,22},{8,24},{10,26},{12,28},{14,30},{16,0},... | collective-permute-start | bytes 442376 | tf_op jit(solution)/shard_map/ppermute | solution.py:694
  289.7 11.7 %collective-permute-start.63 = (bf16[48,1536]{1,0:T(8,128)(2,1)S(1)}, bf16[48,1536]{1,0:T(8,128)(2,1)S(1)}, u32[]{:S(2)}, u32[]{:S(2)}) collective-permute-start(bf16[48,1536]{1,0:T(8,128)(2,1)S(1)} %fusion.16), channel_id=1, source_target_pairs={{0,8},{2,10},{4,12},{6,14},{8,16},{10,18},{12,20},{14,22},{16,24},... | collective-permute-start | bytes 442376 | tf_op jit(solution)/shard_map/ppermute | solution.py:694
  292.0 61.8 %collective-permute-start.73 = (bf16[4,192,384]{2,1,0:T(8,128)(2,1)S(1)}, bf16[4,192,384]{2,1,0:T(8,128)(2,1)S(1)}, u32[]{:S(2)}, u32[]{:S(2)}) collective-permute-start(bf16[4,192,384]{2,1,0:T(8,128)(2,1)S(1)} %select_select_fusion), channel_id=1, source_target_pairs={{0,4},{2,6},{4,0},{6,2},{8,12},{10,14},{12,8},{14,10},{16,20},{18,... | collective-permute-start | bytes 1769480 | tf_op jit(solution)/shard_map/ppermute | solution.py:694
  301.0 13.3 %collective-permute-start.27 = (bf16[4,48,1152]{2,1,0:T(8,128)(2,1)S(1)}, bf16[4,48,1152]{2,1,0:T(8,128)(2,1)S(1)}, u32[]{:S(2)}, u32[]{:S(2)}) collective-permute-start(bf16[4,48,1152]{2,1,0:T(8,128)(2,1)S(1)} %fusion.2), channel_id=1, source_target_pairs={{0,4},{2,6},{4,0},{6,2},{8,12},{10,14},{12,8},{14,10},{16,20},{18,... | collective-permute-start | bytes 1327112 | tf_op jit(solution)/shard_map/ppermute | solution.py:694
  329.3 29.5 %collective-permute-start.64 = (bf16[4,48,1536]{2,1,0:T(8,128)(2,1)S(1)}, bf16[4,48,1536]{2,1,0:T(8,128)(2,1)S(1)}, u32[]{:S(2)}, u32[]{:S(2)}) collective-permute-start(bf16[4,48,1536]{2,1,0:T(8,128)(2,1)S(1)} %select_select_fusion.1), channel_id=1, source_target_pairs={{0,4},{2,6},{4,0},{6,2},{8,12},{10,14},{12,8},{14,10},{16,20},{18,... | collective-permute-start | bytes 1769480 | tf_op jit(solution)/shard_map/ppermute | solution.py:694
  338.4 31.7 %collective-permute-start.34 = (bf16[4,48,1152]{2,1,0:T(8,128)(2,1)}, bf16[4,48,1152]{2,1,0:T(8,128)(2,1)}, u32[]{:S(2)}, u32[]{:S(2)}) collective-permute-start(bf16[4,48,1152]{2,1,0:T(8,128)(2,1)} %select_select_fusion.2), channel_id=1, source_target_pairs={{0,4},{2,6},{4,0},{6,2},{8,12},{10,14},{12,8},{14,10},{16,20},{18,... | collective-permute-start | bytes 1327112 | tf_op jit(solution)/shard_map/ppermute | solution.py:694
  347.3 14.1 %collective-permute-start.54 = (f32[3840]{0:T(1024)}, f32[3840]{0:T(1024)}, u32[]{:S(2)}, u32[]{:S(2)}) collective-permute-start(f32[3840]{0:T(1024)} %add.763), channel_id=1, source_target_pairs={{0,4},{2,6},{4,0},{6,2},{8,12},{10,14},{12,8},{14,10},{16,20},{18,... | collective-permute-start | bytes 46088 | tf_op jit(solution)/shard_map/ppermute | solution.py:694
  348.4 12.8 %collective-permute-start.37 = (f32[1344]{0:T(1024)S(1)}, f32[1344]{0:T(1024)S(1)}, u32[]{:S(2)}, u32[]{:S(2)}) collective-permute-start(f32[1344]{0:T(1024)S(1)} %add.744), channel_id=1, source_target_pairs={{0,2},{2,0},{4,6},{6,4},{8,10},{10,8},{12,14},{14,12},{16,18},{18,... | collective-permute-start | bytes 16136 | tf_op jit(solution)/shard_map/ppermute | solution.py:694
  353.8 10.2 %collective-permute-start.47 = (bf16[48,384]{1,0:T(8,128)(2,1)}, bf16[48,384]{1,0:T(8,128)(2,1)S(1)}, u32[]{:S(2)}, u32[]{:S(2)}) collective-permute-start(bf16[48,384]{1,0:T(8,128)(2,1)} %fusion.31), channel_id=1, source_target_pairs={{0,24},{2,26},{4,28},{6,30},{8,0},{10,2},{12,4},{14,6},{16,8},{18,... | collective-permute-start | bytes 110600 | tf_op jit(solution)/shard_map/ppermute | solution.py:694
  359.6 34.2 %collective-permute-start.74 = (bf16[1536,384]{1,0:T(8,128)(2,1)S(1)}, bf16[1536,384]{1,0:T(8,128)(2,1)}, u32[]{:S(2)}, u32[]{:S(2)}) collective-permute-start(bf16[1536,384]{1,0:T(8,128)(2,1)S(1)} %bitcast_select_fusion.mine_ref), channel_id=1, source_target_pairs={{0,2},{2,0},{4,6},{6,4},{8,10},{10,8},{12,14},{14,12},{16,18},{18,... | collective-permute-start | bytes 3538952 | tf_op jit(solution)/shard_map/ppermute | solution.py:694
  361.2 37.1 %collective-permute-start.65 = (bf16[384,1536]{1,0:T(8,128)(2,1)S(1)}, bf16[384,1536]{1,0:T(8,128)(2,1)}, u32[]{:S(2)}, u32[]{:S(2)}) collective-permute-start(bf16[384,1536]{1,0:T(8,128)(2,1)S(1)} %bitcast_select_fusion.1.mine_ref), channel_id=1, source_target_pairs={{0,2},{2,0},{4,6},{6,4},{8,10},{10,8},{12,14},{14,12},{16,18},{18,... | collective-permute-start | bytes 3538952 | tf_op jit(solution)/shard_map/ppermute | solution.py:694
  374.5 28.2 %collective-permute-start.35 = (bf16[384,1152]{1,0:T(8,128)(2,1)S(1)}, bf16[384,1152]{1,0:T(8,128)(2,1)}, u32[]{:S(2)}, u32[]{:S(2)}) collective-permute-start(bf16[384,1152]{1,0:T(8,128)(2,1)S(1)} %bitcast_select_fusion.2.mine_ref), channel_id=1, source_target_pairs={{0,2},{2,0},{4,6},{6,4},{8,10},{10,8},{12,14},{14,12},{16,18},{18,... | collective-permute-start | bytes 2654216 | tf_op jit(solution)/shard_map/ppermute | solution.py:694
  (81 other events, 1240.2 us)
